TPU v7x, 32 devices: a whole 2x2x4 slice. The times are simulated.
32 devices in a mesh: parts: 2 (over x), mag: 16 (over z, y, core).
Axes of the slice: x: 2, y: 2, z: 4, core: 2. Of those that a mesh axis runs over, the one named last changes fastest.
Arguments:
- density: float32 [128, 16, 128], P(('parts', 'mag')), parts along dimension 0, may hold values from 0.5 to 2
- velocity: float32 [3, 128, 16, 128], P(None, ('parts', 'mag')), parts along dimension 1, may hold values from -1.2 to 1.2
- mag_field: float32 [3, 128, 16, 128], P(None, ('parts', 'mag')), parts along dimension 1, may hold values from -2 to 2
- pressure: float32 [128, 16, 128], P(('parts', 'mag')), parts along dimension 0, may hold values from 0.5 to 2
- conductance: float32 [128, 2048], P(('parts', 'mag')), parts along dimension 0, may hold values from 0.5 to 5
- shell_cell: int32 [16384], P('mag'), may hold values from 0 to 8191
- foot_owner: int32 [16384, 1], replicated, may hold values from 0 to 15; in each aligned block of 1024 rows (0 to 1023, 1024 to 2047, ...) at most 160 rows name the same one
- foot_row: int32 [16384], replicated, may hold values from 0 to 3
- foot_lon: int32 [16384], replicated, may hold values from 0 to 2047
Outputs:
- new_density: float32 [128, 16, 128], P(('parts', 'mag')), parts along dimension 0
- new_velocity: float32 [3, 128, 16, 128], P(None, ('parts', 'mag')), parts along dimension 1
- new_field: float32 [3, 128, 16, 128], P(None, ('parts', 'mag')), parts along dimension 1
- new_pressure: float32 [128, 16, 128], P(('parts', 'mag')), parts along dimension 0
- potential: float32 [128, 2048], P(('parts', 'mag')), parts along dimension 0
- shell_potential: float32 [32768], P(('parts', 'mag')), parts along dimension 0
There are 2 independent parts, one for each index of `parts`. A program takes and returns all parts, laid end to end along the dimension named above; an argument that names none is the same for every part. Nothing has to cross between parts.
Inputs may be any that keep to these rules, and one draw needn't show every extreme that they name: `foot_owner`: in each device's aligned block of 1024 rows no owner is named by more than 160 rows.
All inputs are finite; a program needn't handle non-finite values.
Results may differ from a plain program's by a relative error of at most 0.0003.
Values sent between devices are 32-bit elements; how exact they have to be, the bound alone decides.
No kernel may reach another device: no remote copies, remote signals or barrier semaphores. Data moves between devices by JAX's collectives and lax.ppermute only.
A program may use at most 64 MiB of HBM per device.

v0:
```python
import jax
import jax.numpy as jnp
from jax import lax
from jax.sharding import PartitionSpec as P

SWEEPS = 4


ADIABATIC = 5.0 / 3.0
TIME_STEP = 0.02
LON_WEIGHT = 0.25
LEAK_RATE = 0.05
SOURCE_GAIN = 10.0
SLOT_BLOCK = 512


def with_halo(block, sides, width):
    for axis, dim in sides:
        count = lax.axis_size(axis)
        forward = [(i, i + 1) for i in range(count - 1)]
        backward = [(target, source) for source, target in forward]
        low = lax.ppermute(
            lax.slice_in_dim(block, block.shape[dim] - width, None, axis=dim), axis, forward
        )
        high = lax.ppermute(lax.slice_in_dim(block, 0, width, axis=dim), axis, backward)
        block = jnp.concatenate([low, block, high], axis=dim)
    return block


def minmod(lower_diff, upper_diff):
    smaller = jnp.minimum(jnp.abs(lower_diff), jnp.abs(upper_diff))
    return jnp.where(lower_diff * upper_diff > 0.0, jnp.sign(lower_diff) * smaller, 0.0)


def conserved(primitives):
    density = primitives[0]
    velocity = primitives[1:4]
    field_part = primitives[4:7]
    kinetic = 0.5 * density * jnp.sum(velocity * velocity, axis=0)
    magnetic = 0.5 * jnp.sum(field_part * field_part, axis=0)
    energy = primitives[7] / (ADIABATIC - 1.0) + kinetic + magnetic
    return jnp.concatenate(
        [density[None], density[None] * velocity, field_part, energy[None]], axis=0
    )


def primitive(states):
    density = states[0]
    velocity = states[1:4] / density
    field_part = states[4:7]
    kinetic = 0.5 * density * jnp.sum(velocity * velocity, axis=0)
    magnetic = 0.5 * jnp.sum(field_part * field_part, axis=0)
    pressure = (ADIABATIC - 1.0) * (states[7] - kinetic - magnetic)
    return jnp.concatenate([density[None], velocity, field_part, pressure[None]], axis=0)


def flux_of(primitives, states, normal):
    density = primitives[0]
    velocity = primitives[1:4]
    field_part = primitives[4:7]
    normal_speed = velocity[normal]
    normal_field = field_part[normal]
    total_pressure = primitives[7] + 0.5 * jnp.sum(field_part * field_part, axis=0)
    momentum = density * normal_speed * velocity - normal_field * field_part
    momentum = momentum.at[normal].add(total_pressure)
    induction = normal_speed * field_part - normal_field * velocity
    energy = (states[7] + total_pressure) * normal_speed - normal_field * jnp.sum(
        velocity * field_part, axis=0
    )
    return jnp.concatenate(
        [(density * normal_speed)[None], momentum, induction, energy[None]], axis=0
    )


def wave_speed(primitives, normal):
    field_sq = jnp.sum(primitives[4:7] * primitives[4:7], axis=0)
    return jnp.abs(primitives[1 + normal]) + jnp.sqrt(
        (ADIABATIC * jnp.abs(primitives[7]) + field_sq) / primitives[0]
    )


def interface(outer_left, left_cell, right_cell, outer_right, normal):
    left_state = left_cell + 0.5 * minmod(left_cell - outer_left, right_cell - left_cell)
    right_state = right_cell - 0.5 * minmod(right_cell - left_cell, outer_right - right_cell)
    left_cons = conserved(left_state)
    right_cons = conserved(right_state)
    fastest = jnp.maximum(wave_speed(left_state, normal), wave_speed(right_state, normal))
    average = 0.5 * (
        flux_of(left_state, left_cons, normal) + flux_of(right_state, right_cons, normal)
    )
    return average - 0.5 * fastest * (right_cons - left_cons)


def tendency(padded):
    inner_width = padded.shape[1] - 4
    face_flux = interface(
        padded[:, 0 : inner_width + 1],
        padded[:, 1 : inner_width + 2],
        padded[:, 2 : inner_width + 3],
        padded[:, 3 : inner_width + 4],
        0,
    )
    change = face_flux[:, 1:] - face_flux[:, :-1]
    centre = padded[:, 2 : inner_width + 2]
    for normal, roll_axis in ((1, 2), (2, 3)):
        face_flux = interface(
            jnp.roll(centre, 2, roll_axis),
            jnp.roll(centre, 1, roll_axis),
            centre,
            jnp.roll(centre, -1, roll_axis),
            normal,
        )
        change = change + jnp.roll(face_flux, -1, roll_axis) - face_flux
    return -change


def parallel_current(field_pad):
    centre = field_pad[:, 1:-1]

    def along_x(values):
        return 0.5 * (values[2:] - values[:-2])

    def along_y(values):
        return 0.5 * (jnp.roll(values, -1, 1) - jnp.roll(values, 1, 1))

    def along_z(values):
        return 0.5 * (jnp.roll(values, -1, 2) - jnp.roll(values, 1, 2))

    current_x = along_y(centre[2]) - along_z(centre[1])
    current_y = along_z(centre[0]) - along_x(field_pad[2])
    current_z = along_x(field_pad[1]) - along_y(centre[0])
    aligned = current_x * centre[0] + current_y * centre[1] + current_z * centre[2]
    return aligned / jnp.sqrt(jnp.sum(centre * centre, axis=0) + 1.0)


def coefficients(cond_pad):
    conduct = cond_pad[1:-1]
    north_w = 0.5 * (conduct + cond_pad[:-2])
    south_w = 0.5 * (conduct + cond_pad[2:])
    east_w = LON_WEIGHT * 0.5 * (conduct + jnp.roll(conduct, -1, 1))
    west_w = LON_WEIGHT * 0.5 * (conduct + jnp.roll(conduct, 1, 1))
    diagonal = north_w + south_w + east_w + west_w + LEAK_RATE * conduct
    return (north_w, south_w, east_w, west_w, diagonal)


def relax_sweep(pot_pad, source, weights):
    north_w, south_w, east_w, west_w, diagonal = weights
    middle_rows = pot_pad[1:-1]
    numerator = (
        source
        + north_w * pot_pad[:-2]
        + south_w * pot_pad[2:]
        + east_w * jnp.roll(middle_rows, -1, 1)
        + west_w * jnp.roll(middle_rows, 1, 1)
    )
    return numerator / diagonal


def close_ends(padded, layers):
    my_index = lax.axis_index("mag")
    devices = lax.axis_size("mag")
    inner_width = padded.shape[1] - 2 * layers
    first_copy = jnp.repeat(padded[:, layers : layers + 1], layers, axis=1)
    last_copy = jnp.repeat(
        padded[:, layers + inner_width - 1 : layers + inner_width], layers, axis=1
    )
    lower_rim = jnp.where(my_index == 0, first_copy, padded[:, :layers])
    upper_rim = jnp.where(my_index == devices - 1, last_copy, padded[:, layers + inner_width :])
    return jnp.concatenate([lower_rim, padded[:, layers : layers + inner_width], upper_rim], axis=1)


def section_rim(primitives):
    padded = with_halo(primitives, (("mag", 1),), 2)
    return close_ends(padded, 2)


def onehot(index, count):
    return (index[..., None] == jnp.arange(count, dtype=jnp.int32)).astype(jnp.float32)


def exact_dot(left, right):
    return jnp.dot(left, right, precision=lax.Precision.HIGHEST, preferred_element_type=jnp.float32)


def shards(
    density, velocity, mag_field, pressure, conductance, shell_cell, foot_owner, foot_row, foot_lon
):
    my_index = lax.axis_index("mag")
    devices = lax.axis_size("mag")
    primitives = jnp.concatenate([density[None], velocity, mag_field, pressure[None]], axis=0)
    padded = section_rim(primitives)
    current = parallel_current(padded[4:7, 1:-1])
    start_state = conserved(primitives)
    first_state = start_state + TIME_STEP * tendency(padded)
    final_state = 0.5 * start_state + 0.5 * (
        first_state + TIME_STEP * tendency(section_rim(primitive(first_state)))
    )
    result = primitive(final_state)
    shell_count = shell_cell.shape[0]
    capacity = max(2, shell_count * 5 // (2 * devices))
    slot_total = devices * capacity
    lat_rows = conductance.shape[0]
    columns = conductance.shape[1]
    depth = current.shape[2]
    planes = current.shape[0] * current.shape[1]
    lane_part = exact_dot(current.reshape(planes, depth), onehot(shell_cell % depth, depth).T)
    picked = jnp.sum(lane_part * onehot(shell_cell // depth, planes).T, axis=0)
    currents = SOURCE_GAIN * picked
    owners = foot_owner[:, 0]
    own_dest = lax.dynamic_slice_in_dim(owners, my_index * shell_count, shell_count)
    dest_table = (own_dest[:, None] == jnp.arange(devices, dtype=jnp.int32)[None, :]).astype(
        jnp.int32
    )
    own_rank = jnp.sum((jnp.cumsum(dest_table, axis=0) - 1) * dest_table, axis=1)
    dest_float = dest_table.astype(jnp.float32)
    rank_hot = onehot(own_rank, capacity)
    outgoing = exact_dot((dest_float * currents[:, None]).T, rank_hot)
    incoming = lax.all_to_all(outgoing, "mag", split_axis=0, concat_axis=0, tiled=True)
    mine_mask = owners.reshape(devices, shell_count) == my_index
    slot_rank = jnp.cumsum(mine_mask.astype(jnp.int32), axis=1) - 1
    selector = onehot(slot_rank, capacity) * mine_mask.astype(jnp.float32)[:, :, None]
    row_float = foot_row.reshape(devices, shell_count).astype(jnp.float32)
    lon_float = foot_lon.reshape(devices, shell_count).astype(jnp.float32)
    row_slot = jnp.einsum("jsc,js->jc", selector, row_float, precision=lax.Precision.HIGHEST)
    lon_slot = jnp.einsum("jsc,js->jc", selector, lon_float, precision=lax.Precision.HIGHEST)
    occupied = jnp.sum(selector, axis=1)
    slot_rows = jnp.where(occupied > 0.5, row_slot.astype(jnp.int32), -1).reshape(-1)
    slot_lons = lon_slot.astype(jnp.int32).reshape(-1)
    block_count = -(-slot_total // SLOT_BLOCK)
    rows_blocks = slot_rows.reshape(block_count, SLOT_BLOCK)
    lons_blocks = slot_lons.reshape(block_count, SLOT_BLOCK)
    vals_blocks = incoming.reshape(-1).reshape(block_count, SLOT_BLOCK)

    def add_block(total, items):
        rows_here, lons_here, vals_here = items
        weighted = onehot(rows_here, lat_rows).T * vals_here[None, :]
        return (total + exact_dot(weighted, onehot(lons_here, columns)), None)

    source, unused = lax.scan(
        add_block,
        jnp.zeros((lat_rows, columns), jnp.float32),
        (rows_blocks, lons_blocks, vals_blocks),
    )
    cond_pad = with_halo(conductance, (("mag", 0),), 1)
    weights = coefficients(cond_pad)
    potential = source / weights[4]
    for sweep_index in range(SWEEPS - 1):
        pot_pad = with_halo(potential, (("mag", 0),), 1)
        potential = relax_sweep(pot_pad, source, weights)

    def read_block(items):
        rows_here, lons_here = items
        by_lon = exact_dot(potential, onehot(lons_here, columns).T)
        return jnp.sum(by_lon * onehot(rows_here, lat_rows).T, axis=0)

    read_values = lax.map(read_block, (rows_blocks, lons_blocks))
    values = read_values.reshape(-1).reshape(devices, capacity)
    returned = lax.all_to_all(values, "mag", split_axis=0, concat_axis=0, tiled=True)
    back_table = exact_dot(rank_hot, returned.T)
    shell_potential = jnp.sum(back_table * dest_float, axis=1)
    return (result[0], result[1:4], result[4:7], result[7], potential, shell_potential)


def solution(mesh):
    in_specs = (
        P(("parts", "mag"), None, None),
        P(None, ("parts", "mag"), None, None),
        P(None, ("parts", "mag"), None, None),
        P(("parts", "mag"), None, None),
        P(("parts", "mag"), None),
        P("mag"),
        P(),
        P(),
        P(),
    )
    out_specs = (
        P(("parts", "mag"), None, None),
        P(None, ("parts", "mag"), None, None),
        P(None, ("parts", "mag"), None, None),
        P(("parts", "mag"), None, None),
        P(("parts", "mag"), None),
        P(("parts", "mag")),
    )
    return jax.shard_map(shards, mesh=mesh, in_specs=in_specs, out_specs=out_specs, check_vma=False)
```

profile of v0, /device:TPU:0, one launch (start us, length us, event | category | flops | bytes accessed | tf_op | source)
XLA Modules:
  0.0 152.3 jit_solution(15580897474267697879)
XLA Ops:
  3.6 3.0 %collective-permute-start = (f32[8,2,16,128]{3,2,1,0:T(8,128)}, f32[8,2,16,128]{3,2,1,0:T(8,128)S(1)}, u32[]{:S(2)}, u32[]{:S(2)}) collective-permute-start(f32[8,2,16,128]{3,2,1,0:T(8,128)} %get-tuple-element.494), channel_id=1, source_target_pairs={{0,1},{1,2},{2,3},{3,4},{4,5},{5,6},{6,7},{7,8},{8,9},{9,10},{10,1... | collective-permute-start | bytes 393224 | tf_op jit(solution)/shard_map/ppermute | solution.py:22
  7.3 1.3 collective-permute-start.5
  8.6 5.1 %collective-permute-start.4 = (f32[1,2048]{1,0:T(1,128)}, f32[1,2048]{1,0:T(1,128)S(1)}, u32[]{:S(2)}, u32[]{:S(2)}) collective-permute-start(f32[1,2048]{1,0:T(1,128)} %get-tuple-element.582), channel_id=1, source_target_pairs={{0,1},{1,2},{2,3},{3,4},{4,5},{5,6},{6,7},{7,8},{8,9},{9,10},{10,1... | collective-permute-start | bytes 24584 | tf_op jit(solution)/shard_map/ppermute | solution.py:22
  19.5 4.5 %reduce-window.14 = s32[16,8,128]{2,1,0:T(8,128)S(1)} reduce-window(s32[16,8,128]{2,1,0:T(8,128)S(1)} %bitcast.656, s32[]{:T(128)} %constant.365.clone.1), window={size=1x1x128 pad=0_0x0_0x127_0}, to_apply=%region_42.43 | reduce-window | flops 2080768 | bytes 131076 | tf_op jit(solution)/shard_map/reduce-window
  24.4 1.3 select_reduce_fusion
  25.8 9.8 %fusion.15 = f32[16,1,160]{2,1,0:T(1,128)S(1)} fusion(f32[16,1024,1]{1,2,0:T(1,128)S(1)} %bitcast.661, f32[16,1024]{1,0:T(8,128)S(1)} %reshape.710, s32[16,1024]{1,0:T(8,128)S(1)} %bitcast.658), kind=kOutput, calls=%fused_computation.24 | convolution fusion | flops 36700160 | bytes 206848 | tf_op jit(solution)/shard_map/jsc,js->jc/dot_general | solution.py:224
  35.6 4.7 %reduce-window.16 = s32[16,8,128]{2,1,0:T(8,128)S(1)} reduce-window(s32[16,8,128]{2,1,0:T(8,128)S(1)} %fusion.70, s32[]{:T(128)} %constant.365.clone.1), window={size=1x1x128 pad=0_0x0_0x127_0}, to_apply=%region_46.47 | reduce-window | flops 2080768 | bytes 131076 | tf_op jit(solution)/shard_map/reduce-window.2
  41.4 9.8 %fusion.13 = f32[16,1,160]{2,1,0:T(1,128)S(1)} fusion(f32[16,1024,1]{1,2,0:T(1,128)S(1)} %bitcast.662, f32[16,1024]{1,0:T(8,128)S(1)} %reshape.710, s32[16,1024]{1,0:T(8,128)S(1)} %bitcast.659), kind=kOutput, calls=%fused_computation.22 | convolution fusion | flops 36700160 | bytes 206848 | tf_op jit(solution)/shard_map/jsc,js->jc/dot_general | solution.py:225
  64.0 1.3 collective-permute-start.3
  65.3 4.3 %collective-permute-start.2 = (f32[8,2,16,128]{3,2,1,0:T(8,128)S(1)}, f32[8,2,16,128]{3,2,1,0:T(8,128)S(1)}, u32[]{:S(2)}, u32[]{:S(2)}) collective-permute-start(f32[8,2,16,128]{3,2,1,0:T(8,128)S(1)} %get-tuple-element.426), channel_id=1, source_target_pairs={{0,1},{1,2},{2,3},{3,4},{4,5},{5,6},{6,7},{7,8},{8,9},{9,10},{10,1... | collective-permute-start | bytes 393224 | tf_op jit(solution)/shard_map/ppermute | solution.py:22
  71.5 8.9 %all-to-all-start = ((f32[16,1,160]{2,1,0:T(1,128)}), f32[16,1,160]{2,1,0:T(1,128)}, u32[]{:S(2)}, u32[]{:S(2)}) async-start(f32[16,1,160]{2,1,0:T(1,128)} %copy.48), calls=%async_computation | async-start | bytes 32768 | tf_op jit(solution)/shard_map/all_to_all | solution.py:218
  82.0 5.0 %all-to-all-done = f32[16,1,160]{2,1,0:T(1,128)} async-done(((f32[16,1,160]{2,1,0:T(1,128)}), f32[16,1,160]{2,1,0:T(1,128)}, u32[]{:S(2)}, u32[]{:S(2)}) %all-to-all-start) | async-done | bytes 10272 | tf_op jit(solution)/shard_map/all_to_all | solution.py:218
  87.8 11.2 %while.34 = (s32[]{:T(128)}, f32[4,2048]{1,0:T(4,128)S(1)}, s32[5,512]{1,0:T(8,128)}, f32[5,512]{1,0:T(8,128)S(1)}, s32[5,512]{1,0:T(8,128)}, /*index=5*/s32[]{:T(128)}, s32[]{:T(128)}) while((s32[]{:T(128)}, f32[4,2048]{1,0:T(4,128)S(1)}, s32[5,512]{1,0:T(8,128)}, f32[5,512]{1,0:T(8,128)S(1)}, s32[5,512]{1,0:T(8,128)}, ...), condition=%wide.region_50.51_spmd.clone, body=%wide.region_49.50_spmd.clone.sunk | while | flops 51400704 | bytes 84071 | solution.py:239
  88.6 1.5 fusion.323
  90.8 1.5 fusion.323
  93.1 1.5 fusion.323
  95.3 1.5 fusion.323
  97.6 1.5 fusion.323
  99.3 1.3 collective-permute-start.7
  100.6 3.0 %collective-permute-start.6 = (f32[1,2048]{1,0:T(1,128)S(1)}, f32[1,2048]{1,0:T(1,128)S(1)}, u32[]{:S(2)}, u32[]{:S(2)}) collective-permute-start(f32[1,2048]{1,0:T(1,128)S(1)} %get-tuple-element.576), channel_id=1, source_target_pairs={{0,1},{1,2},{2,3},{3,4},{4,5},{5,6},{6,7},{7,8},{8,9},{9,10},{10,1... | collective-permute-start | bytes 24584 | tf_op jit(solution)/shard_map/ppermute | solution.py:22
  104.7 1.3 collective-permute-start.9
  106.0 3.5 %collective-permute-start.8 = (f32[1,2048]{1,0:T(1,128)S(1)}, f32[1,2048]{1,0:T(1,128)S(1)}, u32[]{:S(2)}, u32[]{:S(2)}) collective-permute-start(f32[1,2048]{1,0:T(1,128)S(1)} %get-tuple-element.570), channel_id=1, source_target_pairs={{0,1},{1,2},{2,3},{3,4},{4,5},{5,6},{6,7},{7,8},{8,9},{9,10},{10,1... | collective-permute-start | bytes 24584 | tf_op jit(solution)/shard_map/ppermute | solution.py:22
  110.5 1.3 collective-permute-start.11
  111.8 4.8 %collective-permute-start.10 = (f32[1,2048]{1,0:T(1,128)S(1)}, f32[1,2048]{1,0:T(1,128)S(1)}, u32[]{:S(2)}, u32[]{:S(2)}) collective-permute-start(f32[1,2048]{1,0:T(1,128)S(1)} %get-tuple-element.564), channel_id=1, source_target_pairs={{0,1},{1,2},{2,3},{3,4},{4,5},{5,6},{6,7},{7,8},{8,9},{9,10},{10,1... | collective-permute-start | bytes 24584 | tf_op jit(solution)/shard_map/ppermute | solution.py:22
  117.6 14.3 %while.33 = (s32[]{:T(128)}, f32[5,512]{1,0:T(8,128)S(1)}, s32[5,512]{1,0:T(8,128)}, s32[5,512]{1,0:T(8,128)}, f32[4,2048]{1,0:T(4,128)S(1)}, /*index=5*/s32[]{:T(128)}, s32[]{:T(128)}) while((s32[]{:T(128)}, f32[5,512]{1,0:T(8,128)S(1)}, s32[5,512]{1,0:T(8,128)}, s32[5,512]{1,0:T(8,128)}, f32[4,2048]{1,0:T(4,128)S(1)}, ...), condition=%wide.region_53.54_spmd, body=%wide.region_51.53_spmd.sunk | while | flops 51385856 | bytes 51293 | solution.py:256
  118.3 2.0 %fusion.321 = f32[512]{0:T(512)S(1)} fusion(f32[4,2048]{1,0:T(4,128)S(1)} %get-tuple-element.737, s32[512]{0:T(512)S(1)} %bitcast.665, s32[512]{0:T(512)S(1)} %bitcast.666), kind=kOutput, calls=%fused_computation.5.clone.1 | convolution fusion | flops 51385856 | bytes 38912 | tf_op jit(solution)/shard_map/while/body/eval_jaxpr/dot_general | solution.py:182
  121.2 2.0 %fusion.321 = f32[512]{0:T(512)S(1)} fusion(f32[4,2048]{1,0:T(4,128)S(1)} %get-tuple-element.737, s32[512]{0:T(512)S(1)} %bitcast.665, s32[512]{0:T(512)S(1)} %bitcast.666), kind=kOutput, calls=%fused_computation.5.clone.1 | convolution fusion | flops 51385856 | bytes 38912 | tf_op jit(solution)/shard_map/while/body/eval_jaxpr/dot_general | solution.py:182
  124.1 2.0 %fusion.321 = f32[512]{0:T(512)S(1)} fusion(f32[4,2048]{1,0:T(4,128)S(1)} %get-tuple-element.737, s32[512]{0:T(512)S(1)} %bitcast.665, s32[512]{0:T(512)S(1)} %bitcast.666), kind=kOutput, calls=%fused_computation.5.clone.1 | convolution fusion | flops 51385856 | bytes 38912 | tf_op jit(solution)/shard_map/while/body/eval_jaxpr/dot_general | solution.py:182
  126.9 2.0 %fusion.321 = f32[512]{0:T(512)S(1)} fusion(f32[4,2048]{1,0:T(4,128)S(1)} %get-tuple-element.737, s32[512]{0:T(512)S(1)} %bitcast.665, s32[512]{0:T(512)S(1)} %bitcast.666), kind=kOutput, calls=%fused_computation.5.clone.1 | convolution fusion | flops 51385856 | bytes 38912 | tf_op jit(solution)/shard_map/while/body/eval_jaxpr/dot_general | solution.py:182
  129.8 2.0 %fusion.321 = f32[512]{0:T(512)S(1)} fusion(f32[4,2048]{1,0:T(4,128)S(1)} %get-tuple-element.737, s32[512]{0:T(512)S(1)} %bitcast.665, s32[512]{0:T(512)S(1)} %bitcast.666), kind=kOutput, calls=%fused_computation.5.clone.1 | convolution fusion | flops 51385856 | bytes 38912 | tf_op jit(solution)/shard_map/while/body/eval_jaxpr/dot_general | solution.py:182
  132.6 8.8 %all-to-all-start.1 = ((f32[16,1,160]{2,1,0:T(1,128)}), f32[16,1,160]{2,1,0:T(1,128)S(1)}, u32[]{:S(2)}, u32[]{:S(2)}) async-start(f32[16,1,160]{2,1,0:T(1,128)} %all_to_all.16), calls=%async_computation.1 | async-start | bytes 32768 | tf_op jit(solution)/shard_map/all_to_all | solution.py:258
  141.7 6.2 %all-to-all-done.1 = f32[16,1,160]{2,1,0:T(1,128)S(1)} async-done(((f32[16,1,160]{2,1,0:T(1,128)}), f32[16,1,160]{2,1,0:T(1,128)S(1)}, u32[]{:S(2)}, u32[]{:S(2)}) %all-to-all-start.1) | async-done | bytes 10272 | tf_op jit(solution)/shard_map/all_to_all | solution.py:258
  (263 shorter events, 43.5 us)
Async XLA Ops:
  2.4 55.5 %collective-permute-start.1 = (f32[8,2,16,128]{3,2,1,0:T(8,128)}, f32[8,2,16,128]{3,2,1,0:T(8,128)}, u32[]{:S(2)}, u32[]{:S(2)}) collective-permute-start(f32[8,2,16,128]{3,2,1,0:T(8,128)} %get-tuple-element.493), channel_id=1, source_target_pairs={{1,0},{2,1},{3,2},{4,3},{5,4},{6,5},{7,6},{8,7},{9,8},{10,9},{11,1... | collective-permute-start | bytes 393224 | tf_op jit(solution)/shard_map/ppermute | solution.py:25
  3.6 55.1 %collective-permute-start = (f32[8,2,16,128]{3,2,1,0:T(8,128)}, f32[8,2,16,128]{3,2,1,0:T(8,128)S(1)}, u32[]{:S(2)}, u32[]{:S(2)}) collective-permute-start(f32[8,2,16,128]{3,2,1,0:T(8,128)} %get-tuple-element.494), channel_id=1, source_target_pairs={{0,1},{1,2},{2,3},{3,4},{4,5},{5,6},{6,7},{7,8},{8,9},{9,10},{10,1... | collective-permute-start | bytes 393224 | tf_op jit(solution)/shard_map/ppermute | solution.py:22
  7.3 91.7 %collective-permute-start.5 = (f32[1,2048]{1,0:T(1,128)}, f32[1,2048]{1,0:T(1,128)S(1)}, u32[]{:S(2)}, u32[]{:S(2)}) collective-permute-start(f32[1,2048]{1,0:T(1,128)} %get-tuple-element.583), channel_id=1, source_target_pairs={{1,0},{2,1},{3,2},{4,3},{5,4},{6,5},{7,6},{8,7},{9,8},{10,9},{11,1... | collective-permute-start | bytes 24584 | tf_op jit(solution)/shard_map/ppermute | solution.py:25
  8.6 90.4 %collective-permute-start.4 = (f32[1,2048]{1,0:T(1,128)}, f32[1,2048]{1,0:T(1,128)S(1)}, u32[]{:S(2)}, u32[]{:S(2)}) collective-permute-start(f32[1,2048]{1,0:T(1,128)} %get-tuple-element.582), channel_id=1, source_target_pairs={{0,1},{1,2},{2,3},{3,4},{4,5},{5,6},{6,7},{7,8},{8,9},{9,10},{10,1... | collective-permute-start | bytes 24584 | tf_op jit(solution)/shard_map/ppermute | solution.py:22
  35.6 15.6 %copy-start.28 = (s32[1024,1]{0,1:T(1,128)}, s32[1024,1]{0,1:T(1,128)S(1)}, u32[]{:S(2)}) copy-start(s32[1024,1]{0,1:T(1,128)S(1)} %constant_dynamic-slice_fusion.5) | copy-start | bytes 12292
  41.3 10.4 %copy-start.8 = (f32[4,16,128]{2,1,0:T(8,128)S(1)}, f32[4,16,128]{2,1,0:T(8,128)}, u32[]{:S(2)}) copy-start(f32[4,16,128]{2,1,0:T(8,128)} %get-tuple-element.559) | copy-start | bytes 98308
  41.3 10.4 %copy-start.9 = (f32[4,16,128]{2,1,0:T(8,128)S(1)}, f32[4,16,128]{2,1,0:T(8,128)}, u32[]{:S(2)}) copy-start(f32[4,16,128]{2,1,0:T(8,128)} %get-tuple-element.619) | copy-start | bytes 98308
  57.8 12.5 %copy-start.38 = (s32[1024]{0:T(1024)}, s32[1024]{0:T(1024)S(1)}, u32[]{:S(2)}) copy-start(s32[1024]{0:T(1024)S(1)} %fusion.66) | copy-start | bytes 12292
  63.4 6.3 %copy-start.41 = (s32[1024]{0:T(1024)S(1)}, s32[1024]{0:T(1024)}, u32[]{:S(2)}) copy-start(s32[1024]{0:T(1024)} %get-tuple-element.603) | copy-start | bytes 12292
  64.0 85.1 %collective-permute-start.3 = (f32[8,2,16,128]{3,2,1,0:T(8,128)S(1)}, f32[8,2,16,128]{3,2,1,0:T(8,128)S(1)}, u32[]{:S(2)}, u32[]{:S(2)}) collective-permute-start(f32[8,2,16,128]{3,2,1,0:T(8,128)S(1)} %get-tuple-element.425), channel_id=1, source_target_pairs={{1,0},{2,1},{3,2},{4,3},{5,4},{6,5},{7,6},{8,7},{9,8},{10,9},{11,1... | collective-permute-start | bytes 393224 | tf_op jit(solution)/shard_map/ppermute | solution.py:25
  65.3 83.8 %collective-permute-start.2 = (f32[8,2,16,128]{3,2,1,0:T(8,128)S(1)}, f32[8,2,16,128]{3,2,1,0:T(8,128)S(1)}, u32[]{:S(2)}, u32[]{:S(2)}) collective-permute-start(f32[8,2,16,128]{3,2,1,0:T(8,128)S(1)} %get-tuple-element.426), channel_id=1, source_target_pairs={{0,1},{1,2},{2,3},{3,4},{4,5},{5,6},{6,7},{7,8},{8,9},{9,10},{10,1... | collective-permute-start | bytes 393224 | tf_op jit(solution)/shard_map/ppermute | solution.py:22
  71.5 15.5 %all-to-all-start = ((f32[16,1,160]{2,1,0:T(1,128)}), f32[16,1,160]{2,1,0:T(1,128)}, u32[]{:S(2)}, u32[]{:S(2)}) async-start(f32[16,1,160]{2,1,0:T(1,128)} %copy.48), calls=%async_computation | async-start | bytes 32768 | tf_op jit(solution)/shard_map/all_to_all | solution.py:218
  87.8 11.2 %copy-start.6 = (f32[4,2047]{1,0:T(4,128)S(1)}, f32[4,2047]{1,0:T(4,128)}, u32[]{:S(2)}) copy-start(f32[4,2047]{1,0:T(4,128)} %get-tuple-element.580) | copy-start | bytes 98260
  87.8 11.3 %copy-start.7 = (f32[4,2047]{1,0:T(4,128)S(1)}, f32[4,2047]{1,0:T(4,128)}, u32[]{:S(2)}) copy-start(f32[4,2047]{1,0:T(4,128)} %get-tuple-element.581) | copy-start | bytes 98260
  87.8 11.3 %copy-start.35 = (f32[4,1]{1,0:T(4,128)S(1)}, f32[4,1]{1,0:T(4,128)}, u32[]{:S(2)}) copy-start(f32[4,1]{1,0:T(4,128)} %get-tuple-element.578) | copy-start | bytes 52
  87.8 11.3 %copy-start.36 = (f32[4,1]{1,0:T(4,128)S(1)}, f32[4,1]{1,0:T(4,128)}, u32[]{:S(2)}) copy-start(f32[4,1]{1,0:T(4,128)} %get-tuple-element.579) | copy-start | bytes 52
  99.3 4.4 %collective-permute-start.7 = (f32[1,2048]{1,0:T(1,128)S(1)}, f32[1,2048]{1,0:T(1,128)S(1)}, u32[]{:S(2)}, u32[]{:S(2)}) collective-permute-start(f32[1,2048]{1,0:T(1,128)S(1)} %get-tuple-element.577), channel_id=1, source_target_pairs={{1,0},{2,1},{3,2},{4,3},{5,4},{6,5},{7,6},{8,7},{9,8},{10,9},{11,1... | collective-permute-start | bytes 24584 | tf_op jit(solution)/shard_map/ppermute | solution.py:25
  100.6 3.8 %collective-permute-start.6 = (f32[1,2048]{1,0:T(1,128)S(1)}, f32[1,2048]{1,0:T(1,128)S(1)}, u32[]{:S(2)}, u32[]{:S(2)}) collective-permute-start(f32[1,2048]{1,0:T(1,128)S(1)} %get-tuple-element.576), channel_id=1, source_target_pairs={{0,1},{1,2},{2,3},{3,4},{4,5},{5,6},{6,7},{7,8},{8,9},{9,10},{10,1... | collective-permute-start | bytes 24584 | tf_op jit(solution)/shard_map/ppermute | solution.py:22
  104.7 4.9 %collective-permute-start.9 = (f32[1,2048]{1,0:T(1,128)S(1)}, f32[1,2048]{1,0:T(1,128)S(1)}, u32[]{:S(2)}, u32[]{:S(2)}) collective-permute-start(f32[1,2048]{1,0:T(1,128)S(1)} %get-tuple-element.571), channel_id=1, source_target_pairs={{1,0},{2,1},{3,2},{4,3},{5,4},{6,5},{7,6},{8,7},{9,8},{10,9},{11,1... | collective-permute-start | bytes 24584 | tf_op jit(solution)/shard_map/ppermute | solution.py:25
  106.0 4.3 %collective-permute-start.8 = (f32[1,2048]{1,0:T(1,128)S(1)}, f32[1,2048]{1,0:T(1,128)S(1)}, u32[]{:S(2)}, u32[]{:S(2)}) collective-permute-start(f32[1,2048]{1,0:T(1,128)S(1)} %get-tuple-element.570), channel_id=1, source_target_pairs={{0,1},{1,2},{2,3},{3,4},{4,5},{5,6},{6,7},{7,8},{8,9},{9,10},{10,1... | collective-permute-start | bytes 24584 | tf_op jit(solution)/shard_map/ppermute | solution.py:22
  110.3 7.2 %copy-start.34 = (f32[5,512]{1,0:T(8,128)S(1)}, f32[5,512]{1,0:T(8,128)}, u32[]{:S(2)}) copy-start(f32[5,512]{1,0:T(8,128)} %custom-call.1) | copy-start | bytes 30724
  110.5 6.2 %collective-permute-start.11 = (f32[1,2048]{1,0:T(1,128)S(1)}, f32[1,2048]{1,0:T(1,128)S(1)}, u32[]{:S(2)}, u32[]{:S(2)}) collective-permute-start(f32[1,2048]{1,0:T(1,128)S(1)} %get-tuple-element.565), channel_id=1, source_target_pairs={{1,0},{2,1},{3,2},{4,3},{5,4},{6,5},{7,6},{8,7},{9,8},{10,9},{11,1... | collective-permute-start | bytes 24584 | tf_op jit(solution)/shard_map/ppermute | solution.py:25
  111.8 5.6 %collective-permute-start.10 = (f32[1,2048]{1,0:T(1,128)S(1)}, f32[1,2048]{1,0:T(1,128)S(1)}, u32[]{:S(2)}, u32[]{:S(2)}) collective-permute-start(f32[1,2048]{1,0:T(1,128)S(1)} %get-tuple-element.564), channel_id=1, source_target_pairs={{0,1},{1,2},{2,3},{3,4},{4,5},{5,6},{6,7},{7,8},{8,9},{9,10},{10,1... | collective-permute-start | bytes 24584 | tf_op jit(solution)/shard_map/ppermute | solution.py:22
  117.5 23.9 %copy-start.14 = (f32[1,4,16,128]{3,2,1,0:T(8,128)S(1)}, f32[1,4,16,128]{3,2,1,0:T(8,128)}, u32[]{:S(2)}) copy-start(f32[1,4,16,128]{3,2,1,0:T(8,128)} %get-tuple-element.297) | copy-start | bytes 98308
  117.5 23.9 %copy-start.15 = (f32[1,4,16,128]{3,2,1,0:T(8,128)S(1)}, f32[1,4,16,128]{3,2,1,0:T(8,128)}, u32[]{:S(2)}) copy-start(f32[1,4,16,128]{3,2,1,0:T(8,128)} %get-tuple-element.298) | copy-start | bytes 98308
  117.5 23.9 %copy-start.16 = (f32[4,16,128]{2,1,0:T(8,128)S(1)}, f32[4,16,128]{2,1,0:T(8,128)}, u32[]{:S(2)}) copy-start(f32[4,16,128]{2,1,0:T(8,128)} %get-tuple-element.398) | copy-start | bytes 98308
  117.5 23.9 %copy-start.17 = (f32[1,4,16,128]{3,2,1,0:T(8,128)S(1)}, f32[1,4,16,128]{3,2,1,0:T(8,128)}, u32[]{:S(2)}) copy-start(f32[1,4,16,128]{3,2,1,0:T(8,128)} %get-tuple-element.455) | copy-start | bytes 98308
  117.6 23.9 %copy-start.18 = (f32[1,4,16,128]{3,2,1,0:T(8,128)S(1)}, f32[1,4,16,128]{3,2,1,0:T(8,128)}, u32[]{:S(2)}) copy-start(f32[1,4,16,128]{3,2,1,0:T(8,128)} %get-tuple-element.462) | copy-start | bytes 98308
  131.9 9.5 %copy-start.32 = (f32[4,2048]{1,0:T(4,128)}, f32[4,2048]{1,0:T(4,128)S(1)}, u32[]{:S(2)}) copy-start(f32[4,2048]{1,0:T(4,128)S(1)} %get-tuple-element.749) | copy-start | bytes 98308
  132.6 15.3 %all-to-all-start.1 = ((f32[16,1,160]{2,1,0:T(1,128)}), f32[16,1,160]{2,1,0:T(1,128)S(1)}, u32[]{:S(2)}, u32[]{:S(2)}) async-start(f32[16,1,160]{2,1,0:T(1,128)} %all_to_all.16), calls=%async_computation.1 | async-start | bytes 32768 | tf_op jit(solution)/shard_map/all_to_all | solution.py:258
  141.6 6.4 %copy-start.31 = (s32[1024,1]{0,1:T(1,128)S(1)}, s32[1024,1]{0,1:T(1,128)}, u32[]{:S(2)}) copy-start(s32[1024,1]{0,1:T(1,128)} %copy-done.28) | copy-start | bytes 12292
  141.6 6.3 %copy-start.39 = (s32[1024]{0:T(1024)S(1)}, s32[1024]{0:T(1024)}, u32[]{:S(2)}) copy-start(s32[1024]{0:T(1024)} %copy-done.38) | copy-start | bytes 12292
  (24 other events, 48.3 us)
where the time goes:
time: 155 us; the launch traced here: 152 us
  starting transfers between devices  49.2 us (32%)
  matrix products  39.4 us (25%)
  other arithmetic  26.8 us (17%)
  local copies, waits for them, and re-layouts  21.4 us (14%)
  waiting for transfers between devices  13.4 us (9%)
  between operations  1.87 us (1%)
    ppermute x6, starting transfers between devices, with_halo(): lax.ppermute(lax.slice_in_dim(block, block.shape[dim] - width, None, axis...  23.7 us
    dot_general x13, matrix products, exact_dot(): jnp.dot(left, right, precision=lax.Precision.HIGHEST, preferred_element_t...  19.9 us
    dot_general x1, matrix products, shards(): jnp.einsum('jsc,js->jc', selector, lon_float, precision=lax.Precision.HIG...  9.78 us
    dot_general x1, matrix products, shards(): jnp.einsum('jsc,js->jc', selector, row_float, precision=lax.Precision.HIG...  9.78 us
    another operation x4, other arithmetic  9.25 us
    all_to_all x1, starting transfers between devices, shards(): lax.all_to_all(outgoing, 'mag', split_axis=0, concat_axis=0, tiled=True)  8.94 us
    all_to_all x1, starting transfers between devices, shards(): lax.all_to_all(values, 'mag', split_axis=0, concat_axis=0, tiled=True)  8.79 us
    ppermute x6, starting transfers between devices, with_halo(): lax.ppermute(lax.slice_in_dim(block, 0, width, axis=dim), axis, backward)  7.71 us
  transfers between devices with their start and end apart: 14, of which 5 were waited for; matrix products, arithmetic and copies ran while one was open for 52% of the time, Pallas kernels for 0%

commit v1 on v0

v1 whole, which is shorter than its diff:
```python
import jax
import jax.numpy as jnp
from jax import lax
from jax.experimental import pallas as pl
from jax.experimental.pallas import tpu as pltpu
from jax.sharding import PartitionSpec as P

SWEEPS = 4
ADIABATIC = 5.0 / 3.0
TIME_STEP = 0.02
LON_WEIGHT = 0.25
LEAK_RATE = 0.05
SOURCE_GAIN = 10.0
LANES = 128
RIM = SWEEPS - 1

F32 = jnp.float32
BF16 = jnp.bfloat16
I32 = jnp.int32
VMEM = pl.BlockSpec(memory_space=pltpu.VMEM)
PARAMS = pltpu.CompilerParams(vmem_limit_bytes=48 * 1024 * 1024)


def call(kernel, outs, scratch=()):
    many = isinstance(outs, (list, tuple))
    return pl.pallas_call(
        kernel,
        out_shape=outs,
        out_specs=[VMEM] * len(outs) if many else VMEM,
        scratch_shapes=list(scratch),
        compiler_params=PARAMS,
    )


def pieces(values):
    first = values.astype(BF16)
    second = (values - first.astype(F32)).astype(BF16)
    return first, second


def rows_hot(key_row, count):
    keys = jnp.broadcast_to(key_row, (count, key_row.shape[1])).astype(BF16)
    index = lax.broadcasted_iota(I32, (count, key_row.shape[1]), 0).astype(F32).astype(BF16)
    return keys == index


def half_slope(lower, centre, upper):
    out = []
    for a, b, c in zip(lower, centre, upper):
        s, t = b - a, c - b
        out.append(0.5 * (jnp.maximum(jnp.minimum(s, t), 0.0) + jnp.minimum(jnp.maximum(s, t), 0.0)))
    return out


def dot3(a, b):
    return a[0] * b[0] + a[1] * b[1] + a[2] * b[2]


def conserved(q):
    rho, v, b, p = q[0], q[1:4], q[4:7], q[7]
    energy = p * (1.0 / (ADIABATIC - 1.0)) + 0.5 * rho * dot3(v, v) + 0.5 * dot3(b, b)
    return [rho, rho * v[0], rho * v[1], rho * v[2], b[0], b[1], b[2], energy]


def primitive(u):
    rho, b = u[0], u[4:7]
    inverse = 1.0 / rho
    v = [u[k] * inverse for k in (1, 2, 3)]
    p = (ADIABATIC - 1.0) * (u[7] - 0.5 * rho * dot3(v, v) - 0.5 * dot3(b, b))
    return [rho] + v + list(b) + [p]


def side(q, d):
    rho, v, b, p = q[0], q[1:4], q[4:7], q[7]
    b2 = dot3(b, b)
    half_b2 = 0.5 * b2
    total = p + half_b2
    mom = [rho * x for x in v]
    energy = p * (1.0 / (ADIABATIC - 1.0)) + 0.5 * dot3(mom, v) + half_b2
    vn, bn, mn = v[d], b[d], mom[d]
    flux = [mn]
    for k in range(3):
        f = mn * v[k] - bn * b[k]
        flux.append(f + total if k == d else f)
    for k in range(3):
        flux.append(None if k == d else vn * b[k] - bn * v[k])
    flux.append((energy + total) * vn - bn * dot3(v, b))
    speed = jnp.abs(vn) + jnp.sqrt((ADIABATIC * jnp.abs(p) + b2) / rho)
    return [rho] + mom + list(b) + [energy], flux, speed


def face(left, right, d):
    cons_l, flux_l, speed_l = side(left, d)
    cons_r, flux_r, speed_r = side(right, d)
    half_c = 0.5 * jnp.maximum(speed_l, speed_r)
    out = []
    for k in range(8):
        jump = half_c * (cons_r[k] - cons_l[k])
        out.append(-jump if flux_l[k] is None else 0.5 * (flux_l[k] + flux_r[k]) - jump)
    return out


def periodic(q, axis, d):
    size = q[0].shape[axis]
    back = [pltpu.roll(x, 1, axis) for x in q]
    ahead = [pltpu.roll(x, size - 1, axis) for x in q]
    slope = half_slope(back, q, ahead)
    left = [x + s for x, s in zip(q, slope)]
    right = [pltpu.roll(x - s, size - 1, axis) for x, s in zip(q, slope)]
    flux = face(left, right, d)
    return [pltpu.roll(f, 1, axis) - f for f in flux]


def add(a, b):
    return [x + y for x, y in zip(a, b)]


def plane(ref, x):
    return [ref[k, x] for k in range(8)]


def upper_face(ref, x):
    a, b, c, d = (plane(ref, x + k) for k in (-1, 0, 1, 2))
    left = add(b, half_slope(a, b, c))
    right = [v - s for v, s in zip(c, half_slope(b, c, d))]
    return face(left, right, 0)


def sweep_planes(ref, first, count, put):
    def body(step, below):
        x = first + step
        above = upper_face(ref, x)
        q = plane(ref, x)
        change = [f - g for f, g in zip(below, above)]
        change = add(change, periodic(q, 0, 1))
        change = add(change, periodic(q, 1, 2))
        put(x, step, q, change)
        return above

    lax.fori_loop(0, count, body, upper_face(ref, first - 1))


def stage_one(own_ref, low_ref, high_ref, next_ref, half_ref, pad_ref):
    me = lax.axis_index("mag")
    last = lax.axis_size("mag") - 1
    cx = own_ref.shape[1]
    for k in range(8):
        first_cell, last_cell = own_ref[k, 0], own_ref[k, cx - 1]
        for x in range(cx):
            pad_ref[k, x] = jnp.where(me == 0, first_cell, low_ref[k, x])
            pad_ref[k, cx + x] = own_ref[k, x]
            pad_ref[k, 2 * cx + x] = jnp.where(me == last, last_cell, high_ref[k, x])

    def put(x, step, q, change):
        start = conserved(q)
        first = [s + TIME_STEP * c for s, c in zip(start, change)]
        q1 = primitive(first)
        for k in range(8):
            next_ref[k, step] = q1[k]

        @pl.when(jnp.logical_and(step >= 2, step < cx + 2))
        def _():
            for k in range(8):
                half_ref[k, step - 2] = 0.5 * (start[k] + first[k])

    sweep_planes(pad_ref, cx - 2, cx + 4, put)

    @pl.when(me == 0)
    def _():
        for k in range(8):
            next_ref[k, 0] = next_ref[k, 2]
            next_ref[k, 1] = next_ref[k, 2]

    @pl.when(me == last)
    def _():
        for k in range(8):
            next_ref[k, cx + 2] = next_ref[k, cx + 1]
            next_ref[k, cx + 3] = next_ref[k, cx + 1]


def stage_two(next_ref, half_ref, rho_ref, vel_ref, mag_ref, prs_ref):
    cx = half_ref.shape[1]

    def put(x, step, q, change):
        final = [half_ref[k, step] + (0.5 * TIME_STEP) * change[k] for k in range(8)]
        q2 = primitive(final)
        rho_ref[step] = q2[0]
        for k in range(3):
            vel_ref[k, step] = q2[1 + k]
            mag_ref[k, step] = q2[4 + k]
        prs_ref[step] = q2[7]

    sweep_planes(next_ref, 2, cx, put)


def pick_current(own_ref, low_ref, high_ref, cell_ref, out_ref):
    me = lax.axis_index("mag")
    last = lax.axis_size("mag") - 1
    cx, ny, nz = own_ref.shape[1:]
    rows = []
    for x in range(cx):
        bx, by, bz = (own_ref[4 + k, x] for k in range(3))

        def neighbour(k, step):
            if 0 <= x + step < cx:
                return own_ref[4 + k, x + step]
            if step < 0:
                return jnp.where(me == 0, own_ref[4 + k, x], low_ref[4 + k, cx - 1])
            return jnp.where(me == last, own_ref[4 + k, x], high_ref[4 + k, 0])

        def along_x(k):
            return 0.5 * (neighbour(k, 1) - neighbour(k, -1))

        def along(v, axis):
            return 0.5 * (pltpu.roll(v, v.shape[axis] - 1, axis) - pltpu.roll(v, 1, axis))

        jx = along(bz, 0) - along(by, 1)
        jy = along(bx, 1) - along_x(2)
        jz = along_x(1) - along(bx, 0)
        norm = jnp.sqrt(bx * bx + by * by + bz * bz + 1.0)
        rows.append(SOURCE_GAIN * (jx * bx + jy * by + jz * bz) / norm)
    table = jnp.concatenate(rows, axis=0)
    count = table.shape[0]
    both = jnp.concatenate(pieces(table), axis=0)
    cells = cell_ref[...]
    hi, lo = cells // nz, (cells % nz).astype(F32)
    index = lax.broadcasted_iota(I32, (count, LANES), 0)
    one, zero = jnp.ones((), BF16), jnp.zeros((), BF16)
    for s in range(cells.shape[0]):
        hot = jnp.where(rows_hot(lo[s : s + 1], nz), one, zero)
        found = jnp.dot(both, hot, preferred_element_type=F32)
        found = found[:count] + found[count:]
        mine = jnp.where(index == hi[s : s + 1], found, 0.0)
        out_ref[s : s + 1, :] = jnp.sum(mine, axis=0, keepdims=True)


def east_of(v):
    lane = lax.broadcasted_iota(I32, v.shape, 2)
    turned = pltpu.roll(v, v.shape[2] - 1, 2)
    return jnp.where(lane == v.shape[2] - 1, pltpu.roll(turned, v.shape[1] - 1, 1), turned)


def west_of(v):
    lane = lax.broadcasted_iota(I32, v.shape, 2)
    turned = pltpu.roll(v, 1, 2)
    return jnp.where(lane == 0, pltpu.roll(turned, 1, 1), turned)


def solve(values_ref, owner_ref, row_ref, lon_ref, own_ref, low_ref, high_ref, phi_ref, flat_ref):
    me = lax.axis_index("mag")
    devices = lax.axis_size("mag")
    lat = own_ref.shape[1]
    strips = own_ref.shape[2]
    rows = lat + 2 * RIM
    count = rows * strips
    base = me * lat - RIM
    group = 8
    one, zero = jnp.ones((), BF16), jnp.zeros((), BF16)

    def body(step, total):
        at = pl.ds(pl.multiple_of(step * group, group), group)
        owner, row, lon = owner_ref[at, :], row_ref[at, :], lon_ref[at, :]
        hi = ((owner * lat + row - base) * strips + lon // LANES).astype(F32)
        lo = (lon % LANES).astype(F32)
        value = values_ref[at, :]
        high_piece = value.astype(BF16).astype(F32)
        low_piece = value - high_piece
        lefts, rights = [], []
        for s in range(group):
            lefts.append(jnp.where(rows_hot(hi[s : s + 1], count), one, zero))
            hot = rows_hot(lo[s : s + 1], LANES)
            two = []
            for piece in (high_piece, low_piece):
                wide = jnp.broadcast_to(piece[s : s + 1], (LANES, LANES)).astype(BF16)
                two.append(jnp.where(hot, wide, zero))
            rights.append(jnp.concatenate(two, axis=0))
        left = jnp.concatenate(lefts, axis=1)
        right = jnp.concatenate(rights, axis=1)
        return total + lax.dot_general(
            left, right, (((1,), (1,)), ((), ())), preferred_element_type=F32
        )

    steps = values_ref.shape[0] // group
    total = lax.fori_loop(0, steps, body, jnp.zeros((count, 2 * LANES), F32))
    source = (total[:, :LANES] + total[:, LANES:]).reshape(rows, strips, LANES)

    zeros = jnp.zeros((1, strips, LANES), F32)
    s_own, s_low, s_high = own_ref[8], low_ref[8], high_ref[8]
    s_low = jnp.where(me == 0, 0.0, s_low)
    s_high = jnp.where(me == devices - 1, 0.0, s_high)
    wide = jnp.concatenate([s_low[lat - RIM - 1 :], s_own, s_high[: RIM + 1]], axis=0)
    s = wide[1:-1]
    north = 0.5 * (s + wide[:-2])
    south = 0.5 * (s + wide[2:])
    east = (0.5 * LON_WEIGHT) * (s + east_of(s))
    west = (0.5 * LON_WEIGHT) * (s + west_of(s))
    diagonal = north + south + east + west + LEAK_RATE * s
    row = lax.broadcasted_iota(I32, s.shape, 0) + base
    inside = jnp.logical_and(row >= 0, row < devices * lat)
    inverse = jnp.where(inside, 1.0 / diagonal, 0.0)
    phi = source * inverse
    for sweep in range(1, SWEEPS):
        keep = slice(sweep, rows - sweep)
        middle = phi[1:-1]
        phi = (
            source[keep]
            + north[keep] * phi[:-2]
            + south[keep] * phi[2:]
            + east[keep] * east_of(middle)
            + west[keep] * west_of(middle)
        ) * inverse[keep]
    phi_ref[...] = phi
    for strip in range(strips):
        flat_ref[:, strip * LANES : (strip + 1) * LANES] = phi[:, strip, :]


def read_back(phi_ref, owner_ref, row_ref, lon_ref, out_ref):
    me = lax.axis_index("mag")
    total, strips = phi_ref.shape[:2]
    devices = lax.axis_size("mag")
    lat = total // devices
    block = min(256, total * strips)
    groups = total * strips // block
    table = phi_ref[...].reshape(groups, block, LANES)
    table = jnp.concatenate([table[g] for g in range(groups)], axis=1)
    both = jnp.concatenate(pieces(table), axis=0)
    mine = out_ref.shape[0]
    at = pl.ds(pl.multiple_of(me * mine, mine), mine)
    owner, row, lon = owner_ref[at, :], row_ref[at, :], lon_ref[at, :]
    hi = (owner * lat + row) * strips + lon // LANES
    group, hi, lo = hi // block, hi % block, lon % LANES
    one, zero = jnp.ones((), BF16), jnp.zeros((), BF16)
    index = lax.broadcasted_iota(I32, (block, LANES), 0)
    columns = []
    for s in range(mine):
        stack = []
        for g in range(groups):
            key = jnp.where(group[s : s + 1] == g, lo[s : s + 1], -1).astype(F32)
            stack.append(jnp.where(rows_hot(key, LANES), one, zero))
        columns.append(jnp.concatenate(stack, axis=0))
    found = jnp.dot(both, jnp.concatenate(columns, axis=1), preferred_element_type=F32)
    found = found[:block] + found[block:]
    for s in range(mine):
        part = found[:, s * LANES : (s + 1) * LANES]
        part = jnp.where(index == hi[s : s + 1], part, 0.0)
        out_ref[s : s + 1, :] = jnp.sum(part, axis=0, keepdims=True)


def shards(
    density, velocity, mag_field, pressure, conductance, shell_cell, foot_owner, foot_row, foot_lon
):
    devices = lax.axis_size("mag")
    cx, ny, nz = density.shape
    lat, columns = conductance.shape
    strips = columns // LANES
    shell_count = shell_cell.shape[0]
    shape = jax.ShapeDtypeStruct

    own = jnp.concatenate(
        [density[None], velocity, mag_field, pressure[None], conductance.reshape(1, lat, strips, LANES)],
        axis=0,
    )
    forward = [(i, i + 1) for i in range(devices - 1)]
    low = lax.ppermute(own, "mag", forward)
    high = lax.ppermute(own, "mag", [(b, a) for a, b in forward])

    cells = shell_cell.reshape(-1, LANES)
    owner = foot_owner.reshape(-1, LANES)
    row = foot_row.reshape(-1, LANES)
    lon = foot_lon.reshape(-1, LANES)

    currents = call(pick_current, shape(cells.shape, F32))(own, low, high, cells)
    values = lax.all_gather(currents, "mag", axis=0, tiled=True)

    slab = shape((8, cx, ny, nz), F32)
    following, half = call(
        stage_one,
        [shape((8, cx + 4, ny, nz), F32), slab],
        [pltpu.VMEM((8, 3 * cx, ny, nz), F32)],
    )(own, low, high)

    phi, potential = call(
        solve, [shape((lat, strips, LANES), F32), shape((lat, columns), F32)]
    )(values, owner, row, lon, own, low, high)
    all_phi = lax.all_gather(phi, "mag", axis=0, tiled=True)

    cell_shape = shape((cx, ny, nz), F32)
    vector_shape = shape((3, cx, ny, nz), F32)
    new_density, new_velocity, new_field, new_pressure = call(
        stage_two, [cell_shape, vector_shape, vector_shape, cell_shape]
    )(following, half)

    shell_potential = call(read_back, shape((shell_count // LANES, LANES), F32))(
        all_phi, owner, row, lon
    )
    return (
        new_density,
        new_velocity,
        new_field,
        new_pressure,
        potential,
        shell_potential.reshape(shell_count),
    )


def solution(mesh):
    both = ("parts", "mag")
    in_specs = (
        P(both, None, None),
        P(None, both, None, None),
        P(None, both, None, None),
        P(both, None, None),
        P(both, None),
        P("mag"),
        P(),
        P(),
        P(),
    )
    out_specs = (
        P(both, None, None),
        P(None, both, None, None),
        P(None, both, None, None),
        P(both, None, None),
        P(both, None),
        P(both),
    )
    return jax.shard_map(shards, mesh=mesh, in_specs=in_specs, out_specs=out_specs, check_vma=False)
```

time: 155 us -> 70 us (0.45); the launches traced: 152 us -> 69.5 us
  starting transfers between devices: 49.2 us -> 3.79 us
  blocking collectives: 0 us -> 44.4 us
  matrix products: 39.4 us -> 0 us
  other arithmetic: 26.8 us -> 0 us
  local copies, waits for them, and re-layouts: 21.4 us -> 3.22 us
  Pallas kernels: 0 us -> 13.1 us
  waiting for transfers between devices: 13.4 us -> 4.29 us
    all_gather x0 -> x2, blocking collectives: none -> 44.4 us  [the longest x1 25.6 us: shards(): values = lax.all_gather(currents, 'mag', axis=0, tiled=True)]
    dot_general x15 -> x0, matrix products: 39.4 us -> none  [the longest x13 19.9 us: exact_dot(): jnp.dot(left, right, precision=lax.Precision.HIGHEST, preferred_element_t...]
    ppermute x12 -> x2, starting transfers between devices: 31.4 us -> 3.79 us  [the longest x1 2.49 us: shards(): low = lax.ppermute(own, 'mag', forward)]
    all_to_all x2 -> x0, starting transfers between devices: 17.7 us -> none  [the longest x1 8.94 us: shards(): lax.all_to_all(outgoing, 'mag', split_axis=0, concat_axis=0, tiled=True)]
    pallas_call x0 -> x5, Pallas kernels: none -> 13.1 us  [the longest x1 6.32 us: shards(): call(solve, [shape((lat, strips, LANES), F32), shape((lat, columns), F32)])]
    all_to_all x2 -> x0, waiting for transfers between devices: 11.2 us -> none  [the longest x1 6.2 us: shards(): lax.all_to_all(values, 'mag', split_axis=0, concat_axis=0, tiled=True)]
    another operation x4 -> x0, other arithmetic: 9.25 us -> none
    dynamic_slice x16 -> x0, local copies, waits for them, and re-layouts: 7.51 us -> none  [the longest x15 7.5 us: shards(): lax.scan(add_block, jnp.zeros((lat_rows, columns), jnp.float32), (rows_bl...]
  transfers between devices with their start and end apart: 14 -> 2, of which waited for: 5 -> 1; matrix products, arithmetic and copies ran while one was open for 52% -> 0% of each run, Pallas kernels for 0% -> 0%
where the time goes in v1:
time: 70 us; the launch traced here: 69.5 us
  blocking collectives  44.4 us (63%)
  Pallas kernels  13.1 us (19%)
  waiting for transfers between devices  4.29 us (6%)
  starting transfers between devices  3.79 us (5%)
  local copies, waits for them, and re-layouts  3.22 us (5%)
    all_gather x1, blocking collectives, shards(): values = lax.all_gather(currents, 'mag', axis=0, tiled=True)  25.6 us
    all_gather x1, blocking collectives, shards(): all_phi = lax.all_gather(phi, 'mag', axis=0, tiled=True)  18.9 us
    pallas_call x1, Pallas kernels, shards(): call(solve, [shape((lat, strips, LANES), F32), shape((lat, columns), F32)])  6.32 us
    ppermute x1, waiting for transfers between devices, shards(): high = lax.ppermute(own, 'mag', [(b, a) for a, b in forward])  4.28 us
    unnamed x18, local copies, waits for them, and re-layouts  3.22 us
    pallas_call x1, Pallas kernels, shards(): call(stage_one, [shape((8, cx + 4, ny, nz), F32), slab], [pltpu.VMEM((8,...  3.02 us
    ppermute x1, starting transfers between devices, shards(): low = lax.ppermute(own, 'mag', forward)  2.49 us
    pallas_call x1, Pallas kernels, shards(): call(stage_two, [cell_shape, vector_shape, vector_shape, cell_shape])  2.13 us
  transfers between devices with their start and end apart: 2, of which 1 were waited for; matrix products, arithmetic and copies ran while one was open for 0% of the time, Pallas kernels for 0%

profile of v1, /device:TPU:0, one launch (start us, length us, event | category | flops | bytes accessed | tf_op | source)
XLA Modules:
  0.0 69.5 jit_solution(3730474780221083550)
XLA Ops:
  0.6 0.8 %bitcast_dynamic-update-slice_fusion.2 = f32[9,4,16,128]{3,2,1,0:T(8,128)S(1)} fusion(f32[4,16,128]{2,1,0:T(8,128)} %param.9), kind=kLoop, calls=%fused_computation.2 | loop fusion | bytes 65536
  1.4 0.0 copy-start.4
  1.4 0.9 %constant_dynamic-update-slice_fusion.1 = f32[9,4,16,128]{3,2,1,0:T(8,128)S(1)} fusion(f32[9,4,16,128]{3,2,1,0:T(8,128)S(1)} %bitcast_dynamic-update-slice_fusion.2, f32[3,4,16,128]{3,2,1,0:T(8,128)} %param.10), kind=kLoop, calls=%fused_computation.4 | loop fusion | bytes 196608
  2.3 0.0 copy-done.4
  2.3 0.0 copy-start.5
  2.4 0.7 %copy-done.5 = f32[4,16,128]{2,1,0:T(8,128)S(1)} copy-done((f32[4,16,128]{2,1,0:T(8,128)S(1)}, f32[4,16,128]{2,1,0:T(8,128)}, u32[]{:S(2)}) %copy-start.5) | copy-done | bytes 32792
  3.1 0.0 copy-start.6
  3.1 0.8 %copy-done.6 = f32[4,2048]{1,0:T(4,128)S(1)} copy-done((f32[4,2048]{1,0:T(4,128)S(1)}, f32[4,2048]{1,0:T(4,128)}, u32[]{:S(2)}) %copy-start.6) | copy-done | bytes 32792
  3.9 0.0 copy-start.3
  3.9 2.5 %collective-permute-start = (f32[9,4,16,128]{3,2,1,0:T(8,128)S(1)}, f32[9,4,16,128]{3,2,1,0:T(8,128)S(1)}, u32[]{:S(2)}, u32[]{:S(2)}) collective-permute-start(f32[9,4,16,128]{3,2,1,0:T(8,128)S(1)} %bitcast_dynamic-update-slice_fusion.own_ref), channel_id=1, source_target_pairs={{0,1},{1,2},{2,3},{3,4},{4,5},{5,6},{6,7},{7,8},{8,9},{9,10},{10,1... | collective-permute-start | bytes 884744 | tf_op jit(solution)/shard_map/ppermute | solution.py:364
  6.4 1.3 %collective-permute-start.1 = (f32[9,4,16,128]{3,2,1,0:T(8,128)S(1)}, f32[9,4,16,128]{3,2,1,0:T(8,128)S(1)}, u32[]{:S(2)}, u32[]{:S(2)}) collective-permute-start(f32[9,4,16,128]{3,2,1,0:T(8,128)S(1)} %bitcast_dynamic-update-slice_fusion.own_ref), channel_id=1, source_target_pairs={{1,0},{2,1},{3,2},{4,3},{5,4},{6,5},{7,6},{8,7},{9,8},{10,9},{11,1... | collective-permute-start | bytes 884744 | tf_op jit(solution)/shard_map/ppermute | solution.py:365
  7.7 0.0 collective-permute-done.low_ref
  7.7 4.3 %collective-permute-done.1.high_ref = f32[9,4,16,128]{3,2,1,0:T(8,128)S(1)} collective-permute-done((f32[9,4,16,128]{3,2,1,0:T(8,128)S(1)}, f32[9,4,16,128]{3,2,1,0:T(8,128)S(1)}, u32[]{:S(2)}, u32[]{:S(2)}) %collective-permute-start.1) | collective-permute-done | bytes 294944 | tf_op jit(solution)/shard_map/ppermute | solution.py:365
  12.0 0.0 copy-done.3
  12.0 0.0 copy-start.1
  12.0 0.0 copy-start.2
  12.0 0.3 shard_map.138
  12.3 0.0 copy-start
  12.3 25.6 %all_gather.6.values_ref = f32[128,128]{1,0:T(8,128)S(1)} all-gather(f32[8,128]{1,0:T(8,128)S(1)} %shard_map.138), channel_id=1, replica_groups=mesh['parts'=2,'mag'=16] {'mag'}, dimensions={0}, use_global_device_ids=true | all-gather | bytes 69632 | tf_op jit(solution)/shard_map/all_gather | solution.py:373
  37.8 0.0 copy-done.1
  37.8 0.0 copy-done.2
  37.8 0.0 copy-done
  37.9 6.3 %shard_map.139 = (f32[4,16,128]{2,1,0:T(8,128)S(1)}, f32[4,2048]{1,0:T(4,128)}) custom-call(f32[128,128]{1,0:T(8,128)S(1)} %all_gather.6.values_ref, s32[128,128]{1,0:T(8,128)S(1)} %bitcast.13, s32[128,128]{1,0:T(8,128)S(1)} %bitcast.15, s32[128,128]{1,0:T(8,128)S(1)} %bitcast.17, f32[9,4,16,128]{3,2,1,0:T(8,128)S(1)} %bitcast_dynamic-update-slice_fusion.own_ref, ...), custom_call_target="tpu_custom_call" | custom-call | tf_op jit(solution)/shard_map/pallas_call | solution.py:382
  44.2 18.9 %all_gather.7.phi_ref = f32[64,16,128]{2,1,0:T(8,128)S(1)} all-gather(f32[4,16,128]{2,1,0:T(8,128)S(1)} %get-tuple-element.21), channel_id=1, replica_groups=mesh['parts'=2,'mag'=16] {'mag'}, dimensions={0}, use_global_device_ids=true | all-gather | bytes 557056 | tf_op jit(solution)/shard_map/all_gather | solution.py:385
  63.0 1.3 %shard_map.140 = f32[8,128]{1,0:T(8,128)} custom-call(f32[64,16,128]{2,1,0:T(8,128)S(1)} %all_gather.7.phi_ref, s32[128,128]{1,0:T(8,128)S(1)} %bitcast.14, s32[128,128]{1,0:T(8,128)S(1)} %bitcast.16, s32[128,128]{1,0:T(8,128)S(1)} %bitcast.18), custom_call_target="tpu_custom_call" | custom-call | tf_op jit(solution)/shard_map/pallas_call | solution.py:393
  64.4 3.0 %shard_map.136 = (f32[8,8,16,128]{3,2,1,0:T(8,128)S(1)}, f32[8,4,16,128]{3,2,1,0:T(8,128)S(1)}) custom-call(f32[9,4,16,128]{3,2,1,0:T(8,128)S(1)} %bitcast_dynamic-update-slice_fusion.own_ref, f32[9,4,16,128]{3,2,1,0:T(8,128)S(1)} %collective-permute-done.low_ref, f32[9,4,16,128]{3,2,1,0:T(8,128)S(1)} %collective-permute-done.1.high_ref), custom_call_target="tpu_custom_call" | custom-call | tf_op jit(solution)/shard_map/pallas_call | solution.py:376
  67.4 2.1 %shard_map.137 = (f32[4,16,128]{2,1,0:T(8,128)}, f32[3,4,16,128]{3,2,1,0:T(8,128)}, f32[3,4,16,128]{3,2,1,0:T(8,128)}, f32[4,16,128]{2,1,0:T(8,128)}) custom-call(f32[8,8,16,128]{3,2,1,0:T(8,128)S(1)} %get-tuple-element.14.next_ref, f32[8,4,16,128]{3,2,1,0:T(8,128)S(1)} %get-tuple-element.15.half_ref), custom_call_target="tpu_custom_call" | custom-call | tf_op jit(solution)/shard_map/pallas_call | solution.py:389
  (3 shorter events, 0.0 us)
Async XLA Ops:
  1.4 0.9 %copy-start.4 = (f32[3,4,16,128]{3,2,1,0:T(8,128)S(1)}, f32[3,4,16,128]{3,2,1,0:T(8,128)}, u32[]{:S(2)}) copy-start(f32[3,4,16,128]{3,2,1,0:T(8,128)} %param.11) | copy-start | bytes 294916
  2.3 0.8 %copy-start.5 = (f32[4,16,128]{2,1,0:T(8,128)S(1)}, f32[4,16,128]{2,1,0:T(8,128)}, u32[]{:S(2)}) copy-start(f32[4,16,128]{2,1,0:T(8,128)} %param.12) | copy-start | bytes 98308
  3.1 0.8 %copy-start.6 = (f32[4,2048]{1,0:T(4,128)S(1)}, f32[4,2048]{1,0:T(4,128)}, u32[]{:S(2)}) copy-start(f32[4,2048]{1,0:T(4,128)} %param.13) | copy-start | bytes 98308
  3.9 8.1 %copy-start.3 = (s32[1024]{0:T(1024)S(1)}, s32[1024]{0:T(1024)}, u32[]{:S(2)}) copy-start(s32[1024]{0:T(1024)} %param.14) | copy-start | bytes 12292
  3.9 3.8 %collective-permute-start = (f32[9,4,16,128]{3,2,1,0:T(8,128)S(1)}, f32[9,4,16,128]{3,2,1,0:T(8,128)S(1)}, u32[]{:S(2)}, u32[]{:S(2)}) collective-permute-start(f32[9,4,16,128]{3,2,1,0:T(8,128)S(1)} %bitcast_dynamic-update-slice_fusion.own_ref), channel_id=1, source_target_pairs={{0,1},{1,2},{2,3},{3,4},{4,5},{5,6},{6,7},{7,8},{8,9},{9,10},{10,1... | collective-permute-start | bytes 884744 | tf_op jit(solution)/shard_map/ppermute | solution.py:364
  6.4 5.6 %collective-permute-start.1 = (f32[9,4,16,128]{3,2,1,0:T(8,128)S(1)}, f32[9,4,16,128]{3,2,1,0:T(8,128)S(1)}, u32[]{:S(2)}, u32[]{:S(2)}) collective-permute-start(f32[9,4,16,128]{3,2,1,0:T(8,128)S(1)} %bitcast_dynamic-update-slice_fusion.own_ref), channel_id=1, source_target_pairs={{1,0},{2,1},{3,2},{4,3},{5,4},{6,5},{7,6},{8,7},{9,8},{10,9},{11,1... | collective-permute-start | bytes 884744 | tf_op jit(solution)/shard_map/ppermute | solution.py:365
  12.0 25.9 %copy-start.1 = (s32[16384]{0:T(1024)S(1)}, s32[16384]{0:T(1024)}, u32[]{:S(2)}) copy-start(s32[16384]{0:T(1024)} %param.16) | copy-start | bytes 196612
  12.0 25.9 %copy-start.2 = (s32[16384]{0:T(1024)S(1)}, s32[16384]{0:T(1024)}, u32[]{:S(2)}) copy-start(s32[16384]{0:T(1024)} %param.17) | copy-start | bytes 196612
  12.3 25.6 %copy-start = (s32[16384,1]{0,1:T(1,128)S(1)}, s32[16384,1]{0,1:T(1,128)}, u32[]{:S(2)}) copy-start(s32[16384,1]{0,1:T(1,128)} %param.15) | copy-start | bytes 196612

commit v2 on v1

v2 whole, which is shorter than its diff:
```python
import jax
import jax.numpy as jnp
from jax import lax
from jax.experimental import pallas as pl
from jax.experimental.pallas import tpu as pltpu
from jax.sharding import PartitionSpec as P

SWEEPS = 4
ADIABATIC = 5.0 / 3.0
TIME_STEP = 0.02
LON_WEIGHT = 0.25
LEAK_RATE = 0.05
SOURCE_GAIN = 10.0
LANES = 128

F32 = jnp.float32
BF16 = jnp.bfloat16
I32 = jnp.int32
VMEM = pl.BlockSpec(memory_space=pltpu.VMEM)
MIB = 1024 * 1024


def call(kernel, outs, scratch=()):
    many = isinstance(outs, (list, tuple))
    return pl.pallas_call(
        kernel,
        out_shape=outs,
        out_specs=[VMEM] * len(outs) if many else VMEM,
        scratch_shapes=list(scratch),
        compiler_params=pltpu.CompilerParams(
            vmem_limit_bytes=(32 if lax.axis_size("mag") <= 32 else 60) * MIB
        ),
    )


def pieces(values):
    first = values.astype(BF16)
    second = (values - first.astype(F32)).astype(BF16)
    return first, second


def rows_hot(key_row, count, group=256):
    lanes = key_row.shape[1]
    out = []
    for first in range(0, count, group):
        size = min(group, count - first)
        key = jnp.broadcast_to(key_row - first, (16, lanes)).astype(BF16)
        keys = jnp.concatenate([key] * (size // 16), axis=0)
        index = lax.broadcasted_iota(I32, (size, lanes), 0).astype(F32).astype(BF16)
        out.append(jnp.where(keys == index, jnp.ones((), BF16), jnp.zeros((), BF16)))
    return jnp.concatenate(out, axis=0) if len(out) > 1 else out[0]


def half_slope(lower, centre, upper):
    out = []
    for a, b, c in zip(lower, centre, upper):
        s, t = b - a, c - b
        out.append(0.5 * (jnp.maximum(jnp.minimum(s, t), 0.0) + jnp.minimum(jnp.maximum(s, t), 0.0)))
    return out


def dot3(a, b):
    return a[0] * b[0] + a[1] * b[1] + a[2] * b[2]


def conserved(q):
    rho, v, b, p = q[0], q[1:4], q[4:7], q[7]
    energy = p * (1.0 / (ADIABATIC - 1.0)) + 0.5 * rho * dot3(v, v) + 0.5 * dot3(b, b)
    return [rho, rho * v[0], rho * v[1], rho * v[2], b[0], b[1], b[2], energy]


def primitive(u):
    rho, b = u[0], u[4:7]
    inverse = 1.0 / rho
    v = [u[k] * inverse for k in (1, 2, 3)]
    p = (ADIABATIC - 1.0) * (u[7] - 0.5 * rho * dot3(v, v) - 0.5 * dot3(b, b))
    return [rho] + v + list(b) + [p]


def side(q, d):
    rho, v, b, p = q[0], q[1:4], q[4:7], q[7]
    b2 = dot3(b, b)
    half_b2 = 0.5 * b2
    total = p + half_b2
    mom = [rho * x for x in v]
    energy = p * (1.0 / (ADIABATIC - 1.0)) + 0.5 * dot3(mom, v) + half_b2
    vn, bn, mn = v[d], b[d], mom[d]
    flux = [mn]
    for k in range(3):
        f = mn * v[k] - bn * b[k]
        flux.append(f + total if k == d else f)
    for k in range(3):
        flux.append(None if k == d else vn * b[k] - bn * v[k])
    flux.append((energy + total) * vn - bn * dot3(v, b))
    speed = jnp.abs(vn) + jnp.sqrt((ADIABATIC * jnp.abs(p) + b2) / rho)
    return [rho] + mom + list(b) + [energy], flux, speed


def face(left, right, d):
    cons_l, flux_l, speed_l = side(left, d)
    cons_r, flux_r, speed_r = side(right, d)
    half_c = 0.5 * jnp.maximum(speed_l, speed_r)
    out = []
    for k in range(8):
        jump = half_c * (cons_r[k] - cons_l[k])
        out.append(-jump if flux_l[k] is None else 0.5 * (flux_l[k] + flux_r[k]) - jump)
    return out


def periodic(q, axis, d):
    size = q[0].shape[axis]
    back = [pltpu.roll(x, 1, axis) for x in q]
    ahead = [pltpu.roll(x, size - 1, axis) for x in q]
    slope = half_slope(back, q, ahead)
    left = [x + s for x, s in zip(q, slope)]
    right = [pltpu.roll(x - s, size - 1, axis) for x, s in zip(q, slope)]
    flux = face(left, right, d)
    return [pltpu.roll(f, 1, axis) - f for f in flux]


def add(a, b):
    return [x + y for x, y in zip(a, b)]


def plane(ref, x):
    return [ref[k, x] for k in range(8)]


def upper_face(ref, x):
    a, b, c, d = (plane(ref, x + k) for k in (-1, 0, 1, 2))
    left = add(b, half_slope(a, b, c))
    right = [v - s for v, s in zip(c, half_slope(b, c, d))]
    return face(left, right, 0)


def sweep_planes(ref, first, count, put):
    def body(step, below):
        x = first + step
        above = upper_face(ref, x)
        q = plane(ref, x)
        change = [f - g for f, g in zip(below, above)]
        change = add(change, periodic(q, 0, 1))
        change = add(change, periodic(q, 1, 2))
        put(x, step, q, change)
        return above

    lax.fori_loop(0, count, body, upper_face(ref, first - 1))


def stage_one(
    rho_ref, vel_ref, mag_ref, prs_ref, mag_a, mag_b, five_a, five_b, next_ref, half_ref, pad_ref
):
    me = lax.axis_index("mag")
    last = lax.axis_size("mag") - 1
    even = me % 2 == 0
    cx = rho_ref.shape[0]

    def own(k, x):
        if k == 0:
            return rho_ref[x]
        if k == 7:
            return prs_ref[x]
        return vel_ref[k - 1, x] if k < 4 else mag_ref[k - 4, x]

    def partner(k, x, mag, five):
        if 4 <= k < 7:
            return mag[k - 4, x]
        return five[min(k, 4), x]

    for k in range(8):
        for x in range(cx):
            from_a, from_b = partner(k, x, mag_a, five_a), partner(k, x, mag_b, five_b)
            low = jnp.where(even, from_b, from_a)
            high = jnp.where(even, from_a, from_b)
            pad_ref[k, x] = jnp.where(me == 0, own(k, 0), low)
            pad_ref[k, cx + x] = own(k, x)
            pad_ref[k, 2 * cx + x] = jnp.where(me == last, own(k, cx - 1), high)

    def put(x, step, q, change):
        start = conserved(q)
        first = [s + TIME_STEP * c for s, c in zip(start, change)]
        q1 = primitive(first)
        for k in range(8):
            next_ref[k, step] = q1[k]

        @pl.when(jnp.logical_and(step >= 2, step < cx + 2))
        def _():
            for k in range(8):
                half_ref[k, step - 2] = 0.5 * (start[k] + first[k])

    sweep_planes(pad_ref, cx - 2, cx + 4, put)

    @pl.when(me == 0)
    def _():
        for k in range(8):
            next_ref[k, 0] = next_ref[k, 2]
            next_ref[k, 1] = next_ref[k, 2]

    @pl.when(me == last)
    def _():
        for k in range(8):
            next_ref[k, cx + 2] = next_ref[k, cx + 1]
            next_ref[k, cx + 3] = next_ref[k, cx + 1]


def stage_two(next_ref, half_ref, rho_ref, vel_ref, mag_ref, prs_ref):
    cx = half_ref.shape[1]

    def put(x, step, q, change):
        final = [half_ref[k, step] + (0.5 * TIME_STEP) * change[k] for k in range(8)]
        q2 = primitive(final)
        rho_ref[step] = q2[0]
        for k in range(3):
            vel_ref[k, step] = q2[1 + k]
            mag_ref[k, step] = q2[4 + k]
        prs_ref[step] = q2[7]

    sweep_planes(next_ref, 2, cx, put)


def pick_current(mag_ref, mag_a, mag_b, cell_ref, cond_ref, out_ref):
    me = lax.axis_index("mag")
    last = lax.axis_size("mag") - 1
    even = me % 2 == 0
    cx, ny, nz = mag_ref.shape[1:]
    rows = []
    for x in range(cx):
        bx, by, bz = (mag_ref[k, x] for k in range(3))

        def neighbour(k, step):
            if 0 <= x + step < cx:
                return mag_ref[k, x + step]
            if step < 0:
                below = jnp.where(even, mag_b[k, cx - 1], mag_a[k, cx - 1])
                return jnp.where(me == 0, mag_ref[k, x], below)
            above = jnp.where(even, mag_a[k, 0], mag_b[k, 0])
            return jnp.where(me == last, mag_ref[k, x], above)

        def along_x(k):
            return 0.5 * (neighbour(k, 1) - neighbour(k, -1))

        def along(v, axis):
            return 0.5 * (pltpu.roll(v, v.shape[axis] - 1, axis) - pltpu.roll(v, 1, axis))

        jx = along(bz, 0) - along(by, 1)
        jy = along(bx, 1) - along_x(2)
        jz = along_x(1) - along(bx, 0)
        norm = jnp.sqrt(bx * bx + by * by + bz * bz + 1.0)
        rows.append(SOURCE_GAIN * (jx * bx + jy * by + jz * bz) / norm)
    table = jnp.concatenate(rows, axis=0)
    count = table.shape[0]
    both = jnp.concatenate(pieces(table), axis=0)
    cells = cell_ref[...]
    hi, lo = cells // nz, (cells % nz).astype(F32)
    index = lax.broadcasted_iota(I32, (count, LANES), 0)
    points = cells.shape[0]
    for s in range(points):
        hot = rows_hot(lo[s : s + 1], nz)
        found = jnp.dot(both, hot, preferred_element_type=F32)
        found = found[:count] + found[count:]
        mine = jnp.where(index == hi[s : s + 1], found, 0.0)
        out_ref[s : s + 1, :] = jnp.sum(mine, axis=0, keepdims=True)
    lat, columns = cond_ref.shape
    strips = columns // LANES
    for r in range(lat):
        for strip in range(strips):
            place = points + r * strips + strip
            out_ref[place : place + 1, :] = cond_ref[
                r : r + 1, strip * LANES : (strip + 1) * LANES
            ]


def pack_five(rho_ref, vel_ref, prs_ref, out_ref):
    out_ref[0] = rho_ref[...]
    out_ref[1:4] = vel_ref[...]
    out_ref[4] = prs_ref[...]


def east_of(v):
    lane = lax.broadcasted_iota(I32, v.shape, 2)
    turned = pltpu.roll(v, v.shape[2] - 1, 2)
    return jnp.where(lane == v.shape[2] - 1, pltpu.roll(turned, v.shape[1] - 1, 1), turned)


def west_of(v):
    lane = lax.broadcasted_iota(I32, v.shape, 2)
    turned = pltpu.roll(v, 1, 2)
    return jnp.where(lane == 0, pltpu.roll(turned, 1, 1), turned)


def scatter_block(value, hi, lo, count):
    hi, lo = hi.astype(F32), lo.astype(F32)
    high_piece = value.astype(BF16).astype(F32)
    low_piece = value - high_piece
    lefts, rights = [], []
    for s in range(value.shape[0]):
        lefts.append(rows_hot(hi[s : s + 1], count))
        hot = rows_hot(lo[s : s + 1], LANES)
        two = []
        for piece in (high_piece, low_piece):
            wide = jnp.broadcast_to(piece[s : s + 1], (16, LANES)).astype(BF16)
            two.append(hot * jnp.concatenate([wide] * (LANES // 16), axis=0))
        rights.append(jnp.concatenate(two, axis=0))
    left = jnp.concatenate(lefts, axis=1)
    right = jnp.concatenate(rights, axis=1)
    return lax.dot_general(left, right, (((1,), (1,)), ((), ())), preferred_element_type=F32)


def repeat(count, body):
    if count <= 8:
        for i in range(count):
            body(i)
    else:
        lax.fori_loop(0, count, lambda i, carry: (body(i), carry)[1], 0)


def origin(me, devices, j):
    mask, bit, k = 0, devices // 2, 0
    while bit > 1:
        mask = mask + ((j >> k) & 1) * bit
        bit, k = bit // 2, k + 1
    return jnp.bitwise_xor(me, mask)


def scatter_new(first, blocks, points, lat, strips):
    def kernel(*refs):
        *total_in, load_ref, owner_ref, row_ref, lon_ref, out_ref = refs
        me = lax.axis_index("mag")
        devices = lax.axis_size("mag")
        count = out_ref.shape[0]
        rows = min(count, 1024)
        stride = load_ref.shape[0] // blocks

        def part(j, g, base_ref):
            device = origin(me, devices, first + j)
            at = pl.ds(pl.multiple_of(device * points, points), points)
            value = load_ref[pl.ds(pl.multiple_of(j * stride, 8), points), :]
            hi = (owner_ref[at, :] * lat + row_ref[at, :]) * strips + lon_ref[at, :] // LANES
            lo = lon_ref[at, :] % LANES
            new = scatter_block(value, hi - g * rows, lo, rows)
            place = pl.ds(pl.multiple_of(g * rows, rows), rows)
            out_ref[place, :] = new if base_ref is None else base_ref[place, :] + new

        def group(g):
            part(0, g, total_in[0] if total_in else None)
            repeat(blocks - 1, lambda j: part(j + 1, g, out_ref))

        repeat(count // rows, group)

    return kernel


def scatter_last(blocks, points, lat, strips):
    def kernel(total_ref, before_ref, load_ref, owner_ref, row_ref, lon_ref, out_ref, work_ref):
        half = blocks // 2
        scatter_new(half, half, points, lat, strips)(
            total_ref, load_ref, owner_ref, row_ref, lon_ref, work_ref
        )
        count = work_ref.shape[0]
        out_ref[:count, :] = work_ref[:, :LANES] + work_ref[:, LANES:]
        cells = lat * strips
        stride = points + cells
        for j in range(blocks):
            ref = before_ref if j < half else load_ref
            start = (j % half) * stride + points
            out_ref[count + j * cells : count + (j + 1) * cells, :] = ref[start : start + cells, :]

    return kernel


def solve_and_read(blocks, points, lat, strips):
    def kernel(
        mine_ref, their_ref, owner_ref, row_ref, lon_ref, flat_ref, out_ref, s_ref, w_ref, phi_ref
    ):
        me = lax.axis_index("mag")
        devices = lax.axis_size("mag")
        rows = devices * lat
        count = rows * strips
        cells = lat * strips
        zeros = jnp.zeros((1, strips, LANES), F32)
        for ref in (s_ref, phi_ref.at[0], phi_ref.at[1]):
            ref[0:1] = zeros
            ref[rows + 1 : rows + 2] = zeros

        def place(j):
            at = pl.ds(pl.multiple_of(count + j * cells, cells), cells)
            for ref, who in ((mine_ref, me), (their_ref, jnp.bitwise_xor(me, 1))):
                device = origin(who, devices, j)
                s_ref[pl.ds(device * lat + 1, lat)] = ref[at, :].reshape(lat, strips, LANES)

        repeat(blocks, place)
        chunk = min(8, rows)

        def prepare(i):
            r = i * chunk
            s, above, below = (s_ref[pl.ds(r + k, chunk)] for k in (1, 0, 2))
            north, south = 0.5 * (s + above), 0.5 * (s + below)
            east = (0.5 * LON_WEIGHT) * (s + east_of(s))
            west = (0.5 * LON_WEIGHT) * (s + west_of(s))
            inverse = 1.0 / (north + south + east + west + LEAK_RATE * s)
            at = pl.ds(pl.multiple_of(r * strips, 8), chunk * strips)
            source = (mine_ref[at, :] + their_ref[at, :]).reshape(chunk, strips, LANES)
            for k, value in enumerate((source, north, south, east, west)):
                w_ref[k, pl.ds(r, chunk)] = value * inverse
            phi_ref[0, pl.ds(r + 1, chunk)] = source * inverse

        repeat(rows // chunk, prepare)
        for sweep in range(SWEEPS - 1):
            old, new = sweep % 2, 1 - sweep % 2

            def relax(i):
                r = i * chunk
                phi, above, below = (phi_ref[old, pl.ds(r + k, chunk)] for k in (1, 0, 2))
                source, north, south, east, west = (w_ref[k, pl.ds(r, chunk)] for k in range(5))
                phi_ref[new, pl.ds(r + 1, chunk)] = (
                    source
                    + north * above
                    + south * below
                    + east * east_of(phi)
                    + west * west_of(phi)
                )

            repeat(rows // chunk, relax)
        last = (SWEEPS - 1) % 2
        own = phi_ref[last, pl.ds(me * lat + 1, lat)]
        for strip in range(strips):
            flat_ref[:, strip * LANES : (strip + 1) * LANES] = own[:, strip, :]

        block = min(256, count)
        groups = count // block
        table = phi_ref[last, pl.ds(1, rows)].reshape(count, LANES)
        table = jnp.concatenate([table[g * block : (g + 1) * block] for g in range(groups)], axis=1)
        both = jnp.concatenate(pieces(table), axis=0)
        at = pl.ds(pl.multiple_of(me * points, points), points)
        owner, row, lon = owner_ref[at, :], row_ref[at, :], lon_ref[at, :]
        hi = (owner * lat + row) * strips + lon // LANES
        group, hi, lo = hi // block, hi % block, lon % LANES
        index = lax.broadcasted_iota(I32, (block, LANES), 0)
        columns = []
        for p in range(points):
            stack = []
            for g in range(groups):
                key = jnp.where(group[p : p + 1] == g, lo[p : p + 1], -1).astype(F32)
                stack.append(rows_hot(key, LANES))
            columns.append(jnp.concatenate(stack, axis=0))
        found = jnp.dot(both, jnp.concatenate(columns, axis=1), preferred_element_type=F32)
        found = found[:block] + found[block:]
        for p in range(points):
            part = found[:, p * LANES : (p + 1) * LANES]
            part = jnp.where(index == hi[p : p + 1], part, 0.0)
            out_ref[p : p + 1, :] = jnp.sum(part, axis=0, keepdims=True)

    return kernel


def swap(values, bit):
    devices = lax.axis_size("mag")
    return lax.ppermute(values, "mag", [(i, i ^ bit) for i in range(devices)])


def swap_next(values):
    pairs = []
    for i in range(1, lax.axis_size("mag") - 1, 2):
        pairs += [(i, i + 1), (i + 1, i)]
    return lax.ppermute(values, "mag", pairs)


def shards(
    density, velocity, mag_field, pressure, conductance, shell_cell, foot_owner, foot_row, foot_lon
):
    devices = lax.axis_size("mag")
    cx, ny, nz = density.shape
    lat, columns = conductance.shape
    strips = columns // LANES
    shell_count = shell_cell.shape[0]
    points = shell_count // LANES
    cells = lat * strips
    count = devices * cells
    shape = jax.ShapeDtypeStruct

    mag_a, mag_b = swap(mag_field, 1), swap_next(mag_field)
    five = call(pack_five, shape((5, cx, ny, nz), F32))(density, velocity, pressure)

    owner = foot_owner.reshape(-1, LANES)
    row = foot_row.reshape(-1, LANES)
    lon = foot_lon.reshape(-1, LANES)

    load = call(pick_current, shape((points + cells, LANES), F32))(
        mag_field, mag_a, mag_b, shell_cell.reshape(-1, LANES), conductance
    )
    grid = shape((count, 2 * LANES), F32)
    total, new, blocks = (), load, 1
    bit = devices // 2
    while bit > 1:
        arrived = swap(load, bit)
        size = max(1, blocks // 2)
        kernel = scatter_new(blocks - size, size, points, lat, strips)
        total = (call(kernel, grid)(*total, new, owner, row, lon),)
        before, new = load, arrived
        load = jnp.concatenate([load, arrived], axis=0)
        blocks, bit = blocks * 2, bit // 2
    grids = shape((count + count // 2, LANES), F32)
    mine = call(
        scatter_last(blocks, points, lat, strips), grids, [pltpu.VMEM((count, 2 * LANES), F32)]
    )(*total, before, new, owner, row, lon)
    theirs = swap(mine, 1)

    five_a, five_b = swap(five, 1), swap_next(five)
    slab = shape((8, cx, ny, nz), F32)
    following, half = call(
        stage_one,
        [shape((8, cx + 4, ny, nz), F32), slab],
        [pltpu.VMEM((8, 3 * cx, ny, nz), F32)],
    )(density, velocity, mag_field, pressure, mag_a, mag_b, five_a, five_b)
    cell_shape = shape((cx, ny, nz), F32)
    vector_shape = shape((3, cx, ny, nz), F32)
    new_density, new_velocity, new_field, new_pressure = call(
        stage_two, [cell_shape, vector_shape, vector_shape, cell_shape]
    )(following, half)

    potential, shell_potential = call(
        solve_and_read(blocks, points, lat, strips),
        [shape((lat, columns), F32), shape((points, LANES), F32)],
        [
            pltpu.VMEM((devices * lat + 2, strips, LANES), F32),
            pltpu.VMEM((5, devices * lat, strips, LANES), F32),
            pltpu.VMEM((2, devices * lat + 2, strips, LANES), F32),
        ],
    )(mine, theirs, owner, row, lon)
    return (
        new_density,
        new_velocity,
        new_field,
        new_pressure,
        potential,
        shell_potential.reshape(shell_count),
    )


def solution(mesh):
    both = ("parts", "mag")
    in_specs = (
        P(both, None, None),
        P(None, both, None, None),
        P(None, both, None, None),
        P(both, None, None),
        P(both, None),
        P("mag"),
        P(),
        P(),
        P(),
    )
    out_specs = (
        P(both, None, None),
        P(None, both, None, None),
        P(None, both, None, None),
        P(both, None, None),
        P(both, None),
        P(both),
    )
    return jax.shard_map(shards, mesh=mesh, in_specs=in_specs, out_specs=out_specs, check_vma=False)
```

time: 70 us -> 45.4 us (0.65)
  the two profiles are of different devices: /device:TPU:0 before, /device:TPU:25 now
where the time goes in v2:
time: 45.4 us; the launch traced here: 45.2 us
  waiting for transfers between devices  19.2 us (42%)
  Pallas kernels  13.3 us (29%)
  starting transfers between devices  9.51 us (21%)
  local copies, waits for them, and re-layouts  2.38 us (5%)
  between operations  0.81 us (2%)
    ppermute x2, waiting for transfers between devices, swap_next(): return lax.ppermute(values, 'mag', pairs)  9.95 us
    ppermute x6, waiting for transfers between devices, swap(): return lax.ppermute(values, 'mag', [(i, i ^ bit) for i in range(devices)])  9.22 us
    ppermute x2, starting transfers between devices, swap_next(): return lax.ppermute(values, 'mag', pairs)  5.59 us
    ppermute x6, starting transfers between devices, swap(): return lax.ppermute(values, 'mag', [(i, i ^ bit) for i in range(devices)])  3.93 us
    pallas_call x1, Pallas kernels, shards(): call(stage_one, [shape((8, cx + 4, ny, nz), F32), slab], [pltpu.VMEM((8,...  3.02 us
    pallas_call x3, Pallas kernels, shards(): total = (call(kernel, grid)(*total, new, owner, row, lon),)  2.82 us
    pallas_call x1, Pallas kernels, shards(): call(solve_and_read(blocks, points, lat, strips), [shape((lat, columns),...  2.57 us
    pallas_call x1, Pallas kernels, shards(): call(scatter_last(blocks, points, lat, strips), grids, [pltpu.VMEM((count...  2.39 us
  transfers between devices with their start and end apart: 8, of which 5 were waited for; matrix products, arithmetic and copies ran while one was open for 0% of the time, Pallas kernels for 18%

profile of v2, /device:TPU:25, one launch (start us, length us, event | category | flops | bytes accessed | tf_op | source)
XLA Modules:
  0.0 45.2 jit_solution(13198490280556099986)
XLA Ops:
  0.6 0.7 %collective-permute-start = (f32[3,4,16,128]{3,2,1,0:T(8,128)}, f32[3,4,16,128]{3,2,1,0:T(8,128)S(1)}, u32[]{:S(2)}, u32[]{:S(2)}) collective-permute-start(f32[3,4,16,128]{3,2,1,0:T(8,128)} %mag_ref.3), channel_id=1, source_target_pairs={{0,1},{1,0},{2,3},{3,2},{4,5},{5,4},{6,7},{7,6},{8,9},{9,8},{10,11... | collective-permute-start | bytes 294920 | tf_op jit(solution)/shard_map/ppermute | solution.py:458
  1.4 3.1 %collective-permute-start.1 = (f32[3,4,16,128]{3,2,1,0:T(8,128)}, f32[3,4,16,128]{3,2,1,0:T(8,128)S(1)}, u32[]{:S(2)}, u32[]{:S(2)}) collective-permute-start(f32[3,4,16,128]{3,2,1,0:T(8,128)} %mag_ref.3), channel_id=1, source_target_pairs={{1,2},{2,1},{3,4},{4,3},{5,6},{6,5},{7,8},{8,7},{9,10},{10,9},{11,... | collective-permute-start | bytes 294920 | tf_op jit(solution)/shard_map/ppermute | solution.py:465
  4.4 0.0 collective-permute-done.mag_a
  4.4 4.1 %collective-permute-done.1.mag_b = f32[3,4,16,128]{3,2,1,0:T(8,128)S(1)} collective-permute-done((f32[3,4,16,128]{3,2,1,0:T(8,128)}, f32[3,4,16,128]{3,2,1,0:T(8,128)S(1)}, u32[]{:S(2)}, u32[]{:S(2)}) %collective-permute-start.1) | collective-permute-done | bytes 98336 | tf_op jit(solution)/shard_map/ppermute | solution.py:465
  8.6 0.9 %copy-done.4 = f32[3,4,16,128]{3,2,1,0:T(8,128)S(1)} copy-done((f32[3,4,16,128]{3,2,1,0:T(8,128)S(1)}, f32[3,4,16,128]{3,2,1,0:T(8,128)}, u32[]{:S(2)}) %copy-start.4) | copy-done | bytes 98328
  9.5 0.8 %copy-done.8 = f32[4,2048]{1,0:T(4,128)S(1)} copy-done((f32[4,2048]{1,0:T(4,128)S(1)}, f32[4,2048]{1,0:T(4,128)}, u32[]{:S(2)}) %copy-start.8) | copy-done | bytes 32792
  10.2 0.7 %copy-done.9 = s32[1024]{0:T(1024)S(1)} copy-done((s32[1024]{0:T(1024)S(1)}, s32[1024]{0:T(1024)}, u32[]{:S(2)}) %copy-start.9) | copy-done | bytes 4120
  10.9 0.3 shard_map.139.refs_0_
  11.2 0.1 collective-permute-start.4
  11.3 5.0 %collective-permute-done.4.refs_1_ = f32[72,128]{1,0:T(8,128)S(1)} collective-permute-done((f32[72,128]{1,0:T(8,128)S(1)}, f32[72,128]{1,0:T(8,128)S(1)}, u32[]{:S(2)}, u32[]{:S(2)}) %collective-permute-start.4) | collective-permute-done | bytes 36896 | tf_op jit(solution)/shard_map/ppermute | solution.py:458
  16.3 0.0 copy-start.1
  16.3 0.0 copy-start.2
  16.3 0.1 collective-permute-start.5
  16.4 3.2 %collective-permute-done.5.refs_1_ = f32[144,128]{1,0:T(8,128)S(1)} collective-permute-done((f32[144,128]{1,0:T(8,128)S(1)}, f32[144,128]{1,0:T(8,128)S(1)}, u32[]{:S(2)}, u32[]{:S(2)}) %collective-permute-start.5) | collective-permute-done | bytes 73760 | tf_op jit(solution)/shard_map/ppermute | solution.py:458
  19.6 0.1 collective-permute-start.6
  19.7 0.8 %shard_map.140.refs_0_ = f32[1024,256]{1,0:T(8,128)S(1)} custom-call(f32[72,128]{1,0:T(8,128)S(1)} %shard_map.139.refs_0_, s32[128,128]{1,0:T(8,128)S(1)} %bitcast.5, s32[128,128]{1,0:T(8,128)S(1)} %bitcast.10, s32[128,128]{1,0:T(8,128)S(1)} %bitcast.15), custom_call_target="tpu_custom_call" | custom-call | tf_op jit(solution)/shard_map/pallas_call | solution.py:498
  20.5 0.8 %shard_map.141.refs_0_ = f32[1024,256]{1,0:T(8,128)S(1)} custom-call(f32[1024,256]{1,0:T(8,128)S(1)} %shard_map.140.refs_0_, f32[72,128]{1,0:T(8,128)S(1)} %collective-permute-done.4.refs_1_, s32[128,128]{1,0:T(8,128)S(1)} %bitcast.6, s32[128,128]{1,0:T(8,128)S(1)} %bitcast.11, s32[128,128]{1,0:T(8,128)S(1)} %bitcast.16), custom_call_target="tpu_custom_call" | custom-call | tf_op jit(solution)/shard_map/pallas_call | solution.py:498
  21.3 1.3 %shard_map.142.total_ref = f32[1024,256]{1,0:T(8,128)S(1)} custom-call(f32[1024,256]{1,0:T(8,128)S(1)} %shard_map.141.refs_0_, f32[144,128]{1,0:T(8,128)S(1)} %collective-permute-done.5.refs_1_, s32[128,128]{1,0:T(8,128)S(1)} %bitcast.7, s32[128,128]{1,0:T(8,128)S(1)} %bitcast.12, s32[128,128]{1,0:T(8,128)S(1)} %bitcast.17), custom_call_target="tpu_custom_call" | custom-call | tf_op jit(solution)/shard_map/pallas_call | solution.py:498
  22.6 0.0 copy-start.3
  22.6 0.0 copy-start.6
  22.6 0.0 copy-start.7
  22.6 1.1 %collective-permute-done.6.load_ref = f32[288,128]{1,0:T(8,128)S(1)} collective-permute-done((f32[288,128]{1,0:T(8,128)S(1)}, f32[288,128]{1,0:T(8,128)S(1)}, u32[]{:S(2)}, u32[]{:S(2)}) %collective-permute-start.6) | collective-permute-done | bytes 147488 | tf_op jit(solution)/shard_map/ppermute | solution.py:458
  23.7 2.4 %shard_map.143.mine_ref = f32[1536,128]{1,0:T(8,128)S(1)} custom-call(f32[1024,256]{1,0:T(8,128)S(1)} %shard_map.142.total_ref, f32[288,128]{1,0:T(8,128)S(1)} %pad_maximum_fusion.before_ref, f32[288,128]{1,0:T(8,128)S(1)} %collective-permute-done.6.load_ref, s32[128,128]{1,0:T(8,128)S(1)} %bitcast.8, s32[128,128]{1,0:T(8,128)S(1)} %bitcast.13, ...), custom_call_target="tpu_custom_call" | custom-call | tf_op jit(solution)/shard_map/pallas_call | solution.py:503
  26.1 0.0 copy-start.5
  26.1 2.8 %collective-permute-start.7 = (f32[1536,128]{1,0:T(8,128)S(1)}, f32[1536,128]{1,0:T(8,128)S(1)}, u32[]{:S(2)}, u32[]{:S(2)}) collective-permute-start(f32[1536,128]{1,0:T(8,128)S(1)} %shard_map.143.mine_ref), channel_id=1, source_target_pairs={{0,1},{1,0},{2,3},{3,2},{4,5},{5,4},{6,7},{7,6},{8,9},{9,8},{10,11... | collective-permute-start | bytes 2359304 | tf_op jit(solution)/shard_map/ppermute | solution.py:458
  28.9 0.1 collective-permute-start.2
  29.0 2.5 %collective-permute-start.3 = (f32[5,4,16,128]{3,2,1,0:T(8,128)S(1)}, f32[5,4,16,128]{3,2,1,0:T(8,128)S(1)}, u32[]{:S(2)}, u32[]{:S(2)}) collective-permute-start(f32[5,4,16,128]{3,2,1,0:T(8,128)S(1)} %shard_map.136), channel_id=1, source_target_pairs={{1,2},{2,1},{3,4},{4,3},{5,6},{6,5},{7,8},{8,7},{9,10},{10,9},{11,... | collective-permute-start | bytes 491528 | tf_op jit(solution)/shard_map/ppermute | solution.py:465
  31.6 0.0 collective-permute-done.2.five_a
  31.6 5.8 %collective-permute-done.3.five_b = f32[5,4,16,128]{3,2,1,0:T(8,128)S(1)} collective-permute-done((f32[5,4,16,128]{3,2,1,0:T(8,128)S(1)}, f32[5,4,16,128]{3,2,1,0:T(8,128)S(1)}, u32[]{:S(2)}, u32[]{:S(2)}) %collective-permute-start.3) | collective-permute-done | bytes 163872 | tf_op jit(solution)/shard_map/ppermute | solution.py:465
  37.4 3.0 %shard_map.137 = (f32[8,8,16,128]{3,2,1,0:T(8,128)S(1)}, f32[8,4,16,128]{3,2,1,0:T(8,128)S(1)}) custom-call(f32[4,16,128]{2,1,0:T(8,128)S(1)} %copy-done.6, f32[3,4,16,128]{3,2,1,0:T(8,128)S(1)} %copy-done.3, f32[3,4,16,128]{3,2,1,0:T(8,128)S(1)} %copy-done.5, f32[4,16,128]{2,1,0:T(8,128)S(1)} %copy-done.7, ...), custom_call_target="tpu_custom_call" | custom-call | tf_op jit(solution)/shard_map/pallas_call | solution.py:510
  40.4 2.1 %shard_map.138 = (f32[4,16,128]{2,1,0:T(8,128)}, f32[3,4,16,128]{3,2,1,0:T(8,128)}, f32[3,4,16,128]{3,2,1,0:T(8,128)}, f32[4,16,128]{2,1,0:T(8,128)}) custom-call(f32[8,8,16,128]{3,2,1,0:T(8,128)S(1)} %get-tuple-element.14.next_ref, f32[8,4,16,128]{3,2,1,0:T(8,128)S(1)} %get-tuple-element.15.half_ref), custom_call_target="tpu_custom_call" | custom-call | tf_op jit(solution)/shard_map/pallas_call | solution.py:517
  42.6 2.6 %shard_map.144 = (f32[4,2048]{1,0:T(4,128)}, f32[8,128]{1,0:T(8,128)}) custom-call(f32[1536,128]{1,0:T(8,128)S(1)} %shard_map.143.mine_ref, f32[1536,128]{1,0:T(8,128)S(1)} %collective-permute-done.7.their_ref, s32[128,128]{1,0:T(8,128)S(1)} %bitcast.9, s32[128,128]{1,0:T(8,128)S(1)} %bitcast.14, s32[128,128]{1,0:T(8,128)S(1)} %bitcast.19), custom_call_target="tpu_custom_call" | custom-call | tf_op jit(solution)/shard_map/pallas_call | solution.py:521
  (15 shorter events, 0.1 us)
Async XLA Ops:
  0.6 3.8 %collective-permute-start = (f32[3,4,16,128]{3,2,1,0:T(8,128)}, f32[3,4,16,128]{3,2,1,0:T(8,128)S(1)}, u32[]{:S(2)}, u32[]{:S(2)}) collective-permute-start(f32[3,4,16,128]{3,2,1,0:T(8,128)} %mag_ref.3), channel_id=1, source_target_pairs={{0,1},{1,0},{2,3},{3,2},{4,5},{5,4},{6,7},{7,6},{8,9},{9,8},{10,11... | collective-permute-start | bytes 294920 | tf_op jit(solution)/shard_map/ppermute | solution.py:458
  1.4 7.2 %collective-permute-start.1 = (f32[3,4,16,128]{3,2,1,0:T(8,128)}, f32[3,4,16,128]{3,2,1,0:T(8,128)S(1)}, u32[]{:S(2)}, u32[]{:S(2)}) collective-permute-start(f32[3,4,16,128]{3,2,1,0:T(8,128)} %mag_ref.3), channel_id=1, source_target_pairs={{1,2},{2,1},{3,4},{4,3},{5,6},{6,5},{7,8},{8,7},{9,10},{10,9},{11,... | collective-permute-start | bytes 294920 | tf_op jit(solution)/shard_map/ppermute | solution.py:465
  8.6 0.9 %copy-start.4 = (f32[3,4,16,128]{3,2,1,0:T(8,128)S(1)}, f32[3,4,16,128]{3,2,1,0:T(8,128)}, u32[]{:S(2)}) copy-start(f32[3,4,16,128]{3,2,1,0:T(8,128)} %mag_ref.3) | copy-start | bytes 294916
  9.5 0.8 %copy-start.8 = (f32[4,2048]{1,0:T(4,128)S(1)}, f32[4,2048]{1,0:T(4,128)}, u32[]{:S(2)}) copy-start(f32[4,2048]{1,0:T(4,128)} %cond_ref.1) | copy-start | bytes 98308
  10.2 0.7 %copy-start.9 = (s32[1024]{0:T(1024)S(1)}, s32[1024]{0:T(1024)}, u32[]{:S(2)}) copy-start(s32[1024]{0:T(1024)} %param.14) | copy-start | bytes 12292
  11.2 5.1 %collective-permute-start.4 = (f32[72,128]{1,0:T(8,128)S(1)}, f32[72,128]{1,0:T(8,128)S(1)}, u32[]{:S(2)}, u32[]{:S(2)}) collective-permute-start(f32[72,128]{1,0:T(8,128)S(1)} %shard_map.139.refs_0_), channel_id=1, source_target_pairs={{0,8},{1,9},{2,10},{3,11},{4,12},{5,13},{6,14},{7,15},{8,0},{9,1},... | collective-permute-start | bytes 110600 | tf_op jit(solution)/shard_map/ppermute | solution.py:458
  16.3 3.4 %copy-start = (s32[16384,1]{0,1:T(1,128)S(1)}, s32[16384,1]{0,1:T(1,128)}, u32[]{:S(2)}) copy-start(s32[16384,1]{0,1:T(1,128)} %param.15) | copy-start | bytes 196612
  16.3 3.4 %copy-start.1 = (s32[16384]{0:T(1024)S(1)}, s32[16384]{0:T(1024)}, u32[]{:S(2)}) copy-start(s32[16384]{0:T(1024)} %param.16) | copy-start | bytes 196612
  16.3 3.4 %copy-start.2 = (s32[16384]{0:T(1024)S(1)}, s32[16384]{0:T(1024)}, u32[]{:S(2)}) copy-start(s32[16384]{0:T(1024)} %param.17) | copy-start | bytes 196612
  16.3 3.3 %collective-permute-start.5 = (f32[144,128]{1,0:T(8,128)S(1)}, f32[144,128]{1,0:T(8,128)S(1)}, u32[]{:S(2)}, u32[]{:S(2)}) collective-permute-start(f32[144,128]{1,0:T(8,128)S(1)} %pad_maximum_fusion.1), channel_id=1, source_target_pairs={{0,4},{1,5},{2,6},{3,7},{4,0},{5,1},{6,2},{7,3},{8,12},{9,13},{10,... | collective-permute-start | bytes 221192 | tf_op jit(solution)/shard_map/ppermute | solution.py:458
  19.6 4.1 %collective-permute-start.6 = (f32[288,128]{1,0:T(8,128)S(1)}, f32[288,128]{1,0:T(8,128)S(1)}, u32[]{:S(2)}, u32[]{:S(2)}) collective-permute-start(f32[288,128]{1,0:T(8,128)S(1)} %pad_maximum_fusion.before_ref), channel_id=1, source_target_pairs={{0,2},{1,3},{2,0},{3,1},{4,6},{5,7},{6,4},{7,5},{8,10},{9,11},{10,... | collective-permute-start | bytes 442376 | tf_op jit(solution)/shard_map/ppermute | solution.py:458
  22.6 6.3 %copy-start.3 = (f32[3,4,16,128]{3,2,1,0:T(8,128)S(1)}, f32[3,4,16,128]{3,2,1,0:T(8,128)}, u32[]{:S(2)}) copy-start(f32[3,4,16,128]{3,2,1,0:T(8,128)} %vel_ref.3) | copy-start | bytes 294916
  22.6 6.3 %copy-start.6 = (f32[4,16,128]{2,1,0:T(8,128)S(1)}, f32[4,16,128]{2,1,0:T(8,128)}, u32[]{:S(2)}) copy-start(f32[4,16,128]{2,1,0:T(8,128)} %rho_ref.3) | copy-start | bytes 98308
  22.6 6.3 %copy-start.7 = (f32[4,16,128]{2,1,0:T(8,128)S(1)}, f32[4,16,128]{2,1,0:T(8,128)}, u32[]{:S(2)}) copy-start(f32[4,16,128]{2,1,0:T(8,128)} %prs_ref.3) | copy-start | bytes 98308
  26.1 11.3 %copy-start.5 = (f32[3,4,16,128]{3,2,1,0:T(8,128)S(1)}, f32[3,4,16,128]{3,2,1,0:T(8,128)}, u32[]{:S(2)}) copy-start(f32[3,4,16,128]{3,2,1,0:T(8,128)} %mag_ref.3) | copy-start | bytes 294916
  26.1 16.5 %collective-permute-start.7 = (f32[1536,128]{1,0:T(8,128)S(1)}, f32[1536,128]{1,0:T(8,128)S(1)}, u32[]{:S(2)}, u32[]{:S(2)}) collective-permute-start(f32[1536,128]{1,0:T(8,128)S(1)} %shard_map.143.mine_ref), channel_id=1, source_target_pairs={{0,1},{1,0},{2,3},{3,2},{4,5},{5,4},{6,7},{7,6},{8,9},{9,8},{10,11... | collective-permute-start | bytes 2359304 | tf_op jit(solution)/shard_map/ppermute | solution.py:458
  28.9 2.7 %collective-permute-start.2 = (f32[5,4,16,128]{3,2,1,0:T(8,128)S(1)}, f32[5,4,16,128]{3,2,1,0:T(8,128)S(1)}, u32[]{:S(2)}, u32[]{:S(2)}) collective-permute-start(f32[5,4,16,128]{3,2,1,0:T(8,128)S(1)} %shard_map.136), channel_id=1, source_target_pairs={{0,1},{1,0},{2,3},{3,2},{4,5},{5,4},{6,7},{7,6},{8,9},{9,8},{10,11... | collective-permute-start | bytes 491528 | tf_op jit(solution)/shard_map/ppermute | solution.py:458
  29.0 8.4 %collective-permute-start.3 = (f32[5,4,16,128]{3,2,1,0:T(8,128)S(1)}, f32[5,4,16,128]{3,2,1,0:T(8,128)S(1)}, u32[]{:S(2)}, u32[]{:S(2)}) collective-permute-start(f32[5,4,16,128]{3,2,1,0:T(8,128)S(1)} %shard_map.136), channel_id=1, source_target_pairs={{1,2},{2,1},{3,4},{4,3},{5,6},{6,5},{7,8},{8,7},{9,10},{10,9},{11,... | collective-permute-start | bytes 491528 | tf_op jit(solution)/shard_map/ppermute | solution.py:465

commit v3 on v2

--- a/solution.py
+++ b/solution.py
@@ -17,13 +17,28 @@
 BF16 = jnp.bfloat16
 I32 = jnp.int32
 VMEM = pl.BlockSpec(memory_space=pltpu.VMEM)
+ANY = pl.BlockSpec(memory_space=pl.ANY)
+HBM = pl.BlockSpec(memory_space=pltpu.HBM)
 MIB = 1024 * 1024
 
 
-def call(kernel, outs, scratch=()):
+def call(kernel, outs, scratch=(), specs=None, after=()):
     many = isinstance(outs, (list, tuple))
+
+    def body(*refs):
+        kernel(*refs[len(after) :])
+
+    def run(*operands):
+        in_specs = [ANY] * len(after) + list(specs or [VMEM] * len(operands))
+        return pallas(body if after else kernel, outs, many, scratch, in_specs)(*after, *operands)
+
+    return run
+
+
+def pallas(kernel, outs, many, scratch, in_specs):
     return pl.pallas_call(
         kernel,
+        in_specs=in_specs,
         out_shape=outs,
         out_specs=[VMEM] * len(outs) if many else VMEM,
         scratch_shapes=list(scratch),
@@ -147,29 +162,23 @@
     lax.fori_loop(0, count, body, upper_face(ref, first - 1))
 
 
-def stage_one(
-    rho_ref, vel_ref, mag_ref, prs_ref, mag_a, mag_b, five_a, five_b, next_ref, half_ref, pad_ref
-):
+def stage_one(mag_ref, five_ref, mag_a, mag_b, five_a, five_b, next_ref, half_ref, pad_ref):
     me = lax.axis_index("mag")
     last = lax.axis_size("mag") - 1
     even = me % 2 == 0
-    cx = rho_ref.shape[0]
-
-    def own(k, x):
-        if k == 0:
-            return rho_ref[x]
-        if k == 7:
-            return prs_ref[x]
-        return vel_ref[k - 1, x] if k < 4 else mag_ref[k - 4, x]
-
-    def partner(k, x, mag, five):
+    cx = mag_ref.shape[1]
+
+    def cell(k, x, mag, five):
         if 4 <= k < 7:
             return mag[k - 4, x]
         return five[min(k, 4), x]
 
+    def own(k, x):
+        return cell(k, x, mag_ref, five_ref)
+
     for k in range(8):
         for x in range(cx):
-            from_a, from_b = partner(k, x, mag_a, five_a), partner(k, x, mag_b, five_b)
+            from_a, from_b = cell(k, x, mag_a, five_a), cell(k, x, mag_b, five_b)
             low = jnp.where(even, from_b, from_a)
             high = jnp.where(even, from_a, from_b)
             pad_ref[k, x] = jnp.where(me == 0, own(k, 0), low)
@@ -203,7 +212,8 @@
             next_ref[k, cx + 3] = next_ref[k, cx + 1]
 
 
-def stage_two(next_ref, half_ref, rho_ref, vel_ref, mag_ref, prs_ref):
+def stage_two(next_ref, half_ref, rho_ref, vel_ref, mag_ref, prs_ref, end_ref):
+    end_ref[...] = half_ref[0, 0, 0:8]
     cx = half_ref.shape[1]
 
     def put(x, step, q, change):
@@ -218,7 +228,7 @@
     sweep_planes(next_ref, 2, cx, put)
 
 
-def pick_current(mag_ref, mag_a, mag_b, cell_ref, cond_ref, out_ref):
+def pick_current(mag_ref, cell_ref, strip_ref, mag_a, mag_b, five_ref, out_ref, five_out):
     me = lax.axis_index("mag")
     last = lax.axis_size("mag") - 1
     even = me % 2 == 0
@@ -260,20 +270,37 @@
         found = found[:count] + found[count:]
         mine = jnp.where(index == hi[s : s + 1], found, 0.0)
         out_ref[s : s + 1, :] = jnp.sum(mine, axis=0, keepdims=True)
-    lat, columns = cond_ref.shape
+    out_ref[points:, :] = strip_ref[...]
+    five_out[...] = five_ref[...]
+
+
+def load_arguments(
+    rho_ref, vel_ref, mag_ref, prs_ref, cell_ref, cond_ref, mag_out, cell_out, strip_out, five_out, rows, sems
+):
+    copies = [
+        pltpu.make_async_copy(source, target, sems.at[k])
+        for k, (source, target) in enumerate(
+            [
+                (cond_ref, rows),
+                (mag_ref, mag_out),
+                (cell_ref, cell_out),
+                (rho_ref, five_out.at[0]),
+                (vel_ref, five_out.at[pl.ds(1, 3)]),
+                (prs_ref, five_out.at[4]),
+            ]
+        )
+    ]
+    for copy in copies:
+        copy.start()
+    copies[0].wait()
+    lat, columns = rows.shape
     strips = columns // LANES
     for r in range(lat):
         for strip in range(strips):
-            place = points + r * strips + strip
-            out_ref[place : place + 1, :] = cond_ref[
-                r : r + 1, strip * LANES : (strip + 1) * LANES
-            ]
-
-
-def pack_five(rho_ref, vel_ref, prs_ref, out_ref):
-    out_ref[0] = rho_ref[...]
-    out_ref[1:4] = vel_ref[...]
-    out_ref[4] = prs_ref[...]
+            place = r * strips + strip
+            strip_out[place : place + 1, :] = rows[r : r + 1, strip * LANES : (strip + 1) * LANES]
+    for copy in copies[1:]:
+        copy.wait()
 
 
 def east_of(v):
@@ -348,6 +375,17 @@
         repeat(count // rows, group)
 
     return kernel
+
+
+def handing_on(kernel, count):
+    def run(*refs):
+        outs = count + 1
+        given = refs[-outs - count : -outs]
+        for source, target in zip(given, refs[-count:]):
+            target[...] = source[...]
+        kernel(*refs[: -outs - count], refs[-outs])
+
+    return run
 
 
 def scatter_last(blocks, points, lat, strips):
@@ -479,43 +517,60 @@
     shape = jax.ShapeDtypeStruct
 
     mag_a, mag_b = swap(mag_field, 1), swap_next(mag_field)
-    five = call(pack_five, shape((5, cx, ny, nz), F32))(density, velocity, pressure)
+    tile = shape((points, LANES), I32)
+    mag, cell, strip, five = call(
+        load_arguments,
+        [shape(mag_field.shape, F32), tile, shape((cells, LANES), F32), shape((5, cx, ny, nz), F32)],
+        [pltpu.VMEM((lat, columns), F32), pltpu.SemaphoreType.DMA((6,))],
+        [HBM] * 6,
+    )(density, velocity, mag_field, pressure, shell_cell.reshape(-1, LANES), conductance)
 
     owner = foot_owner.reshape(-1, LANES)
     row = foot_row.reshape(-1, LANES)
     lon = foot_lon.reshape(-1, LANES)
 
-    load = call(pick_current, shape((points + cells, LANES), F32))(
-        mag_field, mag_a, mag_b, shell_cell.reshape(-1, LANES), conductance
-    )
+    load, five = call(
+        pick_current, [shape((points + cells, LANES), F32), shape(five.shape, F32)]
+    )(mag, cell, strip, mag_a, mag_b, five)
+    five_a, five_b = swap(five, 1), swap_next(five)
+
     grid = shape((count, 2 * LANES), F32)
-    total, new, blocks = (), load, 1
+    total, blocks, done = (), 1, 0
     bit = devices // 2
     while bit > 1:
         arrived = swap(load, bit)
-        size = max(1, blocks // 2)
-        kernel = scatter_new(blocks - size, size, points, lat, strips)
-        total = (call(kernel, grid)(*total, new, owner, row, lon),)
+        if blocks > 1:
+            kernel = handing_on(scatter_new(done, blocks - done, points, lat, strips), 1)
+            total, load = call(kernel, [grid, shape(load.shape, F32)])(
+                *total, new, owner, row, lon, load
+            )
+            total, done = (total,), blocks
         before, new = load, arrived
         load = jnp.concatenate([load, arrived], axis=0)
+        if blocks == 1:
+            new = load
         blocks, bit = blocks * 2, bit // 2
-    grids = shape((count + count // 2, LANES), F32)
-    mine = call(
-        scatter_last(blocks, points, lat, strips), grids, [pltpu.VMEM((count, 2 * LANES), F32)]
-    )(*total, before, new, owner, row, lon)
-    theirs = swap(mine, 1)
-
-    five_a, five_b = swap(five, 1), swap_next(five)
+
     slab = shape((8, cx, ny, nz), F32)
     following, half = call(
         stage_one,
         [shape((8, cx + 4, ny, nz), F32), slab],
         [pltpu.VMEM((8, 3 * cx, ny, nz), F32)],
-    )(density, velocity, mag_field, pressure, mag_a, mag_b, five_a, five_b)
+    )(mag, five, mag_a, mag_b, five_a, five_b)
+
+    grids = shape((count + count // 2, LANES), F32)
+    mine = call(
+        scatter_last(blocks, points, lat, strips),
+        grids,
+        [pltpu.VMEM((count, 2 * LANES), F32)],
+        after=(half,),
+    )(*total, before, new, owner, row, lon)
+    theirs = swap(mine, 1)
+
     cell_shape = shape((cx, ny, nz), F32)
     vector_shape = shape((3, cx, ny, nz), F32)
-    new_density, new_velocity, new_field, new_pressure = call(
-        stage_two, [cell_shape, vector_shape, vector_shape, cell_shape]
+    new_density, new_velocity, new_field, new_pressure, end = call(
+        stage_two, [cell_shape, vector_shape, vector_shape, cell_shape, shape((8, LANES), F32)]
     )(following, half)
 
     potential, shell_potential = call(
@@ -526,6 +581,7 @@
             pltpu.VMEM((5, devices * lat, strips, LANES), F32),
             pltpu.VMEM((2, devices * lat + 2, strips, LANES), F32),
         ],
+        after=(end,),
     )(mine, theirs, owner, row, lon)
     return (
         new_density,

time: 45.4 us -> 35.9 us (0.79)
  the two profiles are of different devices: /device:TPU:25 before, /device:TPU:0 now
where the time goes in v3:
time: 35.9 us; the launch traced here: 35.5 us
  Pallas kernels  13.5 us (38%)
  starting transfers between devices  10.8 us (30%)
  waiting for transfers between devices  5.58 us (16%)
  local copies, waits for them, and re-layouts  4.78 us (13%)
  between operations  0.78 us (2%)
    pallas_call x8, Pallas kernels, run(): pallas(body if after else kernel, outs, many, scratch, in_specs)  13.5 us
    ppermute x6, starting transfers between devices, swap(): return lax.ppermute(values, 'mag', [(i, i ^ bit) for i in range(devices)])  9.53 us
    ppermute x6, waiting for transfers between devices, swap(): return lax.ppermute(values, 'mag', [(i, i ^ bit) for i in range(devices)])  5.57 us
    unnamed x20, local copies, waits for them, and re-layouts  4.77 us
    ppermute x2, starting transfers between devices, swap_next(): return lax.ppermute(values, 'mag', pairs)  1.31 us
  transfers between devices with their start and end apart: 8, of which 4 were waited for; matrix products, arithmetic and copies ran while one was open for 0% of the time, Pallas kernels for 23%

profile of v3, /device:TPU:0, one launch (start us, length us, event | category | flops | bytes accessed | tf_op | source)
XLA Modules:
  0.0 35.5 jit_solution(144704262289923358)
XLA Ops:
  0.6 0.5 %collective-permute-start = (f32[3,4,16,128]{3,2,1,0:T(8,128)}, f32[3,4,16,128]{3,2,1,0:T(8,128)S(1)}, u32[]{:S(2)}, u32[]{:S(2)}) collective-permute-start(f32[3,4,16,128]{3,2,1,0:T(8,128)} %mag_ref.1), channel_id=1, source_target_pairs={{0,1},{1,0},{2,3},{3,2},{4,5},{5,4},{6,7},{7,6},{8,9},{9,8},{10,11... | collective-permute-start | bytes 294920 | tf_op jit(solution)/shard_map/ppermute | solution.py:496
  1.2 0.7 %collective-permute-start.1 = (f32[3,4,16,128]{3,2,1,0:T(8,128)}, f32[3,4,16,128]{3,2,1,0:T(8,128)S(1)}, u32[]{:S(2)}, u32[]{:S(2)}) collective-permute-start(f32[3,4,16,128]{3,2,1,0:T(8,128)} %mag_ref.1), channel_id=1, source_target_pairs={{1,2},{2,1},{3,4},{4,3},{5,6},{6,5},{7,8},{8,7},{9,10},{10,9},{11,... | collective-permute-start | bytes 294920 | tf_op jit(solution)/shard_map/ppermute | solution.py:503
  1.8 0.9 %copy-done.3 = f32[3,4,16,128]{3,2,1,0:T(8,128)S(1)} copy-done((f32[3,4,16,128]{3,2,1,0:T(8,128)S(1)}, f32[3,4,16,128]{3,2,1,0:T(8,128)}, u32[]{:S(2)}) %copy-start.3) | copy-done | bytes 98328
  2.7 0.9 %copy-done.4 = f32[3,4,16,128]{3,2,1,0:T(8,128)S(1)} copy-done((f32[3,4,16,128]{3,2,1,0:T(8,128)S(1)}, f32[3,4,16,128]{3,2,1,0:T(8,128)}, u32[]{:S(2)}) %copy-start.4) | copy-done | bytes 98328
  3.6 0.8 %copy-done.5 = f32[4,16,128]{2,1,0:T(8,128)S(1)} copy-done((f32[4,16,128]{2,1,0:T(8,128)S(1)}, f32[4,16,128]{2,1,0:T(8,128)}, u32[]{:S(2)}) %copy-start.5) | copy-done | bytes 32792
  4.4 0.8 %copy-done.6 = f32[4,16,128]{2,1,0:T(8,128)S(1)} copy-done((f32[4,16,128]{2,1,0:T(8,128)S(1)}, f32[4,16,128]{2,1,0:T(8,128)}, u32[]{:S(2)}) %copy-start.6) | copy-done | bytes 32792
  5.1 0.8 %copy-done.7 = f32[4,2048]{1,0:T(4,128)S(1)} copy-done((f32[4,2048]{1,0:T(4,128)S(1)}, f32[4,2048]{1,0:T(4,128)}, u32[]{:S(2)}) %copy-start.7) | copy-done | bytes 32792
  5.9 0.7 %copy-done.8 = s32[1024]{0:T(1024)S(1)} copy-done((s32[1024]{0:T(1024)S(1)}, s32[1024]{0:T(1024)}, u32[]{:S(2)}) %copy-start.8) | copy-done | bytes 4120
  6.6 0.4 %shard_map.136 = (f32[3,4,16,128]{3,2,1,0:T(8,128)S(1)}, s32[8,128]{1,0:T(8,128)S(1)}, f32[64,128]{1,0:T(8,128)S(1)}, f32[5,4,16,128]{3,2,1,0:T(8,128)S(1)}) custom-call(f32[4,16,128]{2,1,0:T(8,128)S(1)} %copy-done.5, f32[3,4,16,128]{3,2,1,0:T(8,128)S(1)} %copy-done.3, f32[3,4,16,128]{3,2,1,0:T(8,128)S(1)} %copy-done.4, f32[4,16,128]{2,1,0:T(8,128)S(1)} %copy-done.6, ...), custom_call_target="tpu_custom_call" | custom-call | tf_op jit(solution)/shard_map/pallas_call | solution.py:33
  7.0 0.0 collective-permute-done.mag_a
  7.0 0.0 collective-permute-done.1.mag_b
  7.0 0.0 copy-start.2
  7.0 0.3 shard_map.137
  7.4 0.0 copy-start
  7.4 0.0 copy-start.1
  7.4 6.4 %collective-permute-start.4 = (f32[72,128]{1,0:T(8,128)S(1)}, f32[72,128]{1,0:T(8,128)S(1)}, u32[]{:S(2)}, u32[]{:S(2)}) collective-permute-start(f32[72,128]{1,0:T(8,128)S(1)} %get-tuple-element.37), channel_id=1, source_target_pairs={{0,8},{1,9},{2,10},{3,11},{4,12},{5,13},{6,14},{7,15},{8,0},{9,1},... | collective-permute-start | bytes 110600 | tf_op jit(solution)/shard_map/ppermute | solution.py:496
  13.8 0.0 collective-permute-start.2
  13.8 0.7 %collective-permute-start.3 = (f32[5,4,16,128]{3,2,1,0:T(8,128)S(1)}, f32[5,4,16,128]{3,2,1,0:T(8,128)S(1)}, u32[]{:S(2)}, u32[]{:S(2)}) collective-permute-start(f32[5,4,16,128]{3,2,1,0:T(8,128)S(1)} %get-tuple-element.29.five_ref), channel_id=1, source_target_pairs={{1,2},{2,1},{3,4},{4,3},{5,6},{6,5},{7,8},{8,7},{9,10},{10,9},{11,... | collective-permute-start | bytes 491528 | tf_op jit(solution)/shard_map/ppermute | solution.py:503
  14.5 1.3 %collective-permute-done.4 = f32[72,128]{1,0:T(8,128)S(1)} collective-permute-done((f32[72,128]{1,0:T(8,128)S(1)}, f32[72,128]{1,0:T(8,128)S(1)}, u32[]{:S(2)}, u32[]{:S(2)}) %collective-permute-start.4) | collective-permute-done | bytes 36896 | tf_op jit(solution)/shard_map/ppermute | solution.py:496
  15.7 2.5 %collective-permute-start.5 = (f32[144,128]{1,0:T(8,128)S(1)}, f32[144,128]{1,0:T(8,128)S(1)}, u32[]{:S(2)}, u32[]{:S(2)}) collective-permute-start(f32[144,128]{1,0:T(8,128)S(1)} %constant_dynamic-update-slice_fusion.refs_0_.refs_4_), channel_id=1, source_target_pairs={{0,4},{1,5},{2,6},{3,7},{4,0},{5,1},{6,2},{7,3},{8,12},{9,13},{10,... | collective-permute-start | bytes 221192 | tf_op jit(solution)/shard_map/ppermute | solution.py:496
  18.2 1.3 %shard_map.140 = (f32[1024,256]{1,0:T(8,128)S(1)}, f32[144,128]{1,0:T(8,128)S(1)}) custom-call(f32[144,128]{1,0:T(8,128)S(1)} %constant_dynamic-update-slice_fusion.refs_0_.refs_4_, s32[128,128]{1,0:T(8,128)S(1)} %bitcast.5, s32[128,128]{1,0:T(8,128)S(1)} %bitcast.9, s32[128,128]{1,0:T(8,128)S(1)} %bitcast.13, ...), custom_call_target="tpu_custom_call" | custom-call | tf_op jit(solution)/shard_map/pallas_call | solution.py:33
  19.6 3.4 %collective-permute-done.5.refs_1_ = f32[144,128]{1,0:T(8,128)S(1)} collective-permute-done((f32[144,128]{1,0:T(8,128)S(1)}, f32[144,128]{1,0:T(8,128)S(1)}, u32[]{:S(2)}, u32[]{:S(2)}) %collective-permute-start.5) | collective-permute-done | bytes 73760 | tf_op jit(solution)/shard_map/ppermute | solution.py:496
  23.0 0.0 collective-permute-start.6
  23.0 1.3 %shard_map.141 = (f32[1024,256]{1,0:T(8,128)S(1)}, f32[288,128]{1,0:T(8,128)S(1)}) custom-call(f32[1024,256]{1,0:T(8,128)S(1)} %get-tuple-element.38.refs_0_, f32[144,128]{1,0:T(8,128)S(1)} %collective-permute-done.5.refs_1_, s32[128,128]{1,0:T(8,128)S(1)} %bitcast.6, s32[128,128]{1,0:T(8,128)S(1)} %bitcast.10, s32[128,128]{1,0:T(8,128)S(1)} %bitcast.14, ...), custom_call_target="tpu_custom_call" | custom-call | tf_op jit(solution)/shard_map/pallas_call | solution.py:33
  24.3 0.0 collective-permute-done.2.five_a
  24.4 3.0 %shard_map.138 = (f32[8,8,16,128]{3,2,1,0:T(8,128)S(1)}, f32[8,4,16,128]{3,2,1,0:T(8,128)S(1)}) custom-call(f32[3,4,16,128]{3,2,1,0:T(8,128)S(1)} %get-tuple-element.25.mag_ref, f32[5,4,16,128]{3,2,1,0:T(8,128)S(1)} %get-tuple-element.29.five_ref, f32[3,4,16,128]{3,2,1,0:T(8,128)S(1)} %collective-permute-done.mag_a, ...), custom_call_target="tpu_custom_call" | custom-call | tf_op jit(solution)/shard_map/pallas_call | solution.py:33
  27.4 0.7 %collective-permute-done.6.refs_3_ = f32[288,128]{1,0:T(8,128)S(1)} collective-permute-done((f32[288,128]{1,0:T(8,128)S(1)}, f32[288,128]{1,0:T(8,128)S(1)}, u32[]{:S(2)}, u32[]{:S(2)}) %collective-permute-start.6) | collective-permute-done | bytes 147488 | tf_op jit(solution)/shard_map/ppermute | solution.py:496
  28.1 2.4 %shard_map.142.refs_1_ = f32[1536,128]{1,0:T(8,128)S(1)} custom-call(f32[8,4,16,128]{3,2,1,0:T(8,128)S(1)} %get-tuple-element.31.half_ref.refs_0_, f32[1024,256]{1,0:T(8,128)S(1)} %get-tuple-element.40.refs_1_, f32[288,128]{1,0:T(8,128)S(1)} %get-tuple-element.41.refs_2_, f32[288,128]{1,0:T(8,128)S(1)} %collective-permute-done.6.refs_3_, ...), custom_call_target="tpu_custom_call" | custom-call | tf_op jit(solution)/shard_map/pallas_call | solution.py:33
  30.5 0.1 collective-permute-start.7
  30.6 2.1 %shard_map.139 = (f32[4,16,128]{2,1,0:T(8,128)}, f32[3,4,16,128]{3,2,1,0:T(8,128)}, f32[3,4,16,128]{3,2,1,0:T(8,128)}, f32[4,16,128]{2,1,0:T(8,128)}, f32[8,128]{1,0:T(8,128)S(1)}) custom-call(f32[8,8,16,128]{3,2,1,0:T(8,128)S(1)} %get-tuple-element.30.next_ref, f32[8,4,16,128]{3,2,1,0:T(8,128)S(1)} %get-tuple-element.31.half_ref.refs_0_), custom_call_target="tpu_custom_call" | custom-call | tf_op jit(solution)/shard_map/pallas_call | solution.py:33
  32.8 0.1 collective-permute-done.7.refs_2_
  32.9 2.6 %shard_map.143 = (f32[4,2048]{1,0:T(4,128)}, f32[8,128]{1,0:T(8,128)}) custom-call(f32[8,128]{1,0:T(8,128)S(1)} %get-tuple-element.36.refs_0_, f32[1536,128]{1,0:T(8,128)S(1)} %shard_map.142.refs_1_, f32[1536,128]{1,0:T(8,128)S(1)} %collective-permute-done.7.refs_2_, s32[128,128]{1,0:T(8,128)S(1)} %bitcast.8, s32[128,128]{1,0:T(8,128)S(1)} %bitcast.12, ...), custom_call_target="tpu_custom_call" | custom-call | tf_op jit(solution)/shard_map/pallas_call | solution.py:33
  (14 shorter events, 0.0 us)
Async XLA Ops:
  0.6 6.4 %collective-permute-start = (f32[3,4,16,128]{3,2,1,0:T(8,128)}, f32[3,4,16,128]{3,2,1,0:T(8,128)S(1)}, u32[]{:S(2)}, u32[]{:S(2)}) collective-permute-start(f32[3,4,16,128]{3,2,1,0:T(8,128)} %mag_ref.1), channel_id=1, source_target_pairs={{0,1},{1,0},{2,3},{3,2},{4,5},{5,4},{6,7},{7,6},{8,9},{9,8},{10,11... | collective-permute-start | bytes 294920 | tf_op jit(solution)/shard_map/ppermute | solution.py:496
  1.2 5.9 %collective-permute-start.1 = (f32[3,4,16,128]{3,2,1,0:T(8,128)}, f32[3,4,16,128]{3,2,1,0:T(8,128)S(1)}, u32[]{:S(2)}, u32[]{:S(2)}) collective-permute-start(f32[3,4,16,128]{3,2,1,0:T(8,128)} %mag_ref.1), channel_id=1, source_target_pairs={{1,2},{2,1},{3,4},{4,3},{5,6},{6,5},{7,8},{8,7},{9,10},{10,9},{11,... | collective-permute-start | bytes 294920 | tf_op jit(solution)/shard_map/ppermute | solution.py:503
  1.8 0.9 %copy-start.3 = (f32[3,4,16,128]{3,2,1,0:T(8,128)S(1)}, f32[3,4,16,128]{3,2,1,0:T(8,128)}, u32[]{:S(2)}) copy-start(f32[3,4,16,128]{3,2,1,0:T(8,128)} %vel_ref.1) | copy-start | bytes 294916
  2.7 0.9 %copy-start.4 = (f32[3,4,16,128]{3,2,1,0:T(8,128)S(1)}, f32[3,4,16,128]{3,2,1,0:T(8,128)}, u32[]{:S(2)}) copy-start(f32[3,4,16,128]{3,2,1,0:T(8,128)} %mag_ref.1) | copy-start | bytes 294916
  3.6 0.8 %copy-start.5 = (f32[4,16,128]{2,1,0:T(8,128)S(1)}, f32[4,16,128]{2,1,0:T(8,128)}, u32[]{:S(2)}) copy-start(f32[4,16,128]{2,1,0:T(8,128)} %rho_ref.1) | copy-start | bytes 98308
  4.4 0.8 %copy-start.6 = (f32[4,16,128]{2,1,0:T(8,128)S(1)}, f32[4,16,128]{2,1,0:T(8,128)}, u32[]{:S(2)}) copy-start(f32[4,16,128]{2,1,0:T(8,128)} %prs_ref.1) | copy-start | bytes 98308
  5.1 0.8 %copy-start.7 = (f32[4,2048]{1,0:T(4,128)S(1)}, f32[4,2048]{1,0:T(4,128)}, u32[]{:S(2)}) copy-start(f32[4,2048]{1,0:T(4,128)} %cond_ref.1) | copy-start | bytes 98308
  5.9 0.7 %copy-start.8 = (s32[1024]{0:T(1024)S(1)}, s32[1024]{0:T(1024)}, u32[]{:S(2)}) copy-start(s32[1024]{0:T(1024)} %param.14) | copy-start | bytes 12292
  7.0 11.2 %copy-start.2 = (s32[16384]{0:T(1024)S(1)}, s32[16384]{0:T(1024)}, u32[]{:S(2)}) copy-start(s32[16384]{0:T(1024)} %param.17) | copy-start | bytes 196612
  7.4 10.9 %copy-start = (s32[16384,1]{0,1:T(1,128)S(1)}, s32[16384,1]{0,1:T(1,128)}, u32[]{:S(2)}) copy-start(s32[16384,1]{0,1:T(1,128)} %param.15) | copy-start | bytes 196612
  7.4 10.9 %copy-start.1 = (s32[16384]{0:T(1024)S(1)}, s32[16384]{0:T(1024)}, u32[]{:S(2)}) copy-start(s32[16384]{0:T(1024)} %param.16) | copy-start | bytes 196612
  7.4 8.3 %collective-permute-start.4 = (f32[72,128]{1,0:T(8,128)S(1)}, f32[72,128]{1,0:T(8,128)S(1)}, u32[]{:S(2)}, u32[]{:S(2)}) collective-permute-start(f32[72,128]{1,0:T(8,128)S(1)} %get-tuple-element.37), channel_id=1, source_target_pairs={{0,8},{1,9},{2,10},{3,11},{4,12},{5,13},{6,14},{7,15},{8,0},{9,1},... | collective-permute-start | bytes 110600 | tf_op jit(solution)/shard_map/ppermute | solution.py:496
  13.8 10.5 %collective-permute-start.2 = (f32[5,4,16,128]{3,2,1,0:T(8,128)S(1)}, f32[5,4,16,128]{3,2,1,0:T(8,128)S(1)}, u32[]{:S(2)}, u32[]{:S(2)}) collective-permute-start(f32[5,4,16,128]{3,2,1,0:T(8,128)S(1)} %get-tuple-element.29.five_ref), channel_id=1, source_target_pairs={{0,1},{1,0},{2,3},{3,2},{4,5},{5,4},{6,7},{7,6},{8,9},{9,8},{10,11... | collective-permute-start | bytes 491528 | tf_op jit(solution)/shard_map/ppermute | solution.py:496
  13.8 10.6 %collective-permute-start.3 = (f32[5,4,16,128]{3,2,1,0:T(8,128)S(1)}, f32[5,4,16,128]{3,2,1,0:T(8,128)S(1)}, u32[]{:S(2)}, u32[]{:S(2)}) collective-permute-start(f32[5,4,16,128]{3,2,1,0:T(8,128)S(1)} %get-tuple-element.29.five_ref), channel_id=1, source_target_pairs={{1,2},{2,1},{3,4},{4,3},{5,6},{6,5},{7,8},{8,7},{9,10},{10,9},{11,... | collective-permute-start | bytes 491528 | tf_op jit(solution)/shard_map/ppermute | solution.py:503
  15.7 7.3 %collective-permute-start.5 = (f32[144,128]{1,0:T(8,128)S(1)}, f32[144,128]{1,0:T(8,128)S(1)}, u32[]{:S(2)}, u32[]{:S(2)}) collective-permute-start(f32[144,128]{1,0:T(8,128)S(1)} %constant_dynamic-update-slice_fusion.refs_0_.refs_4_), channel_id=1, source_target_pairs={{0,4},{1,5},{2,6},{3,7},{4,0},{5,1},{6,2},{7,3},{8,12},{9,13},{10,... | collective-permute-start | bytes 221192 | tf_op jit(solution)/shard_map/ppermute | solution.py:496
  23.0 5.1 %collective-permute-start.6 = (f32[288,128]{1,0:T(8,128)S(1)}, f32[288,128]{1,0:T(8,128)S(1)}, u32[]{:S(2)}, u32[]{:S(2)}) collective-permute-start(f32[288,128]{1,0:T(8,128)S(1)} %constant_dynamic-update-slice_fusion.2.refs_5_), channel_id=1, source_target_pairs={{0,2},{1,3},{2,0},{3,1},{4,6},{5,7},{6,4},{7,5},{8,10},{9,11},{10,... | collective-permute-start | bytes 442376 | tf_op jit(solution)/shard_map/ppermute | solution.py:496
  30.5 2.4 %collective-permute-start.7 = (f32[1536,128]{1,0:T(8,128)S(1)}, f32[1536,128]{1,0:T(8,128)S(1)}, u32[]{:S(2)}, u32[]{:S(2)}) collective-permute-start(f32[1536,128]{1,0:T(8,128)S(1)} %shard_map.142.refs_1_), channel_id=1, source_target_pairs={{0,1},{1,0},{2,3},{3,2},{4,5},{5,4},{6,7},{7,6},{8,9},{9,8},{10,11... | collective-permute-start | bytes 2359304 | tf_op jit(solution)/shard_map/ppermute | solution.py:496

commit v4 on v3

--- a/solution.py
+++ b/solution.py
@@ -148,42 +148,52 @@
     return face(left, right, 0)
 
 
-def sweep_planes(ref, first, count, put):
+def sideways(q):
+    return add(periodic(q, 0, 1), periodic(q, 1, 2))
+
+
+def sweep_planes(ref, first, count, put, others):
     def body(step, below):
         x = first + step
         above = upper_face(ref, x)
         q = plane(ref, x)
         change = [f - g for f, g in zip(below, above)]
-        change = add(change, periodic(q, 0, 1))
-        change = add(change, periodic(q, 1, 2))
-        put(x, step, q, change)
+        put(x, step, q, add(change, others(step, q)))
         return above
 
     lax.fori_loop(0, count, body, upper_face(ref, first - 1))
 
 
-def stage_one(mag_ref, five_ref, mag_a, mag_b, five_a, five_b, next_ref, half_ref, pad_ref):
+def stage_own(own_ref, side_ref):
+    def body(x, carry):
+        for k, value in enumerate(sideways(plane(own_ref, x))):
+            side_ref[k, x] = value
+        return carry
+
+    lax.fori_loop(0, own_ref.shape[1], body, 0)
+
+
+def stage_one(own_ref, eight_a, eight_b, own_side_ref, next_ref, half_ref, pad_ref, side_ref):
     me = lax.axis_index("mag")
     last = lax.axis_size("mag") - 1
     even = me % 2 == 0
-    cx = mag_ref.shape[1]
-
-    def cell(k, x, mag, five):
-        if 4 <= k < 7:
-            return mag[k - 4, x]
-        return five[min(k, 4), x]
-
-    def own(k, x):
-        return cell(k, x, mag_ref, five_ref)
-
+    cx = own_ref.shape[1]
     for k in range(8):
         for x in range(cx):
-            from_a, from_b = cell(k, x, mag_a, five_a), cell(k, x, mag_b, five_b)
-            low = jnp.where(even, from_b, from_a)
-            high = jnp.where(even, from_a, from_b)
-            pad_ref[k, x] = jnp.where(me == 0, own(k, 0), low)
-            pad_ref[k, cx + x] = own(k, x)
-            pad_ref[k, 2 * cx + x] = jnp.where(me == last, own(k, cx - 1), high)
+            low = jnp.where(even, eight_b[k, x], eight_a[k, x])
+            high = jnp.where(even, eight_a[k, x], eight_b[k, x])
+            pad_ref[k, x] = jnp.where(me == 0, own_ref[k, 0], low)
+            pad_ref[k, cx + x] = own_ref[k, x]
+            pad_ref[k, 2 * cx + x] = jnp.where(me == last, own_ref[k, cx - 1], high)
+            side_ref[k, 2 + x] = own_side_ref[k, x]
+
+    def beside(i, carry):
+        step = jnp.where(i < 2, i, cx + i)
+        for k, value in enumerate(sideways(plane(pad_ref, cx - 2 + step))):
+            side_ref[k, step] = value
+        return carry
+
+    lax.fori_loop(0, 4, beside, 0)
 
     def put(x, step, q, change):
         start = conserved(q)
@@ -197,7 +207,7 @@
             for k in range(8):
                 half_ref[k, step - 2] = 0.5 * (start[k] + first[k])
 
-    sweep_planes(pad_ref, cx - 2, cx + 4, put)
+    sweep_planes(pad_ref, cx - 2, cx + 4, put, lambda step, q: plane(side_ref, step))
 
     @pl.when(me == 0)
     def _():
@@ -225,26 +235,27 @@
             mag_ref[k, step] = q2[4 + k]
         prs_ref[step] = q2[7]
 
-    sweep_planes(next_ref, 2, cx, put)
-
-
-def pick_current(mag_ref, cell_ref, strip_ref, mag_a, mag_b, five_ref, out_ref, five_out):
+    sweep_planes(next_ref, 2, cx, put, lambda step, q: sideways(q))
+
+
+def pick_current(own_ref, cell_ref, strip_ref, edge_a, edge_b, out_ref, own_out):
     me = lax.axis_index("mag")
     last = lax.axis_size("mag") - 1
     even = me % 2 == 0
-    cx, ny, nz = mag_ref.shape[1:]
+    cx, ny, nz = own_ref.shape[1:]
+    own_out[...] = own_ref[...]
     rows = []
     for x in range(cx):
-        bx, by, bz = (mag_ref[k, x] for k in range(3))
+        bx, by, bz = (own_ref[4 + k, x] for k in range(3))
 
         def neighbour(k, step):
             if 0 <= x + step < cx:
-                return mag_ref[k, x + step]
+                return own_ref[4 + k, x + step]
             if step < 0:
-                below = jnp.where(even, mag_b[k, cx - 1], mag_a[k, cx - 1])
-                return jnp.where(me == 0, mag_ref[k, x], below)
-            above = jnp.where(even, mag_a[k, 0], mag_b[k, 0])
-            return jnp.where(me == last, mag_ref[k, x], above)
+                below = jnp.where(even, edge_b[k - 1, 1], edge_a[k - 1, 1])
+                return jnp.where(me == 0, own_ref[4 + k, x], below)
+            above = jnp.where(even, edge_a[k - 1, 0], edge_b[k - 1, 0])
+            return jnp.where(me == last, own_ref[4 + k, x], above)
 
         def along_x(k):
             return 0.5 * (neighbour(k, 1) - neighbour(k, -1))
@@ -271,24 +282,25 @@
         mine = jnp.where(index == hi[s : s + 1], found, 0.0)
         out_ref[s : s + 1, :] = jnp.sum(mine, axis=0, keepdims=True)
     out_ref[points:, :] = strip_ref[...]
-    five_out[...] = five_ref[...]
 
 
 def load_arguments(
-    rho_ref, vel_ref, mag_ref, prs_ref, cell_ref, cond_ref, mag_out, cell_out, strip_out, five_out, rows, sems
+    rho_ref, vel_ref, mag_ref, prs_ref, cell_ref, cond_ref, own_out, edge_out, cell_out, strip_out, rows, sems
 ):
+    last = mag_ref.shape[1] - 1
+    pairs = [
+        (cond_ref, rows),
+        (mag_ref.at[pl.ds(1, 2), pl.ds(0, 1)], edge_out.at[:, pl.ds(0, 1)]),
+        (mag_ref.at[pl.ds(1, 2), pl.ds(last, 1)], edge_out.at[:, pl.ds(1, 1)]),
+        (cell_ref, cell_out),
+        (rho_ref, own_out.at[0]),
+        (vel_ref, own_out.at[pl.ds(1, 3)]),
+        (mag_ref, own_out.at[pl.ds(4, 3)]),
+        (prs_ref, own_out.at[7]),
+    ]
     copies = [
         pltpu.make_async_copy(source, target, sems.at[k])
-        for k, (source, target) in enumerate(
-            [
-                (cond_ref, rows),
-                (mag_ref, mag_out),
-                (cell_ref, cell_out),
-                (rho_ref, five_out.at[0]),
-                (vel_ref, five_out.at[pl.ds(1, 3)]),
-                (prs_ref, five_out.at[4]),
-            ]
-        )
+        for k, (source, target) in enumerate(pairs)
     ]
     for copy in copies:
         copy.start()
@@ -516,23 +528,37 @@
     count = devices * cells
     shape = jax.ShapeDtypeStruct
 
-    mag_a, mag_b = swap(mag_field, 1), swap_next(mag_field)
     tile = shape((points, LANES), I32)
-    mag, cell, strip, five = call(
+    slab = shape((8, cx, ny, nz), F32)
+    own, edge, cell, strip = call(
         load_arguments,
-        [shape(mag_field.shape, F32), tile, shape((cells, LANES), F32), shape((5, cx, ny, nz), F32)],
-        [pltpu.VMEM((lat, columns), F32), pltpu.SemaphoreType.DMA((6,))],
+        [slab, shape((2, 2, ny, nz), F32), tile, shape((cells, LANES), F32)],
+        [pltpu.VMEM((lat, columns), F32), pltpu.SemaphoreType.DMA((8,))],
         [HBM] * 6,
-    )(density, velocity, mag_field, pressure, shell_cell.reshape(-1, LANES), conductance)
+    )(
+        *(
+            pltpu.with_memory_space_constraint(x, pltpu.HBM)
+            for x in (
+                density,
+                velocity,
+                mag_field,
+                pressure,
+                shell_cell.reshape(-1, LANES),
+                conductance,
+            )
+        )
+    )
+    edge_a, edge_b = swap(edge, 1), swap_next(edge)
+    own_side = call(stage_own, slab)(own)
 
     owner = foot_owner.reshape(-1, LANES)
     row = foot_row.reshape(-1, LANES)
     lon = foot_lon.reshape(-1, LANES)
 
-    load, five = call(
-        pick_current, [shape((points + cells, LANES), F32), shape(five.shape, F32)]
-    )(mag, cell, strip, mag_a, mag_b, five)
-    five_a, five_b = swap(five, 1), swap_next(five)
+    load, own = call(
+        pick_current, [shape((points + cells, LANES), F32), slab], after=(own_side,)
+    )(own, cell, strip, edge_a, edge_b)
+    eight_a, eight_b = swap(own, 1), swap_next(own)
 
     grid = shape((count, 2 * LANES), F32)
     total, blocks, done = (), 1, 0
@@ -551,12 +577,11 @@
             new = load
         blocks, bit = blocks * 2, bit // 2
 
-    slab = shape((8, cx, ny, nz), F32)
     following, half = call(
         stage_one,
         [shape((8, cx + 4, ny, nz), F32), slab],
-        [pltpu.VMEM((8, 3 * cx, ny, nz), F32)],
-    )(mag, five, mag_a, mag_b, five_a, five_b)
+        [pltpu.VMEM((8, 3 * cx, ny, nz), F32), pltpu.VMEM((8, cx + 4, ny, nz), F32)],
+    )(own, eight_a, eight_b, own_side)
 
     grids = shape((count + count // 2, LANES), F32)
     mine = call(

time: 35.9 us -> 34.9 us (0.972)
  local copies, waits for them, and re-layouts: 4.78 us -> 0.04 us
  starting transfers between devices: 10.8 us -> 13.5 us
  Pallas kernels: 13.5 us -> 14.4 us
  waiting for transfers between devices: 5.58 us -> 6.04 us
    unnamed x20 -> x8, local copies, waits for them, and re-layouts: 4.77 us -> 0.03 us
    ppermute x6, starting transfers between devices: 9.53 us -> 12.2 us  [swap(): return lax.ppermute(values, 'mag', [(i, i ^ bit) for i in range(devices)])]
    pallas_call x8 -> x9, Pallas kernels: 13.5 us -> 14.4 us  [run(): pallas(body if after else kernel, outs, many, scratch, in_specs)]
    ppermute x6, waiting for transfers between devices: 5.57 us -> 6.04 us  [swap(): return lax.ppermute(values, 'mag', [(i, i ^ bit) for i in range(devices)])]
  transfers between devices with their start and end apart: 8 -> 8, of which waited for: 4 -> 3; matrix products, arithmetic and copies ran while one was open for 0% -> 0% of each run, Pallas kernels for 23% -> 23%
where the time goes in v4:
time: 34.9 us; the launch traced here: 34.7 us
  Pallas kernels  14.4 us (41%)
  starting transfers between devices  13.5 us (39%)
  waiting for transfers between devices  6.04 us (17%)
  between operations  0.78 us (2%)
    pallas_call x9, Pallas kernels, run(): pallas(body if after else kernel, outs, many, scratch, in_specs)  14.4 us
    ppermute x6, starting transfers between devices, swap(): return lax.ppermute(values, 'mag', [(i, i ^ bit) for i in range(devices)])  12.2 us
    ppermute x6, waiting for transfers between devices, swap(): return lax.ppermute(values, 'mag', [(i, i ^ bit) for i in range(devices)])  6.04 us
    ppermute x2, starting transfers between devices, swap_next(): return lax.ppermute(values, 'mag', pairs)  1.33 us
  transfers between devices with their start and end apart: 8, of which 3 were waited for; matrix products, arithmetic and copies ran while one was open for 0% of the time, Pallas kernels for 23%

profile of v4, /device:TPU:0, one launch (start us, length us, event | category | flops | bytes accessed | tf_op | source)
XLA Modules:
  0.0 34.7 jit_solution(10701712918934781191)
XLA Ops:
  0.6 1.1 %shard_map.136 = (f32[8,4,16,128]{3,2,1,0:T(8,128)S(1)}, f32[2,2,16,128]{3,2,1,0:T(8,128)S(1)}, s32[8,128]{1,0:T(8,128)S(1)}, f32[64,128]{1,0:T(8,128)S(1)}) custom-call(f32[4,16,128]{2,1,0:T(8,128)} %rho_ref.1, f32[3,4,16,128]{3,2,1,0:T(8,128)} %vel_ref.1, f32[3,4,16,128]{3,2,1,0:T(8,128)} %mag_ref.1, f32[4,16,128]{2,1,0:T(8,128)} %prs_ref.1, ...), custom_call_target="tpu_custom_call" | custom-call | tf_op jit(solution)/shard_map/pallas_call | solution.py:33
  1.7 0.7 %collective-permute-start.1 = (f32[2,2,16,128]{3,2,1,0:T(8,128)S(1)}, f32[2,2,16,128]{3,2,1,0:T(8,128)S(1)}, u32[]{:S(2)}, u32[]{:S(2)}) collective-permute-start(f32[2,2,16,128]{3,2,1,0:T(8,128)S(1)} %get-tuple-element.28), channel_id=1, source_target_pairs={{1,2},{2,1},{3,4},{4,3},{5,6},{6,5},{7,8},{8,7},{9,10},{10,9},{11,... | collective-permute-start | bytes 98312 | tf_op jit(solution)/shard_map/ppermute | solution.py:515
  2.4 4.4 %collective-permute-start = (f32[2,2,16,128]{3,2,1,0:T(8,128)S(1)}, f32[2,2,16,128]{3,2,1,0:T(8,128)S(1)}, u32[]{:S(2)}, u32[]{:S(2)}) collective-permute-start(f32[2,2,16,128]{3,2,1,0:T(8,128)S(1)} %get-tuple-element.28), channel_id=1, source_target_pairs={{0,1},{1,0},{2,3},{3,2},{4,5},{5,4},{6,7},{7,6},{8,9},{9,8},{10,11... | collective-permute-start | bytes 98312 | tf_op jit(solution)/shard_map/ppermute | solution.py:508
  6.8 1.1 %shard_map.137.refs_0_.own_side_ref = f32[8,4,16,128]{3,2,1,0:T(8,128)S(1)} custom-call(f32[8,4,16,128]{3,2,1,0:T(8,128)S(1)} %get-tuple-element.25.own_ref.refs_1_), custom_call_target="tpu_custom_call" | custom-call | tf_op jit(solution)/shard_map/pallas_call | solution.py:33
  7.9 0.0 collective-permute-done.1.refs_5_
  7.9 0.0 collective-permute-done.refs_4_
  7.9 0.0 copy-start.2
  7.9 0.3 shard_map.138
  8.2 0.0 copy-start
  8.3 0.0 copy-start.1
  8.3 4.1 %collective-permute-start.4 = (f32[72,128]{1,0:T(8,128)S(1)}, f32[72,128]{1,0:T(8,128)S(1)}, u32[]{:S(2)}, u32[]{:S(2)}) collective-permute-start(f32[72,128]{1,0:T(8,128)S(1)} %get-tuple-element.37), channel_id=1, source_target_pairs={{0,8},{1,9},{2,10},{3,11},{4,12},{5,13},{6,14},{7,15},{8,0},{9,1},... | collective-permute-start | bytes 110600 | tf_op jit(solution)/shard_map/ppermute | solution.py:508
  12.3 0.7 %collective-permute-start.3 = (f32[8,4,16,128]{3,2,1,0:T(8,128)S(1)}, f32[8,4,16,128]{3,2,1,0:T(8,128)S(1)}, u32[]{:S(2)}, u32[]{:S(2)}) collective-permute-start(f32[8,4,16,128]{3,2,1,0:T(8,128)S(1)} %get-tuple-element.29.own_ref), channel_id=1, source_target_pairs={{1,2},{2,1},{3,4},{4,3},{5,6},{6,5},{7,8},{8,7},{9,10},{10,9},{11,... | collective-permute-start | bytes 786440 | tf_op jit(solution)/shard_map/ppermute | solution.py:515
  13.0 2.0 %collective-permute-start.2 = (f32[8,4,16,128]{3,2,1,0:T(8,128)S(1)}, f32[8,4,16,128]{3,2,1,0:T(8,128)S(1)}, u32[]{:S(2)}, u32[]{:S(2)}) collective-permute-start(f32[8,4,16,128]{3,2,1,0:T(8,128)S(1)} %get-tuple-element.29.own_ref), channel_id=1, source_target_pairs={{0,1},{1,0},{2,3},{3,2},{4,5},{5,4},{6,7},{7,6},{8,9},{9,8},{10,11... | collective-permute-start | bytes 786440 | tf_op jit(solution)/shard_map/ppermute | solution.py:508
  15.0 0.0 collective-permute-done.4
  15.0 1.6 %collective-permute-start.5 = (f32[144,128]{1,0:T(8,128)S(1)}, f32[144,128]{1,0:T(8,128)S(1)}, u32[]{:S(2)}, u32[]{:S(2)}) collective-permute-start(f32[144,128]{1,0:T(8,128)S(1)} %constant_dynamic-update-slice_fusion.refs_0_.refs_4_), channel_id=1, source_target_pairs={{0,4},{1,5},{2,6},{3,7},{4,0},{5,1},{6,2},{7,3},{8,12},{9,13},{10,... | collective-permute-start | bytes 221192 | tf_op jit(solution)/shard_map/ppermute | solution.py:508
  16.6 0.0 copy-done.2
  16.6 0.0 copy-done
  16.6 0.0 copy-done.1
  16.7 1.3 %shard_map.141 = (f32[1024,256]{1,0:T(8,128)S(1)}, f32[144,128]{1,0:T(8,128)S(1)}) custom-call(f32[144,128]{1,0:T(8,128)S(1)} %constant_dynamic-update-slice_fusion.refs_0_.refs_4_, s32[128,128]{1,0:T(8,128)S(1)} %bitcast.5, s32[128,128]{1,0:T(8,128)S(1)} %bitcast.9, s32[128,128]{1,0:T(8,128)S(1)} %bitcast.13, ...), custom_call_target="tpu_custom_call" | custom-call | tf_op jit(solution)/shard_map/pallas_call | solution.py:33
  18.0 4.3 %collective-permute-done.5.refs_1_ = f32[144,128]{1,0:T(8,128)S(1)} collective-permute-done((f32[144,128]{1,0:T(8,128)S(1)}, f32[144,128]{1,0:T(8,128)S(1)}, u32[]{:S(2)}, u32[]{:S(2)}) %collective-permute-start.5) | collective-permute-done | bytes 73760 | tf_op jit(solution)/shard_map/ppermute | solution.py:508
  22.3 0.0 collective-permute-start.6
  22.3 1.3 %shard_map.142 = (f32[1024,256]{1,0:T(8,128)S(1)}, f32[288,128]{1,0:T(8,128)S(1)}) custom-call(f32[1024,256]{1,0:T(8,128)S(1)} %get-tuple-element.38.refs_0_, f32[144,128]{1,0:T(8,128)S(1)} %collective-permute-done.5.refs_1_, s32[128,128]{1,0:T(8,128)S(1)} %bitcast.6, s32[128,128]{1,0:T(8,128)S(1)} %bitcast.10, s32[128,128]{1,0:T(8,128)S(1)} %bitcast.14, ...), custom_call_target="tpu_custom_call" | custom-call | tf_op jit(solution)/shard_map/pallas_call | solution.py:33
  23.6 0.0 collective-permute-done.3.eight_b
  23.6 0.0 collective-permute-done.2.eight_a
  23.6 2.2 %shard_map.139 = (f32[8,8,16,128]{3,2,1,0:T(8,128)S(1)}, f32[8,4,16,128]{3,2,1,0:T(8,128)S(1)}) custom-call(f32[8,4,16,128]{3,2,1,0:T(8,128)S(1)} %get-tuple-element.29.own_ref, f32[8,4,16,128]{3,2,1,0:T(8,128)S(1)} %collective-permute-done.2.eight_a, f32[8,4,16,128]{3,2,1,0:T(8,128)S(1)} %collective-permute-done.3.eight_b, ...), custom_call_target="tpu_custom_call" | custom-call | tf_op jit(solution)/shard_map/pallas_call | solution.py:33
  25.8 1.6 %collective-permute-done.6.refs_3_ = f32[288,128]{1,0:T(8,128)S(1)} collective-permute-done((f32[288,128]{1,0:T(8,128)S(1)}, f32[288,128]{1,0:T(8,128)S(1)}, u32[]{:S(2)}, u32[]{:S(2)}) %collective-permute-start.6) | collective-permute-done | bytes 147488 | tf_op jit(solution)/shard_map/ppermute | solution.py:508
  27.4 2.4 %shard_map.143.refs_1_ = f32[1536,128]{1,0:T(8,128)S(1)} custom-call(f32[8,4,16,128]{3,2,1,0:T(8,128)S(1)} %get-tuple-element.31.half_ref.refs_0_, f32[1024,256]{1,0:T(8,128)S(1)} %get-tuple-element.40.refs_1_, f32[288,128]{1,0:T(8,128)S(1)} %get-tuple-element.41.refs_2_, f32[288,128]{1,0:T(8,128)S(1)} %collective-permute-done.6.refs_3_, ...), custom_call_target="tpu_custom_call" | custom-call | tf_op jit(solution)/shard_map/pallas_call | solution.py:33
  29.8 0.1 collective-permute-start.7
  29.9 2.1 %shard_map.140 = (f32[4,16,128]{2,1,0:T(8,128)}, f32[3,4,16,128]{3,2,1,0:T(8,128)}, f32[3,4,16,128]{3,2,1,0:T(8,128)}, f32[4,16,128]{2,1,0:T(8,128)}, f32[8,128]{1,0:T(8,128)S(1)}) custom-call(f32[8,8,16,128]{3,2,1,0:T(8,128)S(1)} %get-tuple-element.30.next_ref, f32[8,4,16,128]{3,2,1,0:T(8,128)S(1)} %get-tuple-element.31.half_ref.refs_0_), custom_call_target="tpu_custom_call" | custom-call | tf_op jit(solution)/shard_map/pallas_call | solution.py:33
  32.0 0.1 collective-permute-done.7.refs_2_
  32.1 2.6 %shard_map.144 = (f32[4,2048]{1,0:T(4,128)}, f32[8,128]{1,0:T(8,128)}) custom-call(f32[8,128]{1,0:T(8,128)S(1)} %get-tuple-element.36.refs_0_, f32[1536,128]{1,0:T(8,128)S(1)} %shard_map.143.refs_1_, f32[1536,128]{1,0:T(8,128)S(1)} %collective-permute-done.7.refs_2_, s32[128,128]{1,0:T(8,128)S(1)} %bitcast.8, s32[128,128]{1,0:T(8,128)S(1)} %bitcast.12, ...), custom_call_target="tpu_custom_call" | custom-call | tf_op jit(solution)/shard_map/pallas_call | solution.py:33
  (4 shorter events, 0.0 us)
Async XLA Ops:
  1.7 6.2 %collective-permute-start.1 = (f32[2,2,16,128]{3,2,1,0:T(8,128)S(1)}, f32[2,2,16,128]{3,2,1,0:T(8,128)S(1)}, u32[]{:S(2)}, u32[]{:S(2)}) collective-permute-start(f32[2,2,16,128]{3,2,1,0:T(8,128)S(1)} %get-tuple-element.28), channel_id=1, source_target_pairs={{1,2},{2,1},{3,4},{4,3},{5,6},{6,5},{7,8},{8,7},{9,10},{10,9},{11,... | collective-permute-start | bytes 98312 | tf_op jit(solution)/shard_map/ppermute | solution.py:515
  2.4 5.5 %collective-permute-start = (f32[2,2,16,128]{3,2,1,0:T(8,128)S(1)}, f32[2,2,16,128]{3,2,1,0:T(8,128)S(1)}, u32[]{:S(2)}, u32[]{:S(2)}) collective-permute-start(f32[2,2,16,128]{3,2,1,0:T(8,128)S(1)} %get-tuple-element.28), channel_id=1, source_target_pairs={{0,1},{1,0},{2,3},{3,2},{4,5},{5,4},{6,7},{7,6},{8,9},{9,8},{10,11... | collective-permute-start | bytes 98312 | tf_op jit(solution)/shard_map/ppermute | solution.py:508
  7.9 8.7 %copy-start.2 = (s32[16384]{0:T(1024)S(1)}, s32[16384]{0:T(1024)}, u32[]{:S(2)}) copy-start(s32[16384]{0:T(1024)} %param.17) | copy-start | bytes 196612
  8.2 8.4 %copy-start = (s32[16384,1]{0,1:T(1,128)S(1)}, s32[16384,1]{0,1:T(1,128)}, u32[]{:S(2)}) copy-start(s32[16384,1]{0,1:T(1,128)} %param.15) | copy-start | bytes 196612
  8.3 8.4 %copy-start.1 = (s32[16384]{0:T(1024)S(1)}, s32[16384]{0:T(1024)}, u32[]{:S(2)}) copy-start(s32[16384]{0:T(1024)} %param.16) | copy-start | bytes 196612
  8.3 6.8 %collective-permute-start.4 = (f32[72,128]{1,0:T(8,128)S(1)}, f32[72,128]{1,0:T(8,128)S(1)}, u32[]{:S(2)}, u32[]{:S(2)}) collective-permute-start(f32[72,128]{1,0:T(8,128)S(1)} %get-tuple-element.37), channel_id=1, source_target_pairs={{0,8},{1,9},{2,10},{3,11},{4,12},{5,13},{6,14},{7,15},{8,0},{9,1},... | collective-permute-start | bytes 110600 | tf_op jit(solution)/shard_map/ppermute | solution.py:508
  12.3 11.2 %collective-permute-start.3 = (f32[8,4,16,128]{3,2,1,0:T(8,128)S(1)}, f32[8,4,16,128]{3,2,1,0:T(8,128)S(1)}, u32[]{:S(2)}, u32[]{:S(2)}) collective-permute-start(f32[8,4,16,128]{3,2,1,0:T(8,128)S(1)} %get-tuple-element.29.own_ref), channel_id=1, source_target_pairs={{1,2},{2,1},{3,4},{4,3},{5,6},{6,5},{7,8},{8,7},{9,10},{10,9},{11,... | collective-permute-start | bytes 786440 | tf_op jit(solution)/shard_map/ppermute | solution.py:515
  13.0 10.6 %collective-permute-start.2 = (f32[8,4,16,128]{3,2,1,0:T(8,128)S(1)}, f32[8,4,16,128]{3,2,1,0:T(8,128)S(1)}, u32[]{:S(2)}, u32[]{:S(2)}) collective-permute-start(f32[8,4,16,128]{3,2,1,0:T(8,128)S(1)} %get-tuple-element.29.own_ref), channel_id=1, source_target_pairs={{0,1},{1,0},{2,3},{3,2},{4,5},{5,4},{6,7},{7,6},{8,9},{9,8},{10,11... | collective-permute-start | bytes 786440 | tf_op jit(solution)/shard_map/ppermute | solution.py:508
  15.0 7.2 %collective-permute-start.5 = (f32[144,128]{1,0:T(8,128)S(1)}, f32[144,128]{1,0:T(8,128)S(1)}, u32[]{:S(2)}, u32[]{:S(2)}) collective-permute-start(f32[144,128]{1,0:T(8,128)S(1)} %constant_dynamic-update-slice_fusion.refs_0_.refs_4_), channel_id=1, source_target_pairs={{0,4},{1,5},{2,6},{3,7},{4,0},{5,1},{6,2},{7,3},{8,12},{9,13},{10,... | collective-permute-start | bytes 221192 | tf_op jit(solution)/shard_map/ppermute | solution.py:508
  22.3 5.1 %collective-permute-start.6 = (f32[288,128]{1,0:T(8,128)S(1)}, f32[288,128]{1,0:T(8,128)S(1)}, u32[]{:S(2)}, u32[]{:S(2)}) collective-permute-start(f32[288,128]{1,0:T(8,128)S(1)} %constant_dynamic-update-slice_fusion.2.refs_5_), channel_id=1, source_target_pairs={{0,2},{1,3},{2,0},{3,1},{4,6},{5,7},{6,4},{7,5},{8,10},{9,11},{10,... | collective-permute-start | bytes 442376 | tf_op jit(solution)/shard_map/ppermute | solution.py:508
  29.8 2.4 %collective-permute-start.7 = (f32[1536,128]{1,0:T(8,128)S(1)}, f32[1536,128]{1,0:T(8,128)S(1)}, u32[]{:S(2)}, u32[]{:S(2)}) collective-permute-start(f32[1536,128]{1,0:T(8,128)S(1)} %shard_map.143.refs_1_), channel_id=1, source_target_pairs={{0,1},{1,0},{2,3},{3,2},{4,5},{5,4},{6,7},{7,6},{8,9},{9,8},{10,11... | collective-permute-start | bytes 2359304 | tf_op jit(solution)/shard_map/ppermute | solution.py:508

commit v5 on v4

--- a/solution.py
+++ b/solution.py
@@ -509,8 +509,9 @@
 
 
 def swap_next(values):
-    pairs = []
-    for i in range(1, lax.axis_size("mag") - 1, 2):
+    last = lax.axis_size("mag") - 1
+    pairs = [(0, 0), (last, last)]
+    for i in range(1, last, 2):
         pairs += [(i, i + 1), (i + 1, i)]
     return lax.ppermute(values, "mag", pairs)
 

time: 34.9 us -> 34.9 us (level)
  no operation moved by 1% of the time
where the time goes in v5:
time: 34.9 us; the launch traced here: 34.7 us
  Pallas kernels  14.4 us (41%)
  starting transfers between devices  13.5 us (39%)
  waiting for transfers between devices  6.04 us (17%)
  between operations  0.78 us (2%)
    pallas_call x9, Pallas kernels, run(): pallas(body if after else kernel, outs, many, scratch, in_specs)  14.4 us
    ppermute x6, starting transfers between devices, swap(): return lax.ppermute(values, 'mag', [(i, i ^ bit) for i in range(devices)])  12.2 us
    ppermute x6, waiting for transfers between devices, swap(): return lax.ppermute(values, 'mag', [(i, i ^ bit) for i in range(devices)])  6.04 us
    ppermute x2, starting transfers between devices, swap_next(): return lax.ppermute(values, 'mag', pairs)  1.33 us
  transfers between devices with their start and end apart: 8, of which 3 were waited for; matrix products, arithmetic and copies ran while one was open for 0% of the time, Pallas kernels for 23%

profile of v5, /device:TPU:0, one launch (start us, length us, event | category | flops | bytes accessed | tf_op | source)
XLA Modules:
  0.0 34.7 jit_solution(10928080149188747215)
XLA Ops:
  0.6 1.1 %shard_map.136 = (f32[8,4,16,128]{3,2,1,0:T(8,128)S(1)}, f32[2,2,16,128]{3,2,1,0:T(8,128)S(1)}, s32[8,128]{1,0:T(8,128)S(1)}, f32[64,128]{1,0:T(8,128)S(1)}) custom-call(f32[4,16,128]{2,1,0:T(8,128)} %rho_ref.1, f32[3,4,16,128]{3,2,1,0:T(8,128)} %vel_ref.1, f32[3,4,16,128]{3,2,1,0:T(8,128)} %mag_ref.1, f32[4,16,128]{2,1,0:T(8,128)} %prs_ref.1, ...), custom_call_target="tpu_custom_call" | custom-call | tf_op jit(solution)/shard_map/pallas_call | solution.py:33
  1.7 0.7 %collective-permute-start.1 = (f32[2,2,16,128]{3,2,1,0:T(8,128)S(1)}, f32[2,2,16,128]{3,2,1,0:T(8,128)S(1)}, u32[]{:S(2)}, u32[]{:S(2)}) collective-permute-start(f32[2,2,16,128]{3,2,1,0:T(8,128)S(1)} %get-tuple-element.28), channel_id=1, source_target_pairs={{0,0},{15,15},{1,2},{2,1},{3,4},{4,3},{5,6},{6,5},{7,8},{8,7},{9,1... | collective-permute-start | bytes 98312 | tf_op jit(solution)/shard_map/ppermute | solution.py:516
  2.4 4.4 %collective-permute-start = (f32[2,2,16,128]{3,2,1,0:T(8,128)S(1)}, f32[2,2,16,128]{3,2,1,0:T(8,128)S(1)}, u32[]{:S(2)}, u32[]{:S(2)}) collective-permute-start(f32[2,2,16,128]{3,2,1,0:T(8,128)S(1)} %get-tuple-element.28), channel_id=1, source_target_pairs={{0,1},{1,0},{2,3},{3,2},{4,5},{5,4},{6,7},{7,6},{8,9},{9,8},{10,11... | collective-permute-start | bytes 98312 | tf_op jit(solution)/shard_map/ppermute | solution.py:508
  6.8 1.1 %shard_map.137.refs_0_.own_side_ref = f32[8,4,16,128]{3,2,1,0:T(8,128)S(1)} custom-call(f32[8,4,16,128]{3,2,1,0:T(8,128)S(1)} %get-tuple-element.25.own_ref.refs_1_), custom_call_target="tpu_custom_call" | custom-call | tf_op jit(solution)/shard_map/pallas_call | solution.py:33
  7.9 0.0 collective-permute-done.1.refs_5_
  7.9 0.0 collective-permute-done.refs_4_
  7.9 0.0 copy-start.2
  7.9 0.3 shard_map.138
  8.2 0.0 copy-start
  8.3 0.0 copy-start.1
  8.3 4.1 %collective-permute-start.4 = (f32[72,128]{1,0:T(8,128)S(1)}, f32[72,128]{1,0:T(8,128)S(1)}, u32[]{:S(2)}, u32[]{:S(2)}) collective-permute-start(f32[72,128]{1,0:T(8,128)S(1)} %get-tuple-element.37), channel_id=1, source_target_pairs={{0,8},{1,9},{2,10},{3,11},{4,12},{5,13},{6,14},{7,15},{8,0},{9,1},... | collective-permute-start | bytes 110600 | tf_op jit(solution)/shard_map/ppermute | solution.py:508
  12.3 0.7 %collective-permute-start.3 = (f32[8,4,16,128]{3,2,1,0:T(8,128)S(1)}, f32[8,4,16,128]{3,2,1,0:T(8,128)S(1)}, u32[]{:S(2)}, u32[]{:S(2)}) collective-permute-start(f32[8,4,16,128]{3,2,1,0:T(8,128)S(1)} %get-tuple-element.29.own_ref), channel_id=1, source_target_pairs={{0,0},{15,15},{1,2},{2,1},{3,4},{4,3},{5,6},{6,5},{7,8},{8,7},{9,1... | collective-permute-start | bytes 786440 | tf_op jit(solution)/shard_map/ppermute | solution.py:516
  13.0 2.0 %collective-permute-start.2 = (f32[8,4,16,128]{3,2,1,0:T(8,128)S(1)}, f32[8,4,16,128]{3,2,1,0:T(8,128)S(1)}, u32[]{:S(2)}, u32[]{:S(2)}) collective-permute-start(f32[8,4,16,128]{3,2,1,0:T(8,128)S(1)} %get-tuple-element.29.own_ref), channel_id=1, source_target_pairs={{0,1},{1,0},{2,3},{3,2},{4,5},{5,4},{6,7},{7,6},{8,9},{9,8},{10,11... | collective-permute-start | bytes 786440 | tf_op jit(solution)/shard_map/ppermute | solution.py:508
  15.0 0.0 collective-permute-done.4
  15.0 1.6 %collective-permute-start.5 = (f32[144,128]{1,0:T(8,128)S(1)}, f32[144,128]{1,0:T(8,128)S(1)}, u32[]{:S(2)}, u32[]{:S(2)}) collective-permute-start(f32[144,128]{1,0:T(8,128)S(1)} %constant_dynamic-update-slice_fusion.refs_0_.refs_4_), channel_id=1, source_target_pairs={{0,4},{1,5},{2,6},{3,7},{4,0},{5,1},{6,2},{7,3},{8,12},{9,13},{10,... | collective-permute-start | bytes 221192 | tf_op jit(solution)/shard_map/ppermute | solution.py:508
  16.6 0.0 copy-done.2
  16.6 0.0 copy-done
  16.6 0.0 copy-done.1
  16.7 1.3 %shard_map.141 = (f32[1024,256]{1,0:T(8,128)S(1)}, f32[144,128]{1,0:T(8,128)S(1)}) custom-call(f32[144,128]{1,0:T(8,128)S(1)} %constant_dynamic-update-slice_fusion.refs_0_.refs_4_, s32[128,128]{1,0:T(8,128)S(1)} %bitcast.5, s32[128,128]{1,0:T(8,128)S(1)} %bitcast.9, s32[128,128]{1,0:T(8,128)S(1)} %bitcast.13, ...), custom_call_target="tpu_custom_call" | custom-call | tf_op jit(solution)/shard_map/pallas_call | solution.py:33
  18.0 4.3 %collective-permute-done.5.refs_1_ = f32[144,128]{1,0:T(8,128)S(1)} collective-permute-done((f32[144,128]{1,0:T(8,128)S(1)}, f32[144,128]{1,0:T(8,128)S(1)}, u32[]{:S(2)}, u32[]{:S(2)}) %collective-permute-start.5) | collective-permute-done | bytes 73760 | tf_op jit(solution)/shard_map/ppermute | solution.py:508
  22.3 0.0 collective-permute-start.6
  22.3 1.3 %shard_map.142 = (f32[1024,256]{1,0:T(8,128)S(1)}, f32[288,128]{1,0:T(8,128)S(1)}) custom-call(f32[1024,256]{1,0:T(8,128)S(1)} %get-tuple-element.38.refs_0_, f32[144,128]{1,0:T(8,128)S(1)} %collective-permute-done.5.refs_1_, s32[128,128]{1,0:T(8,128)S(1)} %bitcast.6, s32[128,128]{1,0:T(8,128)S(1)} %bitcast.10, s32[128,128]{1,0:T(8,128)S(1)} %bitcast.14, ...), custom_call_target="tpu_custom_call" | custom-call | tf_op jit(solution)/shard_map/pallas_call | solution.py:33
  23.6 0.0 collective-permute-done.3.eight_b
  23.6 0.0 collective-permute-done.2.eight_a
  23.6 2.2 %shard_map.139 = (f32[8,8,16,128]{3,2,1,0:T(8,128)S(1)}, f32[8,4,16,128]{3,2,1,0:T(8,128)S(1)}) custom-call(f32[8,4,16,128]{3,2,1,0:T(8,128)S(1)} %get-tuple-element.29.own_ref, f32[8,4,16,128]{3,2,1,0:T(8,128)S(1)} %collective-permute-done.2.eight_a, f32[8,4,16,128]{3,2,1,0:T(8,128)S(1)} %collective-permute-done.3.eight_b, ...), custom_call_target="tpu_custom_call" | custom-call | tf_op jit(solution)/shard_map/pallas_call | solution.py:33
  25.8 1.6 %collective-permute-done.6.refs_3_ = f32[288,128]{1,0:T(8,128)S(1)} collective-permute-done((f32[288,128]{1,0:T(8,128)S(1)}, f32[288,128]{1,0:T(8,128)S(1)}, u32[]{:S(2)}, u32[]{:S(2)}) %collective-permute-start.6) | collective-permute-done | bytes 147488 | tf_op jit(solution)/shard_map/ppermute | solution.py:508
  27.4 2.4 %shard_map.143.refs_1_ = f32[1536,128]{1,0:T(8,128)S(1)} custom-call(f32[8,4,16,128]{3,2,1,0:T(8,128)S(1)} %get-tuple-element.31.half_ref.refs_0_, f32[1024,256]{1,0:T(8,128)S(1)} %get-tuple-element.40.refs_1_, f32[288,128]{1,0:T(8,128)S(1)} %get-tuple-element.41.refs_2_, f32[288,128]{1,0:T(8,128)S(1)} %collective-permute-done.6.refs_3_, ...), custom_call_target="tpu_custom_call" | custom-call | tf_op jit(solution)/shard_map/pallas_call | solution.py:33
  29.8 0.1 collective-permute-start.7
  29.9 2.1 %shard_map.140 = (f32[4,16,128]{2,1,0:T(8,128)}, f32[3,4,16,128]{3,2,1,0:T(8,128)}, f32[3,4,16,128]{3,2,1,0:T(8,128)}, f32[4,16,128]{2,1,0:T(8,128)}, f32[8,128]{1,0:T(8,128)S(1)}) custom-call(f32[8,8,16,128]{3,2,1,0:T(8,128)S(1)} %get-tuple-element.30.next_ref, f32[8,4,16,128]{3,2,1,0:T(8,128)S(1)} %get-tuple-element.31.half_ref.refs_0_), custom_call_target="tpu_custom_call" | custom-call | tf_op jit(solution)/shard_map/pallas_call | solution.py:33
  32.0 0.1 collective-permute-done.7.refs_2_
  32.1 2.6 %shard_map.144 = (f32[4,2048]{1,0:T(4,128)}, f32[8,128]{1,0:T(8,128)}) custom-call(f32[8,128]{1,0:T(8,128)S(1)} %get-tuple-element.36.refs_0_, f32[1536,128]{1,0:T(8,128)S(1)} %shard_map.143.refs_1_, f32[1536,128]{1,0:T(8,128)S(1)} %collective-permute-done.7.refs_2_, s32[128,128]{1,0:T(8,128)S(1)} %bitcast.8, s32[128,128]{1,0:T(8,128)S(1)} %bitcast.12, ...), custom_call_target="tpu_custom_call" | custom-call | tf_op jit(solution)/shard_map/pallas_call | solution.py:33
  (4 shorter events, 0.0 us)
Async XLA Ops:
  1.7 6.2 %collective-permute-start.1 = (f32[2,2,16,128]{3,2,1,0:T(8,128)S(1)}, f32[2,2,16,128]{3,2,1,0:T(8,128)S(1)}, u32[]{:S(2)}, u32[]{:S(2)}) collective-permute-start(f32[2,2,16,128]{3,2,1,0:T(8,128)S(1)} %get-tuple-element.28), channel_id=1, source_target_pairs={{0,0},{15,15},{1,2},{2,1},{3,4},{4,3},{5,6},{6,5},{7,8},{8,7},{9,1... | collective-permute-start | bytes 98312 | tf_op jit(solution)/shard_map/ppermute | solution.py:516
  2.4 5.5 %collective-permute-start = (f32[2,2,16,128]{3,2,1,0:T(8,128)S(1)}, f32[2,2,16,128]{3,2,1,0:T(8,128)S(1)}, u32[]{:S(2)}, u32[]{:S(2)}) collective-permute-start(f32[2,2,16,128]{3,2,1,0:T(8,128)S(1)} %get-tuple-element.28), channel_id=1, source_target_pairs={{0,1},{1,0},{2,3},{3,2},{4,5},{5,4},{6,7},{7,6},{8,9},{9,8},{10,11... | collective-permute-start | bytes 98312 | tf_op jit(solution)/shard_map/ppermute | solution.py:508
  7.9 8.7 %copy-start.2 = (s32[16384]{0:T(1024)S(1)}, s32[16384]{0:T(1024)}, u32[]{:S(2)}) copy-start(s32[16384]{0:T(1024)} %param.17) | copy-start | bytes 196612
  8.2 8.4 %copy-start = (s32[16384,1]{0,1:T(1,128)S(1)}, s32[16384,1]{0,1:T(1,128)}, u32[]{:S(2)}) copy-start(s32[16384,1]{0,1:T(1,128)} %param.15) | copy-start | bytes 196612
  8.3 8.4 %copy-start.1 = (s32[16384]{0:T(1024)S(1)}, s32[16384]{0:T(1024)}, u32[]{:S(2)}) copy-start(s32[16384]{0:T(1024)} %param.16) | copy-start | bytes 196612
  8.3 6.8 %collective-permute-start.4 = (f32[72,128]{1,0:T(8,128)S(1)}, f32[72,128]{1,0:T(8,128)S(1)}, u32[]{:S(2)}, u32[]{:S(2)}) collective-permute-start(f32[72,128]{1,0:T(8,128)S(1)} %get-tuple-element.37), channel_id=1, source_target_pairs={{0,8},{1,9},{2,10},{3,11},{4,12},{5,13},{6,14},{7,15},{8,0},{9,1},... | collective-permute-start | bytes 110600 | tf_op jit(solution)/shard_map/ppermute | solution.py:508
  12.3 11.2 %collective-permute-start.3 = (f32[8,4,16,128]{3,2,1,0:T(8,128)S(1)}, f32[8,4,16,128]{3,2,1,0:T(8,128)S(1)}, u32[]{:S(2)}, u32[]{:S(2)}) collective-permute-start(f32[8,4,16,128]{3,2,1,0:T(8,128)S(1)} %get-tuple-element.29.own_ref), channel_id=1, source_target_pairs={{0,0},{15,15},{1,2},{2,1},{3,4},{4,3},{5,6},{6,5},{7,8},{8,7},{9,1... | collective-permute-start | bytes 786440 | tf_op jit(solution)/shard_map/ppermute | solution.py:516
  13.0 10.6 %collective-permute-start.2 = (f32[8,4,16,128]{3,2,1,0:T(8,128)S(1)}, f32[8,4,16,128]{3,2,1,0:T(8,128)S(1)}, u32[]{:S(2)}, u32[]{:S(2)}) collective-permute-start(f32[8,4,16,128]{3,2,1,0:T(8,128)S(1)} %get-tuple-element.29.own_ref), channel_id=1, source_target_pairs={{0,1},{1,0},{2,3},{3,2},{4,5},{5,4},{6,7},{7,6},{8,9},{9,8},{10,11... | collective-permute-start | bytes 786440 | tf_op jit(solution)/shard_map/ppermute | solution.py:508
  15.0 7.2 %collective-permute-start.5 = (f32[144,128]{1,0:T(8,128)S(1)}, f32[144,128]{1,0:T(8,128)S(1)}, u32[]{:S(2)}, u32[]{:S(2)}) collective-permute-start(f32[144,128]{1,0:T(8,128)S(1)} %constant_dynamic-update-slice_fusion.refs_0_.refs_4_), channel_id=1, source_target_pairs={{0,4},{1,5},{2,6},{3,7},{4,0},{5,1},{6,2},{7,3},{8,12},{9,13},{10,... | collective-permute-start | bytes 221192 | tf_op jit(solution)/shard_map/ppermute | solution.py:508
  22.3 5.1 %collective-permute-start.6 = (f32[288,128]{1,0:T(8,128)S(1)}, f32[288,128]{1,0:T(8,128)S(1)}, u32[]{:S(2)}, u32[]{:S(2)}) collective-permute-start(f32[288,128]{1,0:T(8,128)S(1)} %constant_dynamic-update-slice_fusion.2.refs_5_), channel_id=1, source_target_pairs={{0,2},{1,3},{2,0},{3,1},{4,6},{5,7},{6,4},{7,5},{8,10},{9,11},{10,... | collective-permute-start | bytes 442376 | tf_op jit(solution)/shard_map/ppermute | solution.py:508
  29.8 2.4 %collective-permute-start.7 = (f32[1536,128]{1,0:T(8,128)S(1)}, f32[1536,128]{1,0:T(8,128)S(1)}, u32[]{:S(2)}, u32[]{:S(2)}) collective-permute-start(f32[1536,128]{1,0:T(8,128)S(1)} %shard_map.143.refs_1_), channel_id=1, source_target_pairs={{0,1},{1,0},{2,3},{3,2},{4,5},{5,4},{6,7},{7,6},{8,9},{9,8},{10,11... | collective-permute-start | bytes 2359304 | tf_op jit(solution)/shard_map/ppermute | solution.py:508

commit v6 on v5

--- a/solution.py
+++ b/solution.py
@@ -238,12 +238,21 @@
     sweep_planes(next_ref, 2, cx, put, lambda step, q: sideways(q))
 
 
-def pick_current(own_ref, cell_ref, strip_ref, edge_a, edge_b, out_ref, own_out):
+def pick_current(own_ref, cell_ref, edge_a, *refs):
+    *far, out_ref, own_out = refs
     me = lax.axis_index("mag")
     last = lax.axis_size("mag") - 1
     even = me % 2 == 0
     cx, ny, nz = own_ref.shape[1:]
     own_out[...] = own_ref[...]
+    way = jnp.bitwise_xor(me, me + jnp.where(even, -1, 1))
+
+    def edge_b(k, x):
+        value = far[-1][k, x]
+        for bits, ref in enumerate(far[:-1], 2):
+            value = jnp.where(way == 2**bits - 1, ref[k, x], value)
+        return value
+
     rows = []
     for x in range(cx):
         bx, by, bz = (own_ref[4 + k, x] for k in range(3))
@@ -252,9 +261,9 @@
             if 0 <= x + step < cx:
                 return own_ref[4 + k, x + step]
             if step < 0:
-                below = jnp.where(even, edge_b[k - 1, 1], edge_a[k - 1, 1])
+                below = jnp.where(even, edge_b(k - 1, 1), edge_a[k - 1, 1])
                 return jnp.where(me == 0, own_ref[4 + k, x], below)
-            above = jnp.where(even, edge_a[k - 1, 0], edge_b[k - 1, 0])
+            above = jnp.where(even, edge_a[k - 1, 0], edge_b(k - 1, 0))
             return jnp.where(me == last, own_ref[4 + k, x], above)
 
         def along_x(k):
@@ -281,7 +290,6 @@
         found = found[:count] + found[count:]
         mine = jnp.where(index == hi[s : s + 1], found, 0.0)
         out_ref[s : s + 1, :] = jnp.sum(mine, axis=0, keepdims=True)
-    out_ref[points:, :] = strip_ref[...]
 
 
 def load_arguments(
@@ -401,19 +409,14 @@
 
 
 def scatter_last(blocks, points, lat, strips):
-    def kernel(total_ref, before_ref, load_ref, owner_ref, row_ref, lon_ref, out_ref, work_ref):
+    def kernel(total_ref, load_ref, owner_ref, row_ref, lon_ref, cond_ref, out_ref, work_ref):
         half = blocks // 2
         scatter_new(half, half, points, lat, strips)(
             total_ref, load_ref, owner_ref, row_ref, lon_ref, work_ref
         )
         count = work_ref.shape[0]
         out_ref[:count, :] = work_ref[:, :LANES] + work_ref[:, LANES:]
-        cells = lat * strips
-        stride = points + cells
-        for j in range(blocks):
-            ref = before_ref if j < half else load_ref
-            start = (j % half) * stride + points
-            out_ref[count + j * cells : count + (j + 1) * cells, :] = ref[start : start + cells, :]
+        out_ref[count:, :] = cond_ref[...]
 
     return kernel
 
@@ -549,7 +552,15 @@
             )
         )
     )
-    edge_a, edge_b = swap(edge, 1), swap_next(edge)
+    far, bits, conds = [], [], [strip]
+    bit = devices // 2
+    while bit > 1:
+        bits.append(bit)
+        far.insert(0, swap(edge, 2 * bit - 1))
+        bit //= 2
+    edge_a = swap(edge, 1)
+    for bit in bits:
+        conds.append(jnp.concatenate([conds[-1], swap(conds[-1], bit)], axis=0))
     own_side = call(stage_own, slab)(own)
 
     owner = foot_owner.reshape(-1, LANES)
@@ -557,26 +568,24 @@
     lon = foot_lon.reshape(-1, LANES)
 
     load, own = call(
-        pick_current, [shape((points + cells, LANES), F32), slab], after=(own_side,)
-    )(own, cell, strip, edge_a, edge_b)
+        pick_current, [shape((points, LANES), F32), slab], after=(own_side, conds[1])
+    )(own, cell, edge_a, *far)
     eight_a, eight_b = swap(own, 1), swap_next(own)
 
     grid = shape((count, 2 * LANES), F32)
     total, blocks, done = (), 1, 0
-    bit = devices // 2
-    while bit > 1:
+    for turn, bit in enumerate(bits):
         arrived = swap(load, bit)
-        if blocks > 1:
+        if turn > 0:
             kernel = handing_on(scatter_new(done, blocks - done, points, lat, strips), 1)
-            total, load = call(kernel, [grid, shape(load.shape, F32)])(
+            after = (conds[turn + 1],) if turn + 1 < len(bits) else ()
+            total, load = call(kernel, [grid, shape(load.shape, F32)], after=after)(
                 *total, new, owner, row, lon, load
             )
             total, done = (total,), blocks
-        before, new = load, arrived
         load = jnp.concatenate([load, arrived], axis=0)
-        if blocks == 1:
-            new = load
-        blocks, bit = blocks * 2, bit // 2
+        new = arrived if turn > 0 else load
+        blocks *= 2
 
     following, half = call(
         stage_one,
@@ -590,7 +599,7 @@
         grids,
         [pltpu.VMEM((count, 2 * LANES), F32)],
         after=(half,),
-    )(*total, before, new, owner, row, lon)
+    )(*total, new, owner, row, lon, conds[-1])
     theirs = swap(mine, 1)
 
     cell_shape = shape((cx, ny, nz), F32)

time: 34.9 us -> 38.1 us (1.092)
  starting transfers between devices: 13.5 us -> 17.8 us
  waiting for transfers between devices: 6.04 us -> 4.16 us
  Pallas kernels: 14.4 us -> 14.9 us
    ppermute x6 -> x12, starting transfers between devices: 12.2 us -> 17.2 us  [swap(): return lax.ppermute(values, 'mag', [(i, i ^ bit) for i in range(devices)])]
    ppermute x6 -> x12, waiting for transfers between devices: 6.04 us -> 4.16 us  [swap(): return lax.ppermute(values, 'mag', [(i, i ^ bit) for i in range(devices)])]
    ppermute x2 -> x1, starting transfers between devices: 1.33 us -> 0.67 us  [swap_next(): return lax.ppermute(values, 'mag', pairs)]
    pallas_call x9, Pallas kernels: 14.4 us -> 14.9 us  [run(): pallas(body if after else kernel, outs, many, scratch, in_specs)]
  transfers between devices with their start and end apart: 8 -> 13, of which waited for: 3 -> 2; matrix products, arithmetic and copies ran while one was open for 0% -> 0% of each run, Pallas kernels for 23% -> 23%
where the time goes in v6:
time: 38.1 us; the launch traced here: 37.8 us
  starting transfers between devices  17.8 us (47%)
  Pallas kernels  14.9 us (39%)
  waiting for transfers between devices  4.16 us (11%)
  between operations  0.79 us (2%)
    ppermute x12, starting transfers between devices, swap(): return lax.ppermute(values, 'mag', [(i, i ^ bit) for i in range(devices)])  17.2 us
    pallas_call x9, Pallas kernels, run(): pallas(body if after else kernel, outs, many, scratch, in_specs)  14.9 us
    ppermute x12, waiting for transfers between devices, swap(): return lax.ppermute(values, 'mag', [(i, i ^ bit) for i in range(devices)])  4.16 us
  transfers between devices with their start and end apart: 13, of which 2 were waited for; matrix products, arithmetic and copies ran while one was open for 0% of the time, Pallas kernels for 23%

profile of v6, /device:TPU:0, one launch (start us, length us, event | category | flops | bytes accessed | tf_op | source)
XLA Modules:
  0.0 37.8 jit_solution(18426136050292116045)
XLA Ops:
  0.6 1.1 %shard_map.136 = (f32[8,4,16,128]{3,2,1,0:T(8,128)S(1)}, f32[2,2,16,128]{3,2,1,0:T(8,128)S(1)}, s32[8,128]{1,0:T(8,128)S(1)}, f32[64,128]{1,0:T(8,128)S(1)}) custom-call(f32[4,16,128]{2,1,0:T(8,128)} %rho_ref.1, f32[3,4,16,128]{3,2,1,0:T(8,128)} %vel_ref.1, f32[3,4,16,128]{3,2,1,0:T(8,128)} %mag_ref.1, f32[4,16,128]{2,1,0:T(8,128)} %prs_ref.1, ...), custom_call_target="tpu_custom_call" | custom-call | tf_op jit(solution)/shard_map/pallas_call | solution.py:33
  1.7 5.5 %collective-permute-start.4 = (f32[2,2,16,128]{3,2,1,0:T(8,128)S(1)}, f32[2,2,16,128]{3,2,1,0:T(8,128)S(1)}, u32[]{:S(2)}, u32[]{:S(2)}) collective-permute-start(f32[2,2,16,128]{3,2,1,0:T(8,128)S(1)} %get-tuple-element.27), channel_id=1, source_target_pairs={{0,15},{1,14},{2,13},{3,12},{4,11},{5,10},{6,9},{7,8},{8,7},{9,6},... | collective-permute-start | bytes 98312 | tf_op jit(solution)/shard_map/ppermute | solution.py:511
  7.3 0.0 collective-permute-start.3
  7.3 0.8 %collective-permute-start.2 = (f32[2,2,16,128]{3,2,1,0:T(8,128)S(1)}, f32[2,2,16,128]{3,2,1,0:T(8,128)S(1)}, u32[]{:S(2)}, u32[]{:S(2)}) collective-permute-start(f32[2,2,16,128]{3,2,1,0:T(8,128)S(1)} %get-tuple-element.27), channel_id=1, source_target_pairs={{0,3},{1,2},{2,1},{3,0},{4,7},{5,6},{6,5},{7,4},{8,11},{9,10},{10,... | collective-permute-start | bytes 98312 | tf_op jit(solution)/shard_map/ppermute | solution.py:511
  8.0 0.6 %collective-permute-start.1 = (f32[2,2,16,128]{3,2,1,0:T(8,128)S(1)}, f32[2,2,16,128]{3,2,1,0:T(8,128)S(1)}, u32[]{:S(2)}, u32[]{:S(2)}) collective-permute-start(f32[2,2,16,128]{3,2,1,0:T(8,128)S(1)} %get-tuple-element.27), channel_id=1, source_target_pairs={{0,1},{1,0},{2,3},{3,2},{4,5},{5,4},{6,7},{7,6},{8,9},{9,8},{10,11... | collective-permute-start | bytes 98312 | tf_op jit(solution)/shard_map/ppermute | solution.py:511
  8.7 1.2 %collective-permute-start = (f32[64,128]{1,0:T(8,128)S(1)}, f32[64,128]{1,0:T(8,128)S(1)}, u32[]{:S(2)}, u32[]{:S(2)}) collective-permute-start(f32[64,128]{1,0:T(8,128)S(1)} %get-tuple-element.25), channel_id=1, source_target_pairs={{0,8},{1,9},{2,10},{3,11},{4,12},{5,13},{6,14},{7,15},{8,0},{9,1},... | collective-permute-start | bytes 98312 | tf_op jit(solution)/shard_map/ppermute | solution.py:511
  9.9 1.1 %shard_map.137.refs_0_.own_side_ref = f32[8,4,16,128]{3,2,1,0:T(8,128)S(1)} custom-call(f32[8,4,16,128]{3,2,1,0:T(8,128)S(1)} %get-tuple-element.24.own_ref.refs_2_), custom_call_target="tpu_custom_call" | custom-call | tf_op jit(solution)/shard_map/pallas_call | solution.py:33
  11.0 2.5 %collective-permute-done = f32[64,128]{1,0:T(8,128)S(1)} collective-permute-done((f32[64,128]{1,0:T(8,128)S(1)}, f32[64,128]{1,0:T(8,128)S(1)}, u32[]{:S(2)}, u32[]{:S(2)}) %collective-permute-start) | collective-permute-done | bytes 32800 | tf_op jit(solution)/shard_map/ppermute | solution.py:511
  13.5 2.5 %collective-permute-start.7 = (f32[128,128]{1,0:T(8,128)S(1)}, f32[128,128]{1,0:T(8,128)S(1)}, u32[]{:S(2)}, u32[]{:S(2)}) collective-permute-start(f32[128,128]{1,0:T(8,128)S(1)} %get-tuple-element.43.refs_1_), channel_id=1, source_target_pairs={{0,4},{1,5},{2,6},{3,7},{4,0},{5,1},{6,2},{7,3},{8,12},{9,13},{10,... | collective-permute-start | bytes 196616 | tf_op jit(solution)/shard_map/ppermute | solution.py:511
  16.0 0.0 collective-permute-done.3.refs_6_
  16.0 0.0 collective-permute-done.2.refs_5_
  16.0 0.0 copy-start.2
  16.0 0.3 shard_map.138
  16.3 0.4 %collective-permute-start.8 = (f32[8,128]{1,0:T(8,128)S(1)}, f32[8,128]{1,0:T(8,128)S(1)}, u32[]{:S(2)}, u32[]{:S(2)}) collective-permute-start(f32[8,128]{1,0:T(8,128)S(1)} %get-tuple-element.36), channel_id=1, source_target_pairs={{0,8},{1,9},{2,10},{3,11},{4,12},{5,13},{6,14},{7,15},{8,0},{9,1},... | collective-permute-start | bytes 12296 | tf_op jit(solution)/shard_map/ppermute | solution.py:511
  16.7 0.7 %collective-permute-start.6 = (f32[8,4,16,128]{3,2,1,0:T(8,128)S(1)}, f32[8,4,16,128]{3,2,1,0:T(8,128)S(1)}, u32[]{:S(2)}, u32[]{:S(2)}) collective-permute-start(f32[8,4,16,128]{3,2,1,0:T(8,128)S(1)} %get-tuple-element.28.own_ref), channel_id=1, source_target_pairs={{0,0},{15,15},{1,2},{2,1},{3,4},{4,3},{5,6},{6,5},{7,8},{8,7},{9,1... | collective-permute-start | bytes 786440 | tf_op jit(solution)/shard_map/ppermute | solution.py:519
  17.4 1.9 %collective-permute-start.5 = (f32[8,4,16,128]{3,2,1,0:T(8,128)S(1)}, f32[8,4,16,128]{3,2,1,0:T(8,128)S(1)}, u32[]{:S(2)}, u32[]{:S(2)}) collective-permute-start(f32[8,4,16,128]{3,2,1,0:T(8,128)S(1)} %get-tuple-element.28.own_ref), channel_id=1, source_target_pairs={{0,1},{1,0},{2,3},{3,2},{4,5},{5,4},{6,7},{7,6},{8,9},{9,8},{10,11... | collective-permute-start | bytes 786440 | tf_op jit(solution)/shard_map/ppermute | solution.py:511
  19.3 1.6 %collective-permute-done.8 = f32[8,128]{1,0:T(8,128)S(1)} collective-permute-done((f32[8,128]{1,0:T(8,128)S(1)}, f32[8,128]{1,0:T(8,128)S(1)}, u32[]{:S(2)}, u32[]{:S(2)}) %collective-permute-start.8) | collective-permute-done | bytes 4128 | tf_op jit(solution)/shard_map/ppermute | solution.py:511
  21.0 0.0 copy-start
  21.0 0.0 copy-start.1
  21.0 2.5 %collective-permute-start.11 = (f32[256,128]{1,0:T(8,128)S(1)}, f32[256,128]{1,0:T(8,128)S(1)}, u32[]{:S(2)}, u32[]{:S(2)}) collective-permute-start(f32[256,128]{1,0:T(8,128)S(1)} %constant_dynamic-update-slice_fusion.2.refs_0_), channel_id=1, source_target_pairs={{0,2},{1,3},{2,0},{3,1},{4,6},{5,7},{6,4},{7,5},{8,10},{9,11},{10,... | collective-permute-start | bytes 393224 | tf_op jit(solution)/shard_map/ppermute | solution.py:511
  23.5 1.3 %shard_map.141 = (f32[1024,256]{1,0:T(8,128)S(1)}, f32[16,128]{1,0:T(8,128)S(1)}) custom-call(f32[256,128]{1,0:T(8,128)S(1)} %constant_dynamic-update-slice_fusion.2.refs_0_, f32[16,128]{1,0:T(8,128)S(1)} %constant_dynamic-update-slice_fusion.5.refs_1_.refs_5_, s32[128,128]{1,0:T(8,128)S(1)} %bitcast.5, s32[128,128]{1,0:T(8,128)S(1)} %bitcast.9, ...), custom_call_target="tpu_custom_call" | custom-call | tf_op jit(solution)/shard_map/pallas_call | solution.py:33
  24.9 0.8 %collective-permute-start.10 = (f32[32,128]{1,0:T(8,128)S(1)}, f32[32,128]{1,0:T(8,128)S(1)}, u32[]{:S(2)}, u32[]{:S(2)}) collective-permute-start(f32[32,128]{1,0:T(8,128)S(1)} %constant_dynamic-update-slice_fusion.7.refs_5_), channel_id=1, source_target_pairs={{0,2},{1,3},{2,0},{3,1},{4,6},{5,7},{6,4},{7,5},{8,10},{9,11},{10,... | collective-permute-start | bytes 49160 | tf_op jit(solution)/shard_map/ppermute | solution.py:511
  25.7 1.8 %shard_map.142 = (f32[1024,256]{1,0:T(8,128)S(1)}, f32[32,128]{1,0:T(8,128)}) custom-call(f32[1024,256]{1,0:T(8,128)S(1)} %get-tuple-element.37.refs_0_, f32[16,128]{1,0:T(8,128)S(1)} %collective-permute-done.9.refs_1_, s32[128,128]{1,0:T(8,128)S(1)} %bitcast.6, s32[128,128]{1,0:T(8,128)S(1)} %bitcast.10, s32[128,128]{1,0:T(8,128)S(1)} %bitcast.14, ...), custom_call_target="tpu_custom_call" | custom-call | tf_op jit(solution)/shard_map/pallas_call | solution.py:33
  27.6 0.0 collective-permute-done.6.eight_b
  27.6 0.0 collective-permute-done.5.eight_a
  27.6 2.2 %shard_map.139 = (f32[8,8,16,128]{3,2,1,0:T(8,128)S(1)}, f32[8,4,16,128]{3,2,1,0:T(8,128)S(1)}) custom-call(f32[8,4,16,128]{3,2,1,0:T(8,128)S(1)} %get-tuple-element.28.own_ref, f32[8,4,16,128]{3,2,1,0:T(8,128)S(1)} %collective-permute-done.5.eight_a, f32[8,4,16,128]{3,2,1,0:T(8,128)S(1)} %collective-permute-done.6.eight_b, ...), custom_call_target="tpu_custom_call" | custom-call | tf_op jit(solution)/shard_map/pallas_call | solution.py:33
  29.8 0.0 collective-permute-done.10.refs_2_
  29.8 2.4 %shard_map.143.refs_1_ = f32[1536,128]{1,0:T(8,128)S(1)} custom-call(f32[8,4,16,128]{3,2,1,0:T(8,128)S(1)} %get-tuple-element.30.half_ref.refs_0_, f32[1024,256]{1,0:T(8,128)S(1)} %get-tuple-element.39.refs_1_, f32[32,128]{1,0:T(8,128)S(1)} %collective-permute-done.10.refs_2_, s32[128,128]{1,0:T(8,128)S(1)} %bitcast.7, s32[128,128]{1,0:T(8,128)S(1)} %bitcast.11, ...), custom_call_target="tpu_custom_call" | custom-call | tf_op jit(solution)/shard_map/pallas_call | solution.py:33
  32.2 0.9 %collective-permute-start.12 = (f32[1536,128]{1,0:T(8,128)S(1)}, f32[1536,128]{1,0:T(8,128)S(1)}, u32[]{:S(2)}, u32[]{:S(2)}) collective-permute-start(f32[1536,128]{1,0:T(8,128)S(1)} %shard_map.143.refs_1_), channel_id=1, source_target_pairs={{0,1},{1,0},{2,3},{3,2},{4,5},{5,4},{6,7},{7,6},{8,9},{9,8},{10,11... | collective-permute-start | bytes 2359304 | tf_op jit(solution)/shard_map/ppermute | solution.py:511
  33.1 2.1 %shard_map.140 = (f32[4,16,128]{2,1,0:T(8,128)}, f32[3,4,16,128]{3,2,1,0:T(8,128)}, f32[3,4,16,128]{3,2,1,0:T(8,128)}, f32[4,16,128]{2,1,0:T(8,128)}, f32[8,128]{1,0:T(8,128)S(1)}) custom-call(f32[8,8,16,128]{3,2,1,0:T(8,128)S(1)} %get-tuple-element.29.next_ref, f32[8,4,16,128]{3,2,1,0:T(8,128)S(1)} %get-tuple-element.30.half_ref.refs_0_), custom_call_target="tpu_custom_call" | custom-call | tf_op jit(solution)/shard_map/pallas_call | solution.py:33
  35.2 0.0 collective-permute-done.12.refs_2_
  35.2 2.6 %shard_map.144 = (f32[4,2048]{1,0:T(4,128)}, f32[8,128]{1,0:T(8,128)}) custom-call(f32[8,128]{1,0:T(8,128)S(1)} %get-tuple-element.35.refs_0_, f32[1536,128]{1,0:T(8,128)S(1)} %shard_map.143.refs_1_, f32[1536,128]{1,0:T(8,128)S(1)} %collective-permute-done.12.refs_2_, s32[128,128]{1,0:T(8,128)S(1)} %bitcast.8, s32[128,128]{1,0:T(8,128)S(1)} %bitcast.12, ...), custom_call_target="tpu_custom_call" | custom-call | tf_op jit(solution)/shard_map/pallas_call | solution.py:33
  (17 shorter events, 0.1 us)
Async XLA Ops:
  1.7 14.2 %collective-permute-start.4 = (f32[2,2,16,128]{3,2,1,0:T(8,128)S(1)}, f32[2,2,16,128]{3,2,1,0:T(8,128)S(1)}, u32[]{:S(2)}, u32[]{:S(2)}) collective-permute-start(f32[2,2,16,128]{3,2,1,0:T(8,128)S(1)} %get-tuple-element.27), channel_id=1, source_target_pairs={{0,15},{1,14},{2,13},{3,12},{4,11},{5,10},{6,9},{7,8},{8,7},{9,6},... | collective-permute-start | bytes 98312 | tf_op jit(solution)/shard_map/ppermute | solution.py:511
  7.3 8.7 %collective-permute-start.3 = (f32[2,2,16,128]{3,2,1,0:T(8,128)S(1)}, f32[2,2,16,128]{3,2,1,0:T(8,128)S(1)}, u32[]{:S(2)}, u32[]{:S(2)}) collective-permute-start(f32[2,2,16,128]{3,2,1,0:T(8,128)S(1)} %get-tuple-element.27), channel_id=1, source_target_pairs={{0,7},{1,6},{2,5},{3,4},{4,3},{5,2},{6,1},{7,0},{8,15},{9,14},{10,... | collective-permute-start | bytes 98312 | tf_op jit(solution)/shard_map/ppermute | solution.py:511
  7.3 8.7 %collective-permute-start.2 = (f32[2,2,16,128]{3,2,1,0:T(8,128)S(1)}, f32[2,2,16,128]{3,2,1,0:T(8,128)S(1)}, u32[]{:S(2)}, u32[]{:S(2)}) collective-permute-start(f32[2,2,16,128]{3,2,1,0:T(8,128)S(1)} %get-tuple-element.27), channel_id=1, source_target_pairs={{0,3},{1,2},{2,1},{3,0},{4,7},{5,6},{6,5},{7,4},{8,11},{9,10},{10,... | collective-permute-start | bytes 98312 | tf_op jit(solution)/shard_map/ppermute | solution.py:511
  8.0 7.9 %collective-permute-start.1 = (f32[2,2,16,128]{3,2,1,0:T(8,128)S(1)}, f32[2,2,16,128]{3,2,1,0:T(8,128)S(1)}, u32[]{:S(2)}, u32[]{:S(2)}) collective-permute-start(f32[2,2,16,128]{3,2,1,0:T(8,128)S(1)} %get-tuple-element.27), channel_id=1, source_target_pairs={{0,1},{1,0},{2,3},{3,2},{4,5},{5,4},{6,7},{7,6},{8,9},{9,8},{10,11... | collective-permute-start | bytes 98312 | tf_op jit(solution)/shard_map/ppermute | solution.py:511
  8.7 4.8 %collective-permute-start = (f32[64,128]{1,0:T(8,128)S(1)}, f32[64,128]{1,0:T(8,128)S(1)}, u32[]{:S(2)}, u32[]{:S(2)}) collective-permute-start(f32[64,128]{1,0:T(8,128)S(1)} %get-tuple-element.25), channel_id=1, source_target_pairs={{0,8},{1,9},{2,10},{3,11},{4,12},{5,13},{6,14},{7,15},{8,0},{9,1},... | collective-permute-start | bytes 98312 | tf_op jit(solution)/shard_map/ppermute | solution.py:511
  13.5 7.5 %collective-permute-start.7 = (f32[128,128]{1,0:T(8,128)S(1)}, f32[128,128]{1,0:T(8,128)S(1)}, u32[]{:S(2)}, u32[]{:S(2)}) collective-permute-start(f32[128,128]{1,0:T(8,128)S(1)} %get-tuple-element.43.refs_1_), channel_id=1, source_target_pairs={{0,4},{1,5},{2,6},{3,7},{4,0},{5,1},{6,2},{7,3},{8,12},{9,13},{10,... | collective-permute-start | bytes 196616 | tf_op jit(solution)/shard_map/ppermute | solution.py:511
  16.0 7.5 %copy-start.2 = (s32[16384]{0:T(1024)S(1)}, s32[16384]{0:T(1024)}, u32[]{:S(2)}) copy-start(s32[16384]{0:T(1024)} %param.17) | copy-start | bytes 196612
  16.3 4.7 %collective-permute-start.8 = (f32[8,128]{1,0:T(8,128)S(1)}, f32[8,128]{1,0:T(8,128)S(1)}, u32[]{:S(2)}, u32[]{:S(2)}) collective-permute-start(f32[8,128]{1,0:T(8,128)S(1)} %get-tuple-element.36), channel_id=1, source_target_pairs={{0,8},{1,9},{2,10},{3,11},{4,12},{5,13},{6,14},{7,15},{8,0},{9,1},... | collective-permute-start | bytes 12296 | tf_op jit(solution)/shard_map/ppermute | solution.py:511
  16.7 10.8 %collective-permute-start.6 = (f32[8,4,16,128]{3,2,1,0:T(8,128)S(1)}, f32[8,4,16,128]{3,2,1,0:T(8,128)S(1)}, u32[]{:S(2)}, u32[]{:S(2)}) collective-permute-start(f32[8,4,16,128]{3,2,1,0:T(8,128)S(1)} %get-tuple-element.28.own_ref), channel_id=1, source_target_pairs={{0,0},{15,15},{1,2},{2,1},{3,4},{4,3},{5,6},{6,5},{7,8},{8,7},{9,1... | collective-permute-start | bytes 786440 | tf_op jit(solution)/shard_map/ppermute | solution.py:519
  17.4 10.2 %collective-permute-start.5 = (f32[8,4,16,128]{3,2,1,0:T(8,128)S(1)}, f32[8,4,16,128]{3,2,1,0:T(8,128)S(1)}, u32[]{:S(2)}, u32[]{:S(2)}) collective-permute-start(f32[8,4,16,128]{3,2,1,0:T(8,128)S(1)} %get-tuple-element.28.own_ref), channel_id=1, source_target_pairs={{0,1},{1,0},{2,3},{3,2},{4,5},{5,4},{6,7},{7,6},{8,9},{9,8},{10,11... | collective-permute-start | bytes 786440 | tf_op jit(solution)/shard_map/ppermute | solution.py:511
  21.0 3.9 %collective-permute-start.9 = (f32[16,128]{1,0:T(8,128)S(1)}, f32[16,128]{1,0:T(8,128)S(1)}, u32[]{:S(2)}, u32[]{:S(2)}) collective-permute-start(f32[16,128]{1,0:T(8,128)S(1)} %constant_dynamic-update-slice_fusion.5.refs_1_.refs_5_), channel_id=1, source_target_pairs={{0,4},{1,5},{2,6},{3,7},{4,0},{5,1},{6,2},{7,3},{8,12},{9,13},{10,... | collective-permute-start | bytes 24584 | tf_op jit(solution)/shard_map/ppermute | solution.py:511
  21.0 2.5 %copy-start = (s32[16384,1]{0,1:T(1,128)S(1)}, s32[16384,1]{0,1:T(1,128)}, u32[]{:S(2)}) copy-start(s32[16384,1]{0,1:T(1,128)} %param.15) | copy-start | bytes 196612
  21.0 2.5 %copy-start.1 = (s32[16384]{0:T(1024)S(1)}, s32[16384]{0:T(1024)}, u32[]{:S(2)}) copy-start(s32[16384]{0:T(1024)} %param.16) | copy-start | bytes 196612
  21.0 6.5 %collective-permute-start.11 = (f32[256,128]{1,0:T(8,128)S(1)}, f32[256,128]{1,0:T(8,128)S(1)}, u32[]{:S(2)}, u32[]{:S(2)}) collective-permute-start(f32[256,128]{1,0:T(8,128)S(1)} %constant_dynamic-update-slice_fusion.2.refs_0_), channel_id=1, source_target_pairs={{0,2},{1,3},{2,0},{3,1},{4,6},{5,7},{6,4},{7,5},{8,10},{9,11},{10,... | collective-permute-start | bytes 393224 | tf_op jit(solution)/shard_map/ppermute | solution.py:511
  24.9 4.9 %collective-permute-start.10 = (f32[32,128]{1,0:T(8,128)S(1)}, f32[32,128]{1,0:T(8,128)S(1)}, u32[]{:S(2)}, u32[]{:S(2)}) collective-permute-start(f32[32,128]{1,0:T(8,128)S(1)} %constant_dynamic-update-slice_fusion.7.refs_5_), channel_id=1, source_target_pairs={{0,2},{1,3},{2,0},{3,1},{4,6},{5,7},{6,4},{7,5},{8,10},{9,11},{10,... | collective-permute-start | bytes 49160 | tf_op jit(solution)/shard_map/ppermute | solution.py:511
  32.2 3.0 %collective-permute-start.12 = (f32[1536,128]{1,0:T(8,128)S(1)}, f32[1536,128]{1,0:T(8,128)S(1)}, u32[]{:S(2)}, u32[]{:S(2)}) collective-permute-start(f32[1536,128]{1,0:T(8,128)S(1)} %shard_map.143.refs_1_), channel_id=1, source_target_pairs={{0,1},{1,0},{2,3},{3,2},{4,5},{5,4},{6,7},{7,6},{8,9},{9,8},{10,11... | collective-permute-start | bytes 2359304 | tf_op jit(solution)/shard_map/ppermute | solution.py:511

commit v7 on v4

--- a/solution.py
+++ b/solution.py
@@ -173,27 +173,32 @@
     lax.fori_loop(0, own_ref.shape[1], body, 0)
 
 
-def stage_one(own_ref, eight_a, eight_b, own_side_ref, next_ref, half_ref, pad_ref, side_ref):
+def split_planes(ref, out_a, out_b):
+    odd = lax.axis_index("mag") % 2
+    top = ref.shape[1] - 2
+    for k in range(8):
+        out_a[k] = ref[k, pl.ds((1 - odd) * top, 2)]
+        out_b[k] = ref[k, pl.ds(odd * top, 2)]
+
+
+def pad_planes(ref, from_a, from_b, pad_ref):
     me = lax.axis_index("mag")
     last = lax.axis_size("mag") - 1
     even = me % 2 == 0
-    cx = own_ref.shape[1]
+    cx = ref.shape[1]
     for k in range(8):
+        for x in range(2):
+            low = jnp.where(even, from_b[k, x], from_a[k, x])
+            high = jnp.where(even, from_a[k, x], from_b[k, x])
+            pad_ref[k, x] = jnp.where(me == 0, ref[k, 0], low)
+            pad_ref[k, cx + 2 + x] = jnp.where(me == last, ref[k, cx - 1], high)
         for x in range(cx):
-            low = jnp.where(even, eight_b[k, x], eight_a[k, x])
-            high = jnp.where(even, eight_a[k, x], eight_b[k, x])
-            pad_ref[k, x] = jnp.where(me == 0, own_ref[k, 0], low)
-            pad_ref[k, cx + x] = own_ref[k, x]
-            pad_ref[k, 2 * cx + x] = jnp.where(me == last, own_ref[k, cx - 1], high)
-            side_ref[k, 2 + x] = own_side_ref[k, x]
-
-    def beside(i, carry):
-        step = jnp.where(i < 2, i, cx + i)
-        for k, value in enumerate(sideways(plane(pad_ref, cx - 2 + step))):
-            side_ref[k, step] = value
-        return carry
-
-    lax.fori_loop(0, 4, beside, 0)
+            pad_ref[k, 2 + x] = ref[k, x]
+
+
+def stage_one(own_ref, from_a, from_b, side_ref, load_ref, next_ref, half_ref, out_a, out_b, load_out, pad_ref):
+    pad_planes(own_ref, from_a, from_b, pad_ref)
+    load_out[...] = load_ref[...]
 
     def put(x, step, q, change):
         start = conserved(q)
@@ -201,30 +206,14 @@
         q1 = primitive(first)
         for k in range(8):
             next_ref[k, step] = q1[k]
-
-        @pl.when(jnp.logical_and(step >= 2, step < cx + 2))
-        def _():
-            for k in range(8):
-                half_ref[k, step - 2] = 0.5 * (start[k] + first[k])
-
-    sweep_planes(pad_ref, cx - 2, cx + 4, put, lambda step, q: plane(side_ref, step))
-
-    @pl.when(me == 0)
-    def _():
-        for k in range(8):
-            next_ref[k, 0] = next_ref[k, 2]
-            next_ref[k, 1] = next_ref[k, 2]
-
-    @pl.when(me == last)
-    def _():
-        for k in range(8):
-            next_ref[k, cx + 2] = next_ref[k, cx + 1]
-            next_ref[k, cx + 3] = next_ref[k, cx + 1]
-
-
-def stage_two(next_ref, half_ref, rho_ref, vel_ref, mag_ref, prs_ref, end_ref):
+            half_ref[k, step] = 0.5 * (start[k] + first[k])
+
+    sweep_planes(pad_ref, 2, own_ref.shape[1], put, lambda step, q: plane(side_ref, step))
+    split_planes(next_ref, out_a, out_b)
+
+
+def stage_two(pad_ref, half_ref, rho_ref, vel_ref, mag_ref, prs_ref, end_ref):
     end_ref[...] = half_ref[0, 0, 0:8]
-    cx = half_ref.shape[1]
 
     def put(x, step, q, change):
         final = [half_ref[k, step] + (0.5 * TIME_STEP) * change[k] for k in range(8)]
@@ -235,15 +224,14 @@
             mag_ref[k, step] = q2[4 + k]
         prs_ref[step] = q2[7]
 
-    sweep_planes(next_ref, 2, cx, put, lambda step, q: sideways(q))
-
-
-def pick_current(own_ref, cell_ref, strip_ref, edge_a, edge_b, out_ref, own_out):
+    sweep_planes(pad_ref, 2, half_ref.shape[1], put, lambda step, q: sideways(q))
+
+
+def pick_current(own_ref, cell_ref, strip_ref, from_a, from_b, out_ref):
     me = lax.axis_index("mag")
     last = lax.axis_size("mag") - 1
     even = me % 2 == 0
     cx, ny, nz = own_ref.shape[1:]
-    own_out[...] = own_ref[...]
     rows = []
     for x in range(cx):
         bx, by, bz = (own_ref[4 + k, x] for k in range(3))
@@ -252,9 +240,9 @@
             if 0 <= x + step < cx:
                 return own_ref[4 + k, x + step]
             if step < 0:
-                below = jnp.where(even, edge_b[k - 1, 1], edge_a[k - 1, 1])
+                below = jnp.where(even, from_b[4 + k, 1], from_a[4 + k, 1])
                 return jnp.where(me == 0, own_ref[4 + k, x], below)
-            above = jnp.where(even, edge_a[k - 1, 0], edge_b[k - 1, 0])
+            above = jnp.where(even, from_a[4 + k, 0], from_b[4 + k, 0])
             return jnp.where(me == last, own_ref[4 + k, x], above)
 
         def along_x(k):
@@ -285,13 +273,10 @@
 
 
 def load_arguments(
-    rho_ref, vel_ref, mag_ref, prs_ref, cell_ref, cond_ref, own_out, edge_out, cell_out, strip_out, rows, sems
+    rho_ref, vel_ref, mag_ref, prs_ref, cell_ref, cond_ref, own_out, a_out, b_out, cell_out, strip_out, rows, sems
 ):
-    last = mag_ref.shape[1] - 1
     pairs = [
         (cond_ref, rows),
-        (mag_ref.at[pl.ds(1, 2), pl.ds(0, 1)], edge_out.at[:, pl.ds(0, 1)]),
-        (mag_ref.at[pl.ds(1, 2), pl.ds(last, 1)], edge_out.at[:, pl.ds(1, 1)]),
         (cell_ref, cell_out),
         (rho_ref, own_out.at[0]),
         (vel_ref, own_out.at[pl.ds(1, 3)]),
@@ -313,6 +298,7 @@
             strip_out[place : place + 1, :] = rows[r : r + 1, strip * LANES : (strip + 1) * LANES]
     for copy in copies[1:]:
         copy.wait()
+    split_planes(own_out, a_out, b_out)
 
 
 def east_of(v):
@@ -509,9 +495,8 @@
 
 
 def swap_next(values):
-    pairs = []
-    for i in range(1, lax.axis_size("mag") - 1, 2):
-        pairs += [(i, i + 1), (i + 1, i)]
+    devices = lax.axis_size("mag")
+    pairs = [(i, (i + (1 if i % 2 else -1)) % devices) for i in range(devices)]
     return lax.ppermute(values, "mag", pairs)
 
 
@@ -530,10 +515,11 @@
 
     tile = shape((points, LANES), I32)
     slab = shape((8, cx, ny, nz), F32)
-    own, edge, cell, strip = call(
+    two = shape((8, 2, ny, nz), F32)
+    own, to_a, to_b, cell, strip = call(
         load_arguments,
-        [slab, shape((2, 2, ny, nz), F32), tile, shape((cells, LANES), F32)],
-        [pltpu.VMEM((lat, columns), F32), pltpu.SemaphoreType.DMA((8,))],
+        [slab, two, two, tile, shape((cells, LANES), F32)],
+        [pltpu.VMEM((lat, columns), F32), pltpu.SemaphoreType.DMA((6,))],
         [HBM] * 6,
     )(
         *(
@@ -548,17 +534,20 @@
             )
         )
     )
-    edge_a, edge_b = swap(edge, 1), swap_next(edge)
+    from_a, from_b = swap(to_a, 1), swap_next(to_b)
     own_side = call(stage_own, slab)(own)
 
     owner = foot_owner.reshape(-1, LANES)
     row = foot_row.reshape(-1, LANES)
     lon = foot_lon.reshape(-1, LANES)
 
-    load, own = call(
-        pick_current, [shape((points + cells, LANES), F32), slab], after=(own_side,)
-    )(own, cell, strip, edge_a, edge_b)
-    eight_a, eight_b = swap(own, 1), swap_next(own)
+    payload = shape((points + cells, LANES), F32)
+    load = call(pick_current, payload, after=(own_side,))(own, cell, strip, from_a, from_b)
+    pad = [pltpu.VMEM((8, cx + 4, ny, nz), F32)]
+    following, half, next_a, next_b, after_one = call(
+        stage_one, [slab, slab, two, two, payload], pad
+    )(own, from_a, from_b, own_side, load)
+    next_a, next_b = swap(next_a, 1), swap_next(next_b)
 
     grid = shape((count, 2 * LANES), F32)
     total, blocks, done = (), 1, 0
@@ -572,23 +561,18 @@
             )
             total, done = (total,), blocks
         before, new = load, arrived
-        load = jnp.concatenate([load, arrived], axis=0)
+        load = jnp.concatenate([after_one if blocks == 1 else load, arrived], axis=0)
         if blocks == 1:
             new = load
         blocks, bit = blocks * 2, bit // 2
 
-    following, half = call(
-        stage_one,
-        [shape((8, cx + 4, ny, nz), F32), slab],
-        [pltpu.VMEM((8, 3 * cx, ny, nz), F32), pltpu.VMEM((8, cx + 4, ny, nz), F32)],
-    )(own, eight_a, eight_b, own_side)
-
+    padded = call(pad_planes, shape((8, cx + 4, ny, nz), F32))(following, next_a, next_b)
     grids = shape((count + count // 2, LANES), F32)
     mine = call(
         scatter_last(blocks, points, lat, strips),
         grids,
         [pltpu.VMEM((count, 2 * LANES), F32)],
-        after=(half,),
+        after=(padded,),
     )(*total, before, new, owner, row, lon)
     theirs = swap(mine, 1)
 
@@ -596,7 +580,7 @@
     vector_shape = shape((3, cx, ny, nz), F32)
     new_density, new_velocity, new_field, new_pressure, end = call(
         stage_two, [cell_shape, vector_shape, vector_shape, cell_shape, shape((8, LANES), F32)]
-    )(following, half)
+    )(padded, half)
 
     potential, shell_potential = call(
         solve_and_read(blocks, points, lat, strips),

time: 34.9 us -> 35.3 us (1.011)
  waiting for transfers between devices: 6.04 us -> 9.79 us
  starting transfers between devices: 13.5 us -> 11.7 us
  Pallas kernels: 14.4 us -> 12.8 us
    ppermute x6, starting transfers between devices: 12.2 us -> 1.89 us  [swap(): return lax.ppermute(values, 'mag', [(i, i ^ bit) for i in range(devices)])]
    ppermute x2, starting transfers between devices: 1.33 us -> 9.84 us  [swap_next(): return lax.ppermute(values, 'mag', pairs)]
    ppermute x2, waiting for transfers between devices: 0.01 us -> 3.31 us  [swap_next(): return lax.ppermute(values, 'mag', pairs)]
    pallas_call x9 -> x10, Pallas kernels: 14.4 us -> 12.8 us  [run(): pallas(body if after else kernel, outs, many, scratch, in_specs)]
    ppermute x6, waiting for transfers between devices: 6.04 us -> 6.47 us  [swap(): return lax.ppermute(values, 'mag', [(i, i ^ bit) for i in range(devices)])]
  transfers between devices with their start and end apart: 8 -> 8, of which waited for: 3 -> 4; matrix products, arithmetic and copies ran while one was open for 0% -> 0% of each run, Pallas kernels for 23% -> 18%
where the time goes in v7:
time: 35.3 us; the launch traced here: 35.1 us
  Pallas kernels  12.8 us (36%)
  starting transfers between devices  11.7 us (33%)
  waiting for transfers between devices  9.79 us (28%)
  between operations  0.78 us (2%)
    pallas_call x10, Pallas kernels, run(): pallas(body if after else kernel, outs, many, scratch, in_specs)  12.8 us
    ppermute x2, starting transfers between devices, swap_next(): return lax.ppermute(values, 'mag', pairs)  9.84 us
    ppermute x6, waiting for transfers between devices, swap(): return lax.ppermute(values, 'mag', [(i, i ^ bit) for i in range(devices)])  6.47 us
    ppermute x2, waiting for transfers between devices, swap_next(): return lax.ppermute(values, 'mag', pairs)  3.31 us
    ppermute x6, starting transfers between devices, swap(): return lax.ppermute(values, 'mag', [(i, i ^ bit) for i in range(devices)])  1.89 us
  transfers between devices with their start and end apart: 8, of which 4 were waited for; matrix products, arithmetic and copies ran while one was open for 0% of the time, Pallas kernels for 18%

profile of v7, /device:TPU:0, one launch (start us, length us, event | category | flops | bytes accessed | tf_op | source)
XLA Modules:
  0.0 35.1 jit_solution(6853777108513662649)
XLA Ops:
  0.6 1.1 %shard_map.136 = (f32[8,4,16,128]{3,2,1,0:T(8,128)S(1)}, f32[8,2,16,128]{3,2,1,0:T(8,128)S(1)}, f32[8,2,16,128]{3,2,1,0:T(8,128)S(1)}, s32[8,128]{1,0:T(8,128)S(1)}, f32[64,128]{1,0:T(8,128)S(1)}) custom-call(f32[4,16,128]{2,1,0:T(8,128)} %rho_ref.1, f32[3,4,16,128]{3,2,1,0:T(8,128)} %vel_ref.1, f32[3,4,16,128]{3,2,1,0:T(8,128)} %mag_ref.1, ...), custom_call_target="tpu_custom_call" | custom-call | tf_op jit(solution)/shard_map/pallas_call | solution.py:33
  1.7 0.5 %collective-permute-start = (f32[8,2,16,128]{3,2,1,0:T(8,128)S(1)}, f32[8,2,16,128]{3,2,1,0:T(8,128)S(1)}, u32[]{:S(2)}, u32[]{:S(2)}) collective-permute-start(f32[8,2,16,128]{3,2,1,0:T(8,128)S(1)} %get-tuple-element.28), channel_id=1, source_target_pairs={{0,1},{1,0},{2,3},{3,2},{4,5},{5,4},{6,7},{7,6},{8,9},{9,8},{10,11... | collective-permute-start | bytes 393224 | tf_op jit(solution)/shard_map/ppermute | solution.py:494
  2.2 5.7 %collective-permute-start.1 = (f32[8,2,16,128]{3,2,1,0:T(8,128)S(1)}, f32[8,2,16,128]{3,2,1,0:T(8,128)S(1)}, u32[]{:S(2)}, u32[]{:S(2)}) collective-permute-start(f32[8,2,16,128]{3,2,1,0:T(8,128)S(1)} %get-tuple-element.29), channel_id=1, source_target_pairs={{0,15},{1,2},{2,1},{3,4},{4,3},{5,6},{6,5},{7,8},{8,7},{9,10},{10,... | collective-permute-start | bytes 393224 | tf_op jit(solution)/shard_map/ppermute | solution.py:500
  7.9 1.1 %shard_map.137.refs_0_.side_ref = f32[8,4,16,128]{3,2,1,0:T(8,128)S(1)} custom-call(f32[8,4,16,128]{3,2,1,0:T(8,128)S(1)} %get-tuple-element.27.own_ref.refs_1_), custom_call_target="tpu_custom_call" | custom-call | tf_op jit(solution)/shard_map/pallas_call | solution.py:33
  9.0 0.0 collective-permute-done.refs_4_.from_a
  9.0 1.6 %collective-permute-done.1.refs_5_.from_b = f32[8,2,16,128]{3,2,1,0:T(8,128)S(1)} collective-permute-done((f32[8,2,16,128]{3,2,1,0:T(8,128)S(1)}, f32[8,2,16,128]{3,2,1,0:T(8,128)S(1)}, u32[]{:S(2)}, u32[]{:S(2)}) %collective-permute-start.1) | collective-permute-done | bytes 131104 | tf_op jit(solution)/shard_map/ppermute | solution.py:500
  10.5 0.3 shard_map.138.load_ref
  10.9 0.8 %collective-permute-start.4 = (f32[72,128]{1,0:T(8,128)S(1)}, f32[72,128]{1,0:T(8,128)S(1)}, u32[]{:S(2)}, u32[]{:S(2)}) collective-permute-start(f32[72,128]{1,0:T(8,128)S(1)} %shard_map.138.load_ref), channel_id=1, source_target_pairs={{0,8},{1,9},{2,10},{3,11},{4,12},{5,13},{6,14},{7,15},{8,0},{9,1},... | collective-permute-start | bytes 110600 | tf_op jit(solution)/shard_map/ppermute | solution.py:494
  11.7 0.0 copy-start.2
  11.7 0.6 %shard_map.139 = (f32[8,4,16,128]{3,2,1,0:T(8,128)S(1)}, f32[8,4,16,128]{3,2,1,0:T(8,128)S(1)}, f32[8,2,16,128]{3,2,1,0:T(8,128)S(1)}, f32[8,2,16,128]{3,2,1,0:T(8,128)S(1)}, f32[72,128]{1,0:T(8,128)S(1)}) custom-call(f32[8,4,16,128]{3,2,1,0:T(8,128)S(1)} %get-tuple-element.27.own_ref.refs_1_, f32[8,2,16,128]{3,2,1,0:T(8,128)S(1)} %collective-permute-done.refs_4_.from_a, ...), custom_call_target="tpu_custom_call" | custom-call | tf_op jit(solution)/shard_map/pallas_call | solution.py:33
  12.3 0.0 copy-start
  12.3 0.0 copy-start.1
  12.3 3.5 %collective-permute-done.4 = f32[72,128]{1,0:T(8,128)S(1)} collective-permute-done((f32[72,128]{1,0:T(8,128)S(1)}, f32[72,128]{1,0:T(8,128)S(1)}, u32[]{:S(2)}, u32[]{:S(2)}) %collective-permute-start.4) | collective-permute-done | bytes 36896 | tf_op jit(solution)/shard_map/ppermute | solution.py:494
  15.8 0.0 collective-permute-start.5
  15.8 0.0 copy-done.2
  15.8 0.0 copy-done
  15.8 0.0 copy-done.1
  15.8 1.3 %shard_map.142 = (f32[1024,256]{1,0:T(8,128)S(1)}, f32[144,128]{1,0:T(8,128)S(1)}) custom-call(f32[144,128]{1,0:T(8,128)S(1)} %constant_dynamic-update-slice_fusion.refs_0_.refs_4_, s32[128,128]{1,0:T(8,128)S(1)} %bitcast.5, s32[128,128]{1,0:T(8,128)S(1)} %bitcast.9, s32[128,128]{1,0:T(8,128)S(1)} %bitcast.13, ...), custom_call_target="tpu_custom_call" | custom-call | tf_op jit(solution)/shard_map/pallas_call | solution.py:33
  17.1 3.0 %collective-permute-done.5.refs_1_ = f32[144,128]{1,0:T(8,128)S(1)} collective-permute-done((f32[144,128]{1,0:T(8,128)S(1)}, f32[144,128]{1,0:T(8,128)S(1)}, u32[]{:S(2)}, u32[]{:S(2)}) %collective-permute-start.5) | collective-permute-done | bytes 73760 | tf_op jit(solution)/shard_map/ppermute | solution.py:494
  20.1 0.0 collective-permute-start.6
  20.2 0.1 collective-permute-start.2
  20.2 4.2 %collective-permute-start.3 = (f32[8,2,16,128]{3,2,1,0:T(8,128)S(1)}, f32[8,2,16,128]{3,2,1,0:T(8,128)S(1)}, u32[]{:S(2)}, u32[]{:S(2)}) collective-permute-start(f32[8,2,16,128]{3,2,1,0:T(8,128)S(1)} %get-tuple-element.34), channel_id=1, source_target_pairs={{0,15},{1,2},{2,1},{3,4},{4,3},{5,6},{6,5},{7,8},{8,7},{9,10},{10,... | collective-permute-start | bytes 393224 | tf_op jit(solution)/shard_map/ppermute | solution.py:500
  24.4 1.3 %shard_map.143 = (f32[1024,256]{1,0:T(8,128)S(1)}, f32[288,128]{1,0:T(8,128)S(1)}) custom-call(f32[1024,256]{1,0:T(8,128)S(1)} %get-tuple-element.42.refs_0_, f32[144,128]{1,0:T(8,128)S(1)} %collective-permute-done.5.refs_1_, s32[128,128]{1,0:T(8,128)S(1)} %bitcast.6, s32[128,128]{1,0:T(8,128)S(1)} %bitcast.10, s32[128,128]{1,0:T(8,128)S(1)} %bitcast.14, ...), custom_call_target="tpu_custom_call" | custom-call | tf_op jit(solution)/shard_map/pallas_call | solution.py:33
  25.7 0.0 collective-permute-done.2.from_a
  25.7 1.8 %collective-permute-done.3.from_b = f32[8,2,16,128]{3,2,1,0:T(8,128)S(1)} collective-permute-done((f32[8,2,16,128]{3,2,1,0:T(8,128)S(1)}, f32[8,2,16,128]{3,2,1,0:T(8,128)S(1)}, u32[]{:S(2)}, u32[]{:S(2)}) %collective-permute-start.3) | collective-permute-done | bytes 131104 | tf_op jit(solution)/shard_map/ppermute | solution.py:500
  27.5 0.0 collective-permute-done.6.refs_3_
  27.6 2.4 %shard_map.144.refs_1_ = f32[1536,128]{1,0:T(8,128)S(1)} custom-call(f32[8,8,16,128]{3,2,1,0:T(8,128)S(1)} %shard_map.140.pad_ref.refs_0_, f32[1024,256]{1,0:T(8,128)S(1)} %get-tuple-element.44.refs_1_, f32[288,128]{1,0:T(8,128)S(1)} %get-tuple-element.45.refs_2_, f32[288,128]{1,0:T(8,128)S(1)} %collective-permute-done.6.refs_3_, s32[128,128]{1,0:T(8,128)S(1)} %bitcast.7, ...), custom_call_target="tpu_custom_call" | custom-call | tf_op jit(solution)/shard_map/pallas_call | solution.py:33
  29.9 0.5 %collective-permute-start.7 = (f32[1536,128]{1,0:T(8,128)S(1)}, f32[1536,128]{1,0:T(8,128)S(1)}, u32[]{:S(2)}, u32[]{:S(2)}) collective-permute-start(f32[1536,128]{1,0:T(8,128)S(1)} %shard_map.144.refs_1_), channel_id=1, source_target_pairs={{0,1},{1,0},{2,3},{3,2},{4,5},{5,4},{6,7},{7,6},{8,9},{9,8},{10,11... | collective-permute-start | bytes 2359304 | tf_op jit(solution)/shard_map/ppermute | solution.py:494
  30.4 2.1 %shard_map.141 = (f32[4,16,128]{2,1,0:T(8,128)}, f32[3,4,16,128]{3,2,1,0:T(8,128)}, f32[3,4,16,128]{3,2,1,0:T(8,128)}, f32[4,16,128]{2,1,0:T(8,128)}, f32[8,128]{1,0:T(8,128)S(1)}) custom-call(f32[8,8,16,128]{3,2,1,0:T(8,128)S(1)} %shard_map.140.pad_ref.refs_0_, f32[8,4,16,128]{3,2,1,0:T(8,128)S(1)} %get-tuple-element.35.half_ref), custom_call_target="tpu_custom_call" | custom-call | tf_op jit(solution)/shard_map/pallas_call | solution.py:33
  32.6 0.0 collective-permute-done.7.refs_2_
  32.6 2.6 %shard_map.145 = (f32[4,2048]{1,0:T(4,128)}, f32[8,128]{1,0:T(8,128)}) custom-call(f32[8,128]{1,0:T(8,128)S(1)} %get-tuple-element.40.refs_0_, f32[1536,128]{1,0:T(8,128)S(1)} %shard_map.144.refs_1_, f32[1536,128]{1,0:T(8,128)S(1)} %collective-permute-done.7.refs_2_, s32[128,128]{1,0:T(8,128)S(1)} %bitcast.8, s32[128,128]{1,0:T(8,128)S(1)} %bitcast.12, ...), custom_call_target="tpu_custom_call" | custom-call | tf_op jit(solution)/shard_map/pallas_call | solution.py:33
  (5 shorter events, 0.1 us)
Async XLA Ops:
  1.7 7.3 %collective-permute-start = (f32[8,2,16,128]{3,2,1,0:T(8,128)S(1)}, f32[8,2,16,128]{3,2,1,0:T(8,128)S(1)}, u32[]{:S(2)}, u32[]{:S(2)}) collective-permute-start(f32[8,2,16,128]{3,2,1,0:T(8,128)S(1)} %get-tuple-element.28), channel_id=1, source_target_pairs={{0,1},{1,0},{2,3},{3,2},{4,5},{5,4},{6,7},{7,6},{8,9},{9,8},{10,11... | collective-permute-start | bytes 393224 | tf_op jit(solution)/shard_map/ppermute | solution.py:494
  2.2 8.3 %collective-permute-start.1 = (f32[8,2,16,128]{3,2,1,0:T(8,128)S(1)}, f32[8,2,16,128]{3,2,1,0:T(8,128)S(1)}, u32[]{:S(2)}, u32[]{:S(2)}) collective-permute-start(f32[8,2,16,128]{3,2,1,0:T(8,128)S(1)} %get-tuple-element.29), channel_id=1, source_target_pairs={{0,15},{1,2},{2,1},{3,4},{4,3},{5,6},{6,5},{7,8},{8,7},{9,10},{10,... | collective-permute-start | bytes 393224 | tf_op jit(solution)/shard_map/ppermute | solution.py:500
  10.9 4.9 %collective-permute-start.4 = (f32[72,128]{1,0:T(8,128)S(1)}, f32[72,128]{1,0:T(8,128)S(1)}, u32[]{:S(2)}, u32[]{:S(2)}) collective-permute-start(f32[72,128]{1,0:T(8,128)S(1)} %shard_map.138.load_ref), channel_id=1, source_target_pairs={{0,8},{1,9},{2,10},{3,11},{4,12},{5,13},{6,14},{7,15},{8,0},{9,1},... | collective-permute-start | bytes 110600 | tf_op jit(solution)/shard_map/ppermute | solution.py:494
  11.7 4.1 %copy-start.2 = (s32[16384]{0:T(1024)S(1)}, s32[16384]{0:T(1024)}, u32[]{:S(2)}) copy-start(s32[16384]{0:T(1024)} %param.17) | copy-start | bytes 196612
  12.3 3.5 %copy-start = (s32[16384,1]{0,1:T(1,128)S(1)}, s32[16384,1]{0,1:T(1,128)}, u32[]{:S(2)}) copy-start(s32[16384,1]{0,1:T(1,128)} %param.15) | copy-start | bytes 196612
  12.3 3.5 %copy-start.1 = (s32[16384]{0:T(1024)S(1)}, s32[16384]{0:T(1024)}, u32[]{:S(2)}) copy-start(s32[16384]{0:T(1024)} %param.16) | copy-start | bytes 196612
  15.8 4.4 %collective-permute-start.5 = (f32[144,128]{1,0:T(8,128)S(1)}, f32[144,128]{1,0:T(8,128)S(1)}, u32[]{:S(2)}, u32[]{:S(2)}) collective-permute-start(f32[144,128]{1,0:T(8,128)S(1)} %constant_dynamic-update-slice_fusion.refs_0_.refs_4_), channel_id=1, source_target_pairs={{0,4},{1,5},{2,6},{3,7},{4,0},{5,1},{6,2},{7,3},{8,12},{9,13},{10,... | collective-permute-start | bytes 221192 | tf_op jit(solution)/shard_map/ppermute | solution.py:494
  20.1 7.4 %collective-permute-start.6 = (f32[288,128]{1,0:T(8,128)S(1)}, f32[288,128]{1,0:T(8,128)S(1)}, u32[]{:S(2)}, u32[]{:S(2)}) collective-permute-start(f32[288,128]{1,0:T(8,128)S(1)} %constant_dynamic-update-slice_fusion.2.refs_5_), channel_id=1, source_target_pairs={{0,2},{1,3},{2,0},{3,1},{4,6},{5,7},{6,4},{7,5},{8,10},{9,11},{10,... | collective-permute-start | bytes 442376 | tf_op jit(solution)/shard_map/ppermute | solution.py:494
  20.2 5.6 %collective-permute-start.2 = (f32[8,2,16,128]{3,2,1,0:T(8,128)S(1)}, f32[8,2,16,128]{3,2,1,0:T(8,128)S(1)}, u32[]{:S(2)}, u32[]{:S(2)}) collective-permute-start(f32[8,2,16,128]{3,2,1,0:T(8,128)S(1)} %get-tuple-element.33), channel_id=1, source_target_pairs={{0,1},{1,0},{2,3},{3,2},{4,5},{5,4},{6,7},{7,6},{8,9},{9,8},{10,11... | collective-permute-start | bytes 393224 | tf_op jit(solution)/shard_map/ppermute | solution.py:494
  20.2 7.3 %collective-permute-start.3 = (f32[8,2,16,128]{3,2,1,0:T(8,128)S(1)}, f32[8,2,16,128]{3,2,1,0:T(8,128)S(1)}, u32[]{:S(2)}, u32[]{:S(2)}) collective-permute-start(f32[8,2,16,128]{3,2,1,0:T(8,128)S(1)} %get-tuple-element.34), channel_id=1, source_target_pairs={{0,15},{1,2},{2,1},{3,4},{4,3},{5,6},{6,5},{7,8},{8,7},{9,10},{10,... | collective-permute-start | bytes 393224 | tf_op jit(solution)/shard_map/ppermute | solution.py:500
  29.9 2.6 %collective-permute-start.7 = (f32[1536,128]{1,0:T(8,128)S(1)}, f32[1536,128]{1,0:T(8,128)S(1)}, u32[]{:S(2)}, u32[]{:S(2)}) collective-permute-start(f32[1536,128]{1,0:T(8,128)S(1)} %shard_map.144.refs_1_), channel_id=1, source_target_pairs={{0,1},{1,0},{2,3},{3,2},{4,5},{5,4},{6,7},{7,6},{8,9},{9,8},{10,11... | collective-permute-start | bytes 2359304 | tf_op jit(solution)/shard_map/ppermute | solution.py:494

commit v8 on v4

--- a/solution.py
+++ b/solution.py
@@ -509,9 +509,8 @@
 
 
 def swap_next(values):
-    pairs = []
-    for i in range(1, lax.axis_size("mag") - 1, 2):
-        pairs += [(i, i + 1), (i + 1, i)]
+    devices = lax.axis_size("mag")
+    pairs = [(i, (i + (1 if i % 2 else -1)) % devices) for i in range(devices)]
     return lax.ppermute(values, "mag", pairs)
 
 

time: 34.9 us -> 32.8 us (0.940)
  starting transfers between devices: 13.5 us -> 12.4 us
  waiting for transfers between devices: 6.04 us -> 5.05 us
    ppermute x6, starting transfers between devices: 12.2 us -> 3.58 us  [swap(): return lax.ppermute(values, 'mag', [(i, i ^ bit) for i in range(devices)])]
    ppermute x2, starting transfers between devices: 1.33 us -> 8.8 us  [swap_next(): return lax.ppermute(values, 'mag', pairs)]
    ppermute x6, waiting for transfers between devices: 6.04 us -> 4.54 us  [swap(): return lax.ppermute(values, 'mag', [(i, i ^ bit) for i in range(devices)])]
    ppermute x2, waiting for transfers between devices: 0.01 us -> 0.51 us  [swap_next(): return lax.ppermute(values, 'mag', pairs)]
  transfers between devices with their start and end apart: 8 -> 8, of which waited for: 3 -> 5; matrix products, arithmetic and copies ran while one was open for 0% -> 0% of each run, Pallas kernels for 23% -> 25%
where the time goes in v8:
time: 32.8 us; the launch traced here: 32.6 us
  Pallas kernels  14.4 us (44%)
  starting transfers between devices  12.4 us (38%)
  waiting for transfers between devices  5.05 us (15%)
  between operations  0.74 us (2%)
    pallas_call x9, Pallas kernels, run(): pallas(body if after else kernel, outs, many, scratch, in_specs)  14.4 us
    ppermute x2, starting transfers between devices, swap_next(): return lax.ppermute(values, 'mag', pairs)  8.8 us
    ppermute x6, waiting for transfers between devices, swap(): return lax.ppermute(values, 'mag', [(i, i ^ bit) for i in range(devices)])  4.54 us
    ppermute x6, starting transfers between devices, swap(): return lax.ppermute(values, 'mag', [(i, i ^ bit) for i in range(devices)])  3.58 us
  transfers between devices with their start and end apart: 8, of which 5 were waited for; matrix products, arithmetic and copies ran while one was open for 0% of the time, Pallas kernels for 25%

profile of v8, /device:TPU:0, one launch (start us, length us, event | category | flops | bytes accessed | tf_op | source)
XLA Modules:
  0.0 32.6 jit_solution(7807665364955727090)
XLA Ops:
  0.6 1.1 %shard_map.136 = (f32[8,4,16,128]{3,2,1,0:T(8,128)S(1)}, f32[2,2,16,128]{3,2,1,0:T(8,128)S(1)}, s32[8,128]{1,0:T(8,128)S(1)}, f32[64,128]{1,0:T(8,128)S(1)}) custom-call(f32[4,16,128]{2,1,0:T(8,128)} %rho_ref.1, f32[3,4,16,128]{3,2,1,0:T(8,128)} %vel_ref.1, f32[3,4,16,128]{3,2,1,0:T(8,128)} %mag_ref.1, f32[4,16,128]{2,1,0:T(8,128)} %prs_ref.1, ...), custom_call_target="tpu_custom_call" | custom-call | tf_op jit(solution)/shard_map/pallas_call | solution.py:33
  1.7 5.5 %collective-permute-start.1 = (f32[2,2,16,128]{3,2,1,0:T(8,128)S(1)}, f32[2,2,16,128]{3,2,1,0:T(8,128)S(1)}, u32[]{:S(2)}, u32[]{:S(2)}) collective-permute-start(f32[2,2,16,128]{3,2,1,0:T(8,128)S(1)} %get-tuple-element.28), channel_id=1, source_target_pairs={{0,15},{1,2},{2,1},{3,4},{4,3},{5,6},{6,5},{7,8},{8,7},{9,10},{10,... | collective-permute-start | bytes 98312 | tf_op jit(solution)/shard_map/ppermute | solution.py:514
  7.3 0.0 collective-permute-start
  7.3 1.1 %shard_map.137.refs_0_.own_side_ref = f32[8,4,16,128]{3,2,1,0:T(8,128)S(1)} custom-call(f32[8,4,16,128]{3,2,1,0:T(8,128)S(1)} %get-tuple-element.25.own_ref.refs_1_), custom_call_target="tpu_custom_call" | custom-call | tf_op jit(solution)/shard_map/pallas_call | solution.py:33
  8.3 0.5 %collective-permute-done.1.refs_5_ = f32[2,2,16,128]{3,2,1,0:T(8,128)S(1)} collective-permute-done((f32[2,2,16,128]{3,2,1,0:T(8,128)S(1)}, f32[2,2,16,128]{3,2,1,0:T(8,128)S(1)}, u32[]{:S(2)}, u32[]{:S(2)}) %collective-permute-start.1) | collective-permute-done | bytes 32800 | tf_op jit(solution)/shard_map/ppermute | solution.py:514
  8.9 0.0 collective-permute-done.refs_4_
  8.9 0.0 copy-start.2
  8.9 0.3 shard_map.138
  9.2 0.0 copy-start
  9.2 0.0 copy-start.1
  9.2 1.3 %collective-permute-start.4 = (f32[72,128]{1,0:T(8,128)S(1)}, f32[72,128]{1,0:T(8,128)S(1)}, u32[]{:S(2)}, u32[]{:S(2)}) collective-permute-start(f32[72,128]{1,0:T(8,128)S(1)} %get-tuple-element.37), channel_id=1, source_target_pairs={{0,8},{1,9},{2,10},{3,11},{4,12},{5,13},{6,14},{7,15},{8,0},{9,1},... | collective-permute-start | bytes 110600 | tf_op jit(solution)/shard_map/ppermute | solution.py:508
  10.5 3.3 %collective-permute-start.3 = (f32[8,4,16,128]{3,2,1,0:T(8,128)S(1)}, f32[8,4,16,128]{3,2,1,0:T(8,128)S(1)}, u32[]{:S(2)}, u32[]{:S(2)}) collective-permute-start(f32[8,4,16,128]{3,2,1,0:T(8,128)S(1)} %get-tuple-element.29.own_ref), channel_id=1, source_target_pairs={{0,15},{1,2},{2,1},{3,4},{4,3},{5,6},{6,5},{7,8},{8,7},{9,10},{10,... | collective-permute-start | bytes 786440 | tf_op jit(solution)/shard_map/ppermute | solution.py:514
  13.8 0.0 collective-permute-start.2
  13.8 0.4 %collective-permute-done.4 = f32[72,128]{1,0:T(8,128)S(1)} collective-permute-done((f32[72,128]{1,0:T(8,128)S(1)}, f32[72,128]{1,0:T(8,128)S(1)}, u32[]{:S(2)}, u32[]{:S(2)}) %collective-permute-start.4) | collective-permute-done | bytes 36896 | tf_op jit(solution)/shard_map/ppermute | solution.py:508
  14.2 0.2 collective-permute-start.5
  14.3 0.0 copy-done.2
  14.3 0.0 copy-done
  14.4 0.0 copy-done.1
  14.4 1.3 %shard_map.141 = (f32[1024,256]{1,0:T(8,128)S(1)}, f32[144,128]{1,0:T(8,128)S(1)}) custom-call(f32[144,128]{1,0:T(8,128)S(1)} %constant_dynamic-update-slice_fusion.refs_0_.refs_4_, s32[128,128]{1,0:T(8,128)S(1)} %bitcast.5, s32[128,128]{1,0:T(8,128)S(1)} %bitcast.9, s32[128,128]{1,0:T(8,128)S(1)} %bitcast.13, ...), custom_call_target="tpu_custom_call" | custom-call | tf_op jit(solution)/shard_map/pallas_call | solution.py:33
  15.7 3.4 %collective-permute-done.5.refs_1_ = f32[144,128]{1,0:T(8,128)S(1)} collective-permute-done((f32[144,128]{1,0:T(8,128)S(1)}, f32[144,128]{1,0:T(8,128)S(1)}, u32[]{:S(2)}, u32[]{:S(2)}) %collective-permute-start.5) | collective-permute-done | bytes 73760 | tf_op jit(solution)/shard_map/ppermute | solution.py:508
  19.1 2.0 %collective-permute-start.6 = (f32[288,128]{1,0:T(8,128)S(1)}, f32[288,128]{1,0:T(8,128)S(1)}, u32[]{:S(2)}, u32[]{:S(2)}) collective-permute-start(f32[288,128]{1,0:T(8,128)S(1)} %constant_dynamic-update-slice_fusion.2.refs_5_), channel_id=1, source_target_pairs={{0,2},{1,3},{2,0},{3,1},{4,6},{5,7},{6,4},{7,5},{8,10},{9,11},{10,... | collective-permute-start | bytes 442376 | tf_op jit(solution)/shard_map/ppermute | solution.py:508
  21.1 1.3 %shard_map.142 = (f32[1024,256]{1,0:T(8,128)S(1)}, f32[288,128]{1,0:T(8,128)S(1)}) custom-call(f32[1024,256]{1,0:T(8,128)S(1)} %get-tuple-element.38.refs_0_, f32[144,128]{1,0:T(8,128)S(1)} %collective-permute-done.5.refs_1_, s32[128,128]{1,0:T(8,128)S(1)} %bitcast.6, s32[128,128]{1,0:T(8,128)S(1)} %bitcast.10, s32[128,128]{1,0:T(8,128)S(1)} %bitcast.14, ...), custom_call_target="tpu_custom_call" | custom-call | tf_op jit(solution)/shard_map/pallas_call | solution.py:33
  22.5 0.0 collective-permute-done.3.eight_b
  22.5 0.0 collective-permute-done.2.eight_a
  22.5 2.2 %shard_map.139 = (f32[8,8,16,128]{3,2,1,0:T(8,128)S(1)}, f32[8,4,16,128]{3,2,1,0:T(8,128)S(1)}) custom-call(f32[8,4,16,128]{3,2,1,0:T(8,128)S(1)} %get-tuple-element.29.own_ref, f32[8,4,16,128]{3,2,1,0:T(8,128)S(1)} %collective-permute-done.2.eight_a, f32[8,4,16,128]{3,2,1,0:T(8,128)S(1)} %collective-permute-done.3.eight_b, ...), custom_call_target="tpu_custom_call" | custom-call | tf_op jit(solution)/shard_map/pallas_call | solution.py:33
  24.7 0.6 %collective-permute-done.6.refs_3_ = f32[288,128]{1,0:T(8,128)S(1)} collective-permute-done((f32[288,128]{1,0:T(8,128)S(1)}, f32[288,128]{1,0:T(8,128)S(1)}, u32[]{:S(2)}, u32[]{:S(2)}) %collective-permute-start.6) | collective-permute-done | bytes 147488 | tf_op jit(solution)/shard_map/ppermute | solution.py:508
  25.3 2.4 %shard_map.143.refs_1_ = f32[1536,128]{1,0:T(8,128)S(1)} custom-call(f32[8,4,16,128]{3,2,1,0:T(8,128)S(1)} %get-tuple-element.31.half_ref.refs_0_, f32[1024,256]{1,0:T(8,128)S(1)} %get-tuple-element.40.refs_1_, f32[288,128]{1,0:T(8,128)S(1)} %get-tuple-element.41.refs_2_, f32[288,128]{1,0:T(8,128)S(1)} %collective-permute-done.6.refs_3_, ...), custom_call_target="tpu_custom_call" | custom-call | tf_op jit(solution)/shard_map/pallas_call | solution.py:33
  27.7 0.1 collective-permute-start.7
  27.7 2.1 %shard_map.140 = (f32[4,16,128]{2,1,0:T(8,128)}, f32[3,4,16,128]{3,2,1,0:T(8,128)}, f32[3,4,16,128]{3,2,1,0:T(8,128)}, f32[4,16,128]{2,1,0:T(8,128)}, f32[8,128]{1,0:T(8,128)S(1)}) custom-call(f32[8,8,16,128]{3,2,1,0:T(8,128)S(1)} %get-tuple-element.30.next_ref, f32[8,4,16,128]{3,2,1,0:T(8,128)S(1)} %get-tuple-element.31.half_ref.refs_0_), custom_call_target="tpu_custom_call" | custom-call | tf_op jit(solution)/shard_map/pallas_call | solution.py:33
  29.9 0.1 collective-permute-done.7.refs_2_
  30.0 2.6 %shard_map.144 = (f32[4,2048]{1,0:T(4,128)}, f32[8,128]{1,0:T(8,128)}) custom-call(f32[8,128]{1,0:T(8,128)S(1)} %get-tuple-element.36.refs_0_, f32[1536,128]{1,0:T(8,128)S(1)} %shard_map.143.refs_1_, f32[1536,128]{1,0:T(8,128)S(1)} %collective-permute-done.7.refs_2_, s32[128,128]{1,0:T(8,128)S(1)} %bitcast.8, s32[128,128]{1,0:T(8,128)S(1)} %bitcast.12, ...), custom_call_target="tpu_custom_call" | custom-call | tf_op jit(solution)/shard_map/pallas_call | solution.py:33
  (4 shorter events, 0.0 us)
Async XLA Ops:
  1.7 7.1 %collective-permute-start.1 = (f32[2,2,16,128]{3,2,1,0:T(8,128)S(1)}, f32[2,2,16,128]{3,2,1,0:T(8,128)S(1)}, u32[]{:S(2)}, u32[]{:S(2)}) collective-permute-start(f32[2,2,16,128]{3,2,1,0:T(8,128)S(1)} %get-tuple-element.28), channel_id=1, source_target_pairs={{0,15},{1,2},{2,1},{3,4},{4,3},{5,6},{6,5},{7,8},{8,7},{9,10},{10,... | collective-permute-start | bytes 98312 | tf_op jit(solution)/shard_map/ppermute | solution.py:514
  7.3 1.6 %collective-permute-start = (f32[2,2,16,128]{3,2,1,0:T(8,128)S(1)}, f32[2,2,16,128]{3,2,1,0:T(8,128)S(1)}, u32[]{:S(2)}, u32[]{:S(2)}) collective-permute-start(f32[2,2,16,128]{3,2,1,0:T(8,128)S(1)} %get-tuple-element.28), channel_id=1, source_target_pairs={{0,1},{1,0},{2,3},{3,2},{4,5},{5,4},{6,7},{7,6},{8,9},{9,8},{10,11... | collective-permute-start | bytes 98312 | tf_op jit(solution)/shard_map/ppermute | solution.py:508
  8.9 5.5 %copy-start.2 = (s32[16384]{0:T(1024)S(1)}, s32[16384]{0:T(1024)}, u32[]{:S(2)}) copy-start(s32[16384]{0:T(1024)} %param.17) | copy-start | bytes 196612
  9.2 5.2 %copy-start = (s32[16384,1]{0,1:T(1,128)S(1)}, s32[16384,1]{0,1:T(1,128)}, u32[]{:S(2)}) copy-start(s32[16384,1]{0,1:T(1,128)} %param.15) | copy-start | bytes 196612
  9.2 5.2 %copy-start.1 = (s32[16384]{0:T(1024)S(1)}, s32[16384]{0:T(1024)}, u32[]{:S(2)}) copy-start(s32[16384]{0:T(1024)} %param.16) | copy-start | bytes 196612
  9.2 5.0 %collective-permute-start.4 = (f32[72,128]{1,0:T(8,128)S(1)}, f32[72,128]{1,0:T(8,128)S(1)}, u32[]{:S(2)}, u32[]{:S(2)}) collective-permute-start(f32[72,128]{1,0:T(8,128)S(1)} %get-tuple-element.37), channel_id=1, source_target_pairs={{0,8},{1,9},{2,10},{3,11},{4,12},{5,13},{6,14},{7,15},{8,0},{9,1},... | collective-permute-start | bytes 110600 | tf_op jit(solution)/shard_map/ppermute | solution.py:508
  10.5 12.0 %collective-permute-start.3 = (f32[8,4,16,128]{3,2,1,0:T(8,128)S(1)}, f32[8,4,16,128]{3,2,1,0:T(8,128)S(1)}, u32[]{:S(2)}, u32[]{:S(2)}) collective-permute-start(f32[8,4,16,128]{3,2,1,0:T(8,128)S(1)} %get-tuple-element.29.own_ref), channel_id=1, source_target_pairs={{0,15},{1,2},{2,1},{3,4},{4,3},{5,6},{6,5},{7,8},{8,7},{9,10},{10,... | collective-permute-start | bytes 786440 | tf_op jit(solution)/shard_map/ppermute | solution.py:514
  13.8 8.7 %collective-permute-start.2 = (f32[8,4,16,128]{3,2,1,0:T(8,128)S(1)}, f32[8,4,16,128]{3,2,1,0:T(8,128)S(1)}, u32[]{:S(2)}, u32[]{:S(2)}) collective-permute-start(f32[8,4,16,128]{3,2,1,0:T(8,128)S(1)} %get-tuple-element.29.own_ref), channel_id=1, source_target_pairs={{0,1},{1,0},{2,3},{3,2},{4,5},{5,4},{6,7},{7,6},{8,9},{9,8},{10,11... | collective-permute-start | bytes 786440 | tf_op jit(solution)/shard_map/ppermute | solution.py:508
  14.2 4.9 %collective-permute-start.5 = (f32[144,128]{1,0:T(8,128)S(1)}, f32[144,128]{1,0:T(8,128)S(1)}, u32[]{:S(2)}, u32[]{:S(2)}) collective-permute-start(f32[144,128]{1,0:T(8,128)S(1)} %constant_dynamic-update-slice_fusion.refs_0_.refs_4_), channel_id=1, source_target_pairs={{0,4},{1,5},{2,6},{3,7},{4,0},{5,1},{6,2},{7,3},{8,12},{9,13},{10,... | collective-permute-start | bytes 221192 | tf_op jit(solution)/shard_map/ppermute | solution.py:508
  19.1 6.2 %collective-permute-start.6 = (f32[288,128]{1,0:T(8,128)S(1)}, f32[288,128]{1,0:T(8,128)S(1)}, u32[]{:S(2)}, u32[]{:S(2)}) collective-permute-start(f32[288,128]{1,0:T(8,128)S(1)} %constant_dynamic-update-slice_fusion.2.refs_5_), channel_id=1, source_target_pairs={{0,2},{1,3},{2,0},{3,1},{4,6},{5,7},{6,4},{7,5},{8,10},{9,11},{10,... | collective-permute-start | bytes 442376 | tf_op jit(solution)/shard_map/ppermute | solution.py:508
  27.7 2.4 %collective-permute-start.7 = (f32[1536,128]{1,0:T(8,128)S(1)}, f32[1536,128]{1,0:T(8,128)S(1)}, u32[]{:S(2)}, u32[]{:S(2)}) collective-permute-start(f32[1536,128]{1,0:T(8,128)S(1)} %shard_map.143.refs_1_), channel_id=1, source_target_pairs={{0,1},{1,0},{2,3},{3,2},{4,5},{5,4},{6,7},{7,6},{8,9},{9,8},{10,11... | collective-permute-start | bytes 2359304 | tf_op jit(solution)/shard_map/ppermute | solution.py:508

commit v9 on v8

--- a/solution.py
+++ b/solution.py
@@ -238,12 +238,11 @@
     sweep_planes(next_ref, 2, cx, put, lambda step, q: sideways(q))
 
 
-def pick_current(own_ref, cell_ref, strip_ref, edge_a, edge_b, out_ref, own_out):
+def pick_current(own_ref, cell_ref, strip_ref, edge_a, edge_b, out_ref):
     me = lax.axis_index("mag")
     last = lax.axis_size("mag") - 1
     even = me % 2 == 0
     cx, ny, nz = own_ref.shape[1:]
-    own_out[...] = own_ref[...]
     rows = []
     for x in range(cx):
         bx, by, bz = (own_ref[4 + k, x] for k in range(3))
@@ -361,19 +360,20 @@
     return jnp.bitwise_xor(me, mask)
 
 
-def scatter_new(first, blocks, points, lat, strips):
+def scatter_new(first, blocks, held, base, points, lat, strips):
     def kernel(*refs):
         *total_in, load_ref, owner_ref, row_ref, lon_ref, out_ref = refs
         me = lax.axis_index("mag")
         devices = lax.axis_size("mag")
         count = out_ref.shape[0]
         rows = min(count, 1024)
-        stride = load_ref.shape[0] // blocks
+        stride = load_ref.shape[0] // held
 
         def part(j, g, base_ref):
             device = origin(me, devices, first + j)
             at = pl.ds(pl.multiple_of(device * points, points), points)
-            value = load_ref[pl.ds(pl.multiple_of(j * stride, 8), points), :]
+            start = (first - base + j) * stride
+            value = load_ref[pl.ds(pl.multiple_of(start, 8), points), :]
             hi = (owner_ref[at, :] * lat + row_ref[at, :]) * strips + lon_ref[at, :] // LANES
             lo = lon_ref[at, :] % LANES
             new = scatter_block(value, hi - g * rows, lo, rows)
@@ -400,10 +400,17 @@
     return run
 
 
+def join(first_ref, second_ref, own_ref, out_ref, own_out):
+    size = first_ref.shape[0]
+    out_ref[:size, :] = first_ref[...]
+    out_ref[size:, :] = second_ref[...]
+    own_out[...] = own_ref[...]
+
+
 def scatter_last(blocks, points, lat, strips):
     def kernel(total_ref, before_ref, load_ref, owner_ref, row_ref, lon_ref, out_ref, work_ref):
         half = blocks // 2
-        scatter_new(half, half, points, lat, strips)(
+        scatter_new(half, half, half, half, points, lat, strips)(
             total_ref, load_ref, owner_ref, row_ref, lon_ref, work_ref
         )
         count = work_ref.shape[0]
@@ -554,26 +561,29 @@
     row = foot_row.reshape(-1, LANES)
     lon = foot_lon.reshape(-1, LANES)
 
-    load, own = call(
-        pick_current, [shape((points + cells, LANES), F32), slab], after=(own_side,)
-    )(own, cell, strip, edge_a, edge_b)
-    eight_a, eight_b = swap(own, 1), swap_next(own)
+    load = call(pick_current, shape((points + cells, LANES), F32), after=(own_side,))(
+        own, cell, strip, edge_a, edge_b
+    )
 
     grid = shape((count, 2 * LANES), F32)
     total, blocks, done = (), 1, 0
     bit = devices // 2
     while bit > 1:
         arrived = swap(load, bit)
-        if blocks > 1:
-            kernel = handing_on(scatter_new(done, blocks - done, points, lat, strips), 1)
+        if blocks != 2:
+            kernel = handing_on(scatter_new(done, blocks - done, blocks, 0, points, lat, strips), 1)
             total, load = call(kernel, [grid, shape(load.shape, F32)])(
-                *total, new, owner, row, lon, load
+                *total, load, owner, row, lon, load
             )
             total, done = (total,), blocks
         before, new = load, arrived
-        load = jnp.concatenate([load, arrived], axis=0)
         if blocks == 1:
-            new = load
+            load, own_too = call(join, [shape((2 * (points + cells), LANES), F32), slab])(
+                load, arrived, own
+            )
+            eight_a, eight_b = swap(own_too, 1), swap_next(own_too)
+        else:
+            load = jnp.concatenate([load, arrived], axis=0)
         blocks, bit = blocks * 2, bit // 2
 
     following, half = call(

time: 32.8 us -> 35.5 us (1.082)
  waiting for transfers between devices: 5.05 us -> 9.78 us
  starting transfers between devices: 12.4 us -> 10.5 us
    ppermute x6, waiting for transfers between devices: 4.54 us -> 9.28 us  [swap(): return lax.ppermute(values, 'mag', [(i, i ^ bit) for i in range(devices)])]
    ppermute x6, starting transfers between devices: 3.58 us -> 1.43 us  [swap(): return lax.ppermute(values, 'mag', [(i, i ^ bit) for i in range(devices)])]
    pallas_call x9 -> x10, Pallas kernels: 14.4 us -> 14.4 us  [run(): pallas(body if after else kernel, outs, many, scratch, in_specs)]
  transfers between devices with their start and end apart: 8 -> 8, of which waited for: 5 -> 5; matrix products, arithmetic and copies ran while one was open for 0% -> 0% of each run, Pallas kernels for 25% -> 23%
where the time goes in v9:
time: 35.5 us; the launch traced here: 35.4 us
  Pallas kernels  14.4 us (41%)
  starting transfers between devices  10.5 us (30%)
  waiting for transfers between devices  9.78 us (28%)
  between operations  0.74 us (2%)
    pallas_call x10, Pallas kernels, run(): pallas(body if after else kernel, outs, many, scratch, in_specs)  14.4 us
    ppermute x6, waiting for transfers between devices, swap(): return lax.ppermute(values, 'mag', [(i, i ^ bit) for i in range(devices)])  9.28 us
    ppermute x2, starting transfers between devices, swap_next(): return lax.ppermute(values, 'mag', pairs)  9.02 us
    ppermute x6, starting transfers between devices, swap(): return lax.ppermute(values, 'mag', [(i, i ^ bit) for i in range(devices)])  1.43 us
  transfers between devices with their start and end apart: 8, of which 5 were waited for; matrix products, arithmetic and copies ran while one was open for 0% of the time, Pallas kernels for 23%

profile of v9, /device:TPU:0, one launch (start us, length us, event | category | flops | bytes accessed | tf_op | source)
XLA Modules:
  0.0 35.4 jit_solution(13362265949593631775)
XLA Ops:
  0.6 1.1 %shard_map.136 = (f32[8,4,16,128]{3,2,1,0:T(8,128)S(1)}, f32[2,2,16,128]{3,2,1,0:T(8,128)S(1)}, s32[8,128]{1,0:T(8,128)S(1)}, f32[64,128]{1,0:T(8,128)S(1)}) custom-call(f32[4,16,128]{2,1,0:T(8,128)} %rho_ref.1, f32[3,4,16,128]{3,2,1,0:T(8,128)} %vel_ref.1, f32[3,4,16,128]{3,2,1,0:T(8,128)} %mag_ref.1, f32[4,16,128]{2,1,0:T(8,128)} %prs_ref.1, ...), custom_call_target="tpu_custom_call" | custom-call | tf_op jit(solution)/shard_map/pallas_call | solution.py:33
  1.7 0.5 %collective-permute-start = (f32[2,2,16,128]{3,2,1,0:T(8,128)S(1)}, f32[2,2,16,128]{3,2,1,0:T(8,128)S(1)}, u32[]{:S(2)}, u32[]{:S(2)}) collective-permute-start(f32[2,2,16,128]{3,2,1,0:T(8,128)S(1)} %get-tuple-element.28), channel_id=1, source_target_pairs={{0,1},{1,0},{2,3},{3,2},{4,5},{5,4},{6,7},{7,6},{8,9},{9,8},{10,11... | collective-permute-start | bytes 98312 | tf_op jit(solution)/shard_map/ppermute | solution.py:515
  2.3 5.7 %collective-permute-start.1 = (f32[2,2,16,128]{3,2,1,0:T(8,128)S(1)}, f32[2,2,16,128]{3,2,1,0:T(8,128)S(1)}, u32[]{:S(2)}, u32[]{:S(2)}) collective-permute-start(f32[2,2,16,128]{3,2,1,0:T(8,128)S(1)} %get-tuple-element.28), channel_id=1, source_target_pairs={{0,15},{1,2},{2,1},{3,4},{4,3},{5,6},{6,5},{7,8},{8,7},{9,10},{10,... | collective-permute-start | bytes 98312 | tf_op jit(solution)/shard_map/ppermute | solution.py:521
  7.9 1.1 %shard_map.137.refs_0_.own_side_ref = f32[8,4,16,128]{3,2,1,0:T(8,128)S(1)} custom-call(f32[8,4,16,128]{3,2,1,0:T(8,128)S(1)} %get-tuple-element.25.own_ref.refs_1_), custom_call_target="tpu_custom_call" | custom-call | tf_op jit(solution)/shard_map/pallas_call | solution.py:33
  9.0 0.0 collective-permute-done.refs_4_
  9.0 0.5 %collective-permute-done.1.refs_5_ = f32[2,2,16,128]{3,2,1,0:T(8,128)S(1)} collective-permute-done((f32[2,2,16,128]{3,2,1,0:T(8,128)S(1)}, f32[2,2,16,128]{3,2,1,0:T(8,128)S(1)}, u32[]{:S(2)}, u32[]{:S(2)}) %collective-permute-start.1) | collective-permute-done | bytes 32800 | tf_op jit(solution)/shard_map/ppermute | solution.py:521
  9.5 0.0 copy-start
  9.5 0.0 copy-start.1
  9.5 0.0 copy-start.2
  9.5 0.3 shard_map.138.refs_0_.refs_4_
  9.8 0.8 %collective-permute-start.2 = (f32[72,128]{1,0:T(8,128)S(1)}, f32[72,128]{1,0:T(8,128)S(1)}, u32[]{:S(2)}, u32[]{:S(2)}) collective-permute-start(f32[72,128]{1,0:T(8,128)S(1)} %shard_map.138.refs_0_.refs_4_), channel_id=1, source_target_pairs={{0,8},{1,9},{2,10},{3,11},{4,12},{5,13},{6,14},{7,15},{8,0},{9,1},... | collective-permute-start | bytes 110600 | tf_op jit(solution)/shard_map/ppermute | solution.py:515
  10.6 0.0 copy-done
  10.6 0.0 copy-done.1
  10.6 0.0 copy-done.2
  10.6 0.8 %shard_map.139 = (f32[1024,256]{1,0:T(8,128)S(1)}, f32[72,128]{1,0:T(8,128)S(1)}) custom-call(f32[72,128]{1,0:T(8,128)S(1)} %shard_map.138.refs_0_.refs_4_, s32[128,128]{1,0:T(8,128)S(1)} %bitcast.5, s32[128,128]{1,0:T(8,128)S(1)} %bitcast.9, s32[128,128]{1,0:T(8,128)S(1)} %bitcast.13, f32[72,128]{1,0:T(8,128)S(1)} %shard_map.138.refs_0_.refs_4_), custom_call_target="tpu_custom_call" | custom-call | tf_op jit(solution)/shard_map/pallas_call | solution.py:33
  11.4 3.4 %collective-permute-done.2.second_ref = f32[72,128]{1,0:T(8,128)S(1)} collective-permute-done((f32[72,128]{1,0:T(8,128)S(1)}, f32[72,128]{1,0:T(8,128)S(1)}, u32[]{:S(2)}, u32[]{:S(2)}) %collective-permute-start.2) | collective-permute-done | bytes 36896 | tf_op jit(solution)/shard_map/ppermute | solution.py:515
  14.8 0.1 collective-permute-start.3
  14.9 3.4 %collective-permute-start.4 = (f32[8,4,16,128]{3,2,1,0:T(8,128)S(1)}, f32[8,4,16,128]{3,2,1,0:T(8,128)S(1)}, u32[]{:S(2)}, u32[]{:S(2)}) collective-permute-start(f32[8,4,16,128]{3,2,1,0:T(8,128)S(1)} %get-tuple-element.30), channel_id=1, source_target_pairs={{0,15},{1,2},{2,1},{3,4},{4,3},{5,6},{6,5},{7,8},{8,7},{9,10},{10,... | collective-permute-start | bytes 786440 | tf_op jit(solution)/shard_map/ppermute | solution.py:521
  18.2 0.0 collective-permute-start.5
  18.2 4.7 %collective-permute-done.5 = f32[144,128]{1,0:T(8,128)S(1)} collective-permute-done((f32[144,128]{1,0:T(8,128)S(1)}, f32[144,128]{1,0:T(8,128)S(1)}, u32[]{:S(2)}, u32[]{:S(2)}) %collective-permute-start.5) | collective-permute-done | bytes 73760 | tf_op jit(solution)/shard_map/ppermute | solution.py:515
  22.9 0.0 collective-permute-start.6
  22.9 1.8 %shard_map.143 = (f32[1024,256]{1,0:T(8,128)S(1)}, f32[288,128]{1,0:T(8,128)S(1)}) custom-call(f32[1024,256]{1,0:T(8,128)S(1)} %get-tuple-element.38.refs_0_, f32[288,128]{1,0:T(8,128)S(1)} %constant_dynamic-update-slice_fusion.refs_1_.refs_5_, s32[128,128]{1,0:T(8,128)S(1)} %bitcast.6, s32[128,128]{1,0:T(8,128)S(1)} %bitcast.10, s32[128,128]{1,0:T(8,128)S(1)} %bitcast.14, ...), custom_call_target="tpu_custom_call" | custom-call | tf_op jit(solution)/shard_map/pallas_call | solution.py:33
  24.8 0.0 collective-permute-done.3.eight_a
  24.8 0.0 collective-permute-done.4.eight_b
  24.8 2.2 %shard_map.141 = (f32[8,8,16,128]{3,2,1,0:T(8,128)S(1)}, f32[8,4,16,128]{3,2,1,0:T(8,128)S(1)}) custom-call(f32[8,4,16,128]{3,2,1,0:T(8,128)S(1)} %get-tuple-element.25.own_ref.refs_1_, f32[8,4,16,128]{3,2,1,0:T(8,128)S(1)} %collective-permute-done.3.eight_a, f32[8,4,16,128]{3,2,1,0:T(8,128)S(1)} %collective-permute-done.4.eight_b, ...), custom_call_target="tpu_custom_call" | custom-call | tf_op jit(solution)/shard_map/pallas_call | solution.py:33
  27.0 1.1 %collective-permute-done.6.refs_3_ = f32[288,128]{1,0:T(8,128)S(1)} collective-permute-done((f32[288,128]{1,0:T(8,128)S(1)}, f32[288,128]{1,0:T(8,128)S(1)}, u32[]{:S(2)}, u32[]{:S(2)}) %collective-permute-start.6) | collective-permute-done | bytes 147488 | tf_op jit(solution)/shard_map/ppermute | solution.py:515
  28.1 2.4 %shard_map.144.refs_1_ = f32[1536,128]{1,0:T(8,128)S(1)} custom-call(f32[8,4,16,128]{3,2,1,0:T(8,128)S(1)} %get-tuple-element.32.half_ref.refs_0_, f32[1024,256]{1,0:T(8,128)S(1)} %get-tuple-element.40.refs_1_, f32[288,128]{1,0:T(8,128)S(1)} %get-tuple-element.41.refs_2_, f32[288,128]{1,0:T(8,128)S(1)} %collective-permute-done.6.refs_3_, ...), custom_call_target="tpu_custom_call" | custom-call | tf_op jit(solution)/shard_map/pallas_call | solution.py:33
  30.5 0.1 collective-permute-start.7
  30.5 2.1 %shard_map.142 = (f32[4,16,128]{2,1,0:T(8,128)}, f32[3,4,16,128]{3,2,1,0:T(8,128)}, f32[3,4,16,128]{3,2,1,0:T(8,128)}, f32[4,16,128]{2,1,0:T(8,128)}, f32[8,128]{1,0:T(8,128)S(1)}) custom-call(f32[8,8,16,128]{3,2,1,0:T(8,128)S(1)} %get-tuple-element.31.next_ref, f32[8,4,16,128]{3,2,1,0:T(8,128)S(1)} %get-tuple-element.32.half_ref.refs_0_), custom_call_target="tpu_custom_call" | custom-call | tf_op jit(solution)/shard_map/pallas_call | solution.py:33
  32.7 0.1 collective-permute-done.7.refs_2_
  32.8 2.6 %shard_map.145 = (f32[4,2048]{1,0:T(4,128)}, f32[8,128]{1,0:T(8,128)}) custom-call(f32[8,128]{1,0:T(8,128)S(1)} %get-tuple-element.37.refs_0_, f32[1536,128]{1,0:T(8,128)S(1)} %shard_map.144.refs_1_, f32[1536,128]{1,0:T(8,128)S(1)} %collective-permute-done.7.refs_2_, s32[128,128]{1,0:T(8,128)S(1)} %bitcast.8, s32[128,128]{1,0:T(8,128)S(1)} %bitcast.12, ...), custom_call_target="tpu_custom_call" | custom-call | tf_op jit(solution)/shard_map/pallas_call | solution.py:33
  (3 shorter events, 0.0 us)
Async XLA Ops:
  1.7 7.3 %collective-permute-start = (f32[2,2,16,128]{3,2,1,0:T(8,128)S(1)}, f32[2,2,16,128]{3,2,1,0:T(8,128)S(1)}, u32[]{:S(2)}, u32[]{:S(2)}) collective-permute-start(f32[2,2,16,128]{3,2,1,0:T(8,128)S(1)} %get-tuple-element.28), channel_id=1, source_target_pairs={{0,1},{1,0},{2,3},{3,2},{4,5},{5,4},{6,7},{7,6},{8,9},{9,8},{10,11... | collective-permute-start | bytes 98312 | tf_op jit(solution)/shard_map/ppermute | solution.py:515
  2.3 7.3 %collective-permute-start.1 = (f32[2,2,16,128]{3,2,1,0:T(8,128)S(1)}, f32[2,2,16,128]{3,2,1,0:T(8,128)S(1)}, u32[]{:S(2)}, u32[]{:S(2)}) collective-permute-start(f32[2,2,16,128]{3,2,1,0:T(8,128)S(1)} %get-tuple-element.28), channel_id=1, source_target_pairs={{0,15},{1,2},{2,1},{3,4},{4,3},{5,6},{6,5},{7,8},{8,7},{9,10},{10,... | collective-permute-start | bytes 98312 | tf_op jit(solution)/shard_map/ppermute | solution.py:521
  9.5 1.1 %copy-start = (s32[16384,1]{0,1:T(1,128)S(1)}, s32[16384,1]{0,1:T(1,128)}, u32[]{:S(2)}) copy-start(s32[16384,1]{0,1:T(1,128)} %param.15) | copy-start | bytes 196612
  9.5 1.1 %copy-start.1 = (s32[16384]{0:T(1024)S(1)}, s32[16384]{0:T(1024)}, u32[]{:S(2)}) copy-start(s32[16384]{0:T(1024)} %param.16) | copy-start | bytes 196612
  9.5 1.1 %copy-start.2 = (s32[16384]{0:T(1024)S(1)}, s32[16384]{0:T(1024)}, u32[]{:S(2)}) copy-start(s32[16384]{0:T(1024)} %param.17) | copy-start | bytes 196612
  9.8 4.9 %collective-permute-start.2 = (f32[72,128]{1,0:T(8,128)S(1)}, f32[72,128]{1,0:T(8,128)S(1)}, u32[]{:S(2)}, u32[]{:S(2)}) collective-permute-start(f32[72,128]{1,0:T(8,128)S(1)} %shard_map.138.refs_0_.refs_4_), channel_id=1, source_target_pairs={{0,8},{1,9},{2,10},{3,11},{4,12},{5,13},{6,14},{7,15},{8,0},{9,1},... | collective-permute-start | bytes 110600 | tf_op jit(solution)/shard_map/ppermute | solution.py:515
  14.8 10.0 %collective-permute-start.3 = (f32[8,4,16,128]{3,2,1,0:T(8,128)S(1)}, f32[8,4,16,128]{3,2,1,0:T(8,128)S(1)}, u32[]{:S(2)}, u32[]{:S(2)}) collective-permute-start(f32[8,4,16,128]{3,2,1,0:T(8,128)S(1)} %get-tuple-element.30), channel_id=1, source_target_pairs={{0,1},{1,0},{2,3},{3,2},{4,5},{5,4},{6,7},{7,6},{8,9},{9,8},{10,11... | collective-permute-start | bytes 786440 | tf_op jit(solution)/shard_map/ppermute | solution.py:515
  14.9 9.9 %collective-permute-start.4 = (f32[8,4,16,128]{3,2,1,0:T(8,128)S(1)}, f32[8,4,16,128]{3,2,1,0:T(8,128)S(1)}, u32[]{:S(2)}, u32[]{:S(2)}) collective-permute-start(f32[8,4,16,128]{3,2,1,0:T(8,128)S(1)} %get-tuple-element.30), channel_id=1, source_target_pairs={{0,15},{1,2},{2,1},{3,4},{4,3},{5,6},{6,5},{7,8},{8,7},{9,10},{10,... | collective-permute-start | bytes 786440 | tf_op jit(solution)/shard_map/ppermute | solution.py:521
  18.2 4.7 %collective-permute-start.5 = (f32[144,128]{1,0:T(8,128)S(1)}, f32[144,128]{1,0:T(8,128)S(1)}, u32[]{:S(2)}, u32[]{:S(2)}) collective-permute-start(f32[144,128]{1,0:T(8,128)S(1)} %get-tuple-element.39), channel_id=1, source_target_pairs={{0,4},{1,5},{2,6},{3,7},{4,0},{5,1},{6,2},{7,3},{8,12},{9,13},{10,... | collective-permute-start | bytes 221192 | tf_op jit(solution)/shard_map/ppermute | solution.py:515
  22.9 5.1 %collective-permute-start.6 = (f32[288,128]{1,0:T(8,128)S(1)}, f32[288,128]{1,0:T(8,128)S(1)}, u32[]{:S(2)}, u32[]{:S(2)}) collective-permute-start(f32[288,128]{1,0:T(8,128)S(1)} %constant_dynamic-update-slice_fusion.refs_1_.refs_5_), channel_id=1, source_target_pairs={{0,2},{1,3},{2,0},{3,1},{4,6},{5,7},{6,4},{7,5},{8,10},{9,11},{10,... | collective-permute-start | bytes 442376 | tf_op jit(solution)/shard_map/ppermute | solution.py:515
  30.5 2.4 %collective-permute-start.7 = (f32[1536,128]{1,0:T(8,128)S(1)}, f32[1536,128]{1,0:T(8,128)S(1)}, u32[]{:S(2)}, u32[]{:S(2)}) collective-permute-start(f32[1536,128]{1,0:T(8,128)S(1)} %shard_map.144.refs_1_), channel_id=1, source_target_pairs={{0,1},{1,0},{2,3},{3,2},{4,5},{5,4},{6,7},{7,6},{8,9},{9,8},{10,11... | collective-permute-start | bytes 2359304 | tf_op jit(solution)/shard_map/ppermute | solution.py:515

commit v10 on v7

--- a/solution.py
+++ b/solution.py
@@ -212,8 +212,9 @@
     split_planes(next_ref, out_a, out_b)
 
 
-def stage_two(pad_ref, half_ref, rho_ref, vel_ref, mag_ref, prs_ref, end_ref):
+def stage_two(next_ref, half_ref, from_a, from_b, rho_ref, vel_ref, mag_ref, prs_ref, end_ref, pad_ref):
     end_ref[...] = half_ref[0, 0, 0:8]
+    pad_planes(next_ref, from_a, from_b, pad_ref)
 
     def put(x, step, q, change):
         final = [half_ref[k, step] + (0.5 * TIME_STEP) * change[k] for k in range(8)]
@@ -386,6 +387,12 @@
     return run
 
 
+def join(first_ref, second_ref, out_ref):
+    size = first_ref.shape[0]
+    out_ref[:size, :] = first_ref[...]
+    out_ref[size:, :] = second_ref[...]
+
+
 def scatter_last(blocks, points, lat, strips):
     def kernel(total_ref, before_ref, load_ref, owner_ref, row_ref, lon_ref, out_ref, work_ref):
         half = blocks // 2
@@ -561,26 +568,28 @@
             )
             total, done = (total,), blocks
         before, new = load, arrived
-        load = jnp.concatenate([after_one if blocks == 1 else load, arrived], axis=0)
         if blocks == 1:
-            new = load
+            new = load = call(
+                join, shape((2 * (points + cells), LANES), F32), after=(next_a, next_b)
+            )(after_one, arrived)
+        else:
+            load = jnp.concatenate([load, arrived], axis=0)
         blocks, bit = blocks * 2, bit // 2
 
-    padded = call(pad_planes, shape((8, cx + 4, ny, nz), F32))(following, next_a, next_b)
+    cell_shape = shape((cx, ny, nz), F32)
+    vector_shape = shape((3, cx, ny, nz), F32)
+    new_density, new_velocity, new_field, new_pressure, end = call(
+        stage_two, [cell_shape, vector_shape, vector_shape, cell_shape, shape((8, LANES), F32)], pad
+    )(following, half, next_a, next_b)
+
     grids = shape((count + count // 2, LANES), F32)
     mine = call(
         scatter_last(blocks, points, lat, strips),
         grids,
         [pltpu.VMEM((count, 2 * LANES), F32)],
-        after=(padded,),
+        after=(end,),
     )(*total, before, new, owner, row, lon)
     theirs = swap(mine, 1)
-
-    cell_shape = shape((cx, ny, nz), F32)
-    vector_shape = shape((3, cx, ny, nz), F32)
-    new_density, new_velocity, new_field, new_pressure, end = call(
-        stage_two, [cell_shape, vector_shape, vector_shape, cell_shape, shape((8, LANES), F32)]
-    )(padded, half)
 
     potential, shell_potential = call(
         solve_and_read(blocks, points, lat, strips),
@@ -590,7 +599,6 @@
             pltpu.VMEM((5, devices * lat, strips, LANES), F32),
             pltpu.VMEM((2, devices * lat + 2, strips, LANES), F32),
         ],
-        after=(end,),
     )(mine, theirs, owner, row, lon)
     return (
         new_density,

time: 35.3 us -> 38.2 us (1.082)
  waiting for transfers between devices: 9.79 us -> 12.7 us
  starting transfers between devices: 11.7 us -> 10.9 us
  local copies, waits for them, and re-layouts: 0.04 us -> 0.81 us
    ppermute x6, waiting for transfers between devices: 6.47 us -> 11.1 us  [swap(): return lax.ppermute(values, 'mag', [(i, i ^ bit) for i in range(devices)])]
    ppermute x2, waiting for transfers between devices: 3.31 us -> 1.55 us  [swap_next(): return lax.ppermute(values, 'mag', pairs)]
    ppermute x6, starting transfers between devices: 1.89 us -> 0.74 us  [swap(): return lax.ppermute(values, 'mag', [(i, i ^ bit) for i in range(devices)])]
    unnamed x8 -> x7, local copies, waits for them, and re-layouts: 0.03 us -> 0.8 us
  transfers between devices with their start and end apart: 8 -> 8, of which waited for: 4 -> 5; matrix products, arithmetic and copies ran while one was open for 0% -> 0% of each run, Pallas kernels for 18% -> 15%
where the time goes in v10:
time: 38.2 us; the launch traced here: 38 us
  Pallas kernels  12.8 us (34%)
  waiting for transfers between devices  12.7 us (33%)
  starting transfers between devices  10.9 us (29%)
  local copies, waits for them, and re-layouts  0.81 us (2%)
  between operations  0.76 us (2%)
    pallas_call x10, Pallas kernels, run(): pallas(body if after else kernel, outs, many, scratch, in_specs)  12.8 us
    ppermute x6, waiting for transfers between devices, swap(): return lax.ppermute(values, 'mag', [(i, i ^ bit) for i in range(devices)])  11.1 us
    ppermute x2, starting transfers between devices, swap_next(): return lax.ppermute(values, 'mag', pairs)  10.2 us
    ppermute x2, waiting for transfers between devices, swap_next(): return lax.ppermute(values, 'mag', pairs)  1.55 us
    unnamed x7, local copies, waits for them, and re-layouts  0.8 us
  transfers between devices with their start and end apart: 8, of which 5 were waited for; matrix products, arithmetic and copies ran while one was open for 0% of the time, Pallas kernels for 15%

profile of v10, /device:TPU:0, one launch (start us, length us, event | category | flops | bytes accessed | tf_op | source)
XLA Modules:
  0.0 38.0 jit_solution(14714378001486439133)
XLA Ops:
  0.6 1.1 %shard_map.136 = (f32[8,4,16,128]{3,2,1,0:T(8,128)S(1)}, f32[8,2,16,128]{3,2,1,0:T(8,128)S(1)}, f32[8,2,16,128]{3,2,1,0:T(8,128)S(1)}, s32[8,128]{1,0:T(8,128)S(1)}, f32[64,128]{1,0:T(8,128)S(1)}) custom-call(f32[4,16,128]{2,1,0:T(8,128)} %rho_ref.1, f32[3,4,16,128]{3,2,1,0:T(8,128)} %vel_ref.1, f32[3,4,16,128]{3,2,1,0:T(8,128)} %mag_ref.1, ...), custom_call_target="tpu_custom_call" | custom-call | tf_op jit(solution)/shard_map/pallas_call | solution.py:33
  1.7 0.5 %collective-permute-start = (f32[8,2,16,128]{3,2,1,0:T(8,128)S(1)}, f32[8,2,16,128]{3,2,1,0:T(8,128)S(1)}, u32[]{:S(2)}, u32[]{:S(2)}) collective-permute-start(f32[8,2,16,128]{3,2,1,0:T(8,128)S(1)} %get-tuple-element.28), channel_id=1, source_target_pairs={{0,1},{1,0},{2,3},{3,2},{4,5},{5,4},{6,7},{7,6},{8,9},{9,8},{10,11... | collective-permute-start | bytes 393224 | tf_op jit(solution)/shard_map/ppermute | solution.py:501
  2.2 5.7 %collective-permute-start.1 = (f32[8,2,16,128]{3,2,1,0:T(8,128)S(1)}, f32[8,2,16,128]{3,2,1,0:T(8,128)S(1)}, u32[]{:S(2)}, u32[]{:S(2)}) collective-permute-start(f32[8,2,16,128]{3,2,1,0:T(8,128)S(1)} %get-tuple-element.29), channel_id=1, source_target_pairs={{0,15},{1,2},{2,1},{3,4},{4,3},{5,6},{6,5},{7,8},{8,7},{9,10},{10,... | collective-permute-start | bytes 393224 | tf_op jit(solution)/shard_map/ppermute | solution.py:507
  7.9 1.1 %shard_map.137.refs_0_.side_ref = f32[8,4,16,128]{3,2,1,0:T(8,128)S(1)} custom-call(f32[8,4,16,128]{3,2,1,0:T(8,128)S(1)} %get-tuple-element.27.own_ref.refs_1_), custom_call_target="tpu_custom_call" | custom-call | tf_op jit(solution)/shard_map/pallas_call | solution.py:33
  9.0 0.0 collective-permute-done.refs_4_.from_a
  9.0 1.6 %collective-permute-done.1.refs_5_.from_b = f32[8,2,16,128]{3,2,1,0:T(8,128)S(1)} collective-permute-done((f32[8,2,16,128]{3,2,1,0:T(8,128)S(1)}, f32[8,2,16,128]{3,2,1,0:T(8,128)S(1)}, u32[]{:S(2)}, u32[]{:S(2)}) %collective-permute-start.1) | collective-permute-done | bytes 131104 | tf_op jit(solution)/shard_map/ppermute | solution.py:507
  10.5 0.3 shard_map.138.load_ref
  10.9 0.6 %shard_map.139 = (f32[8,4,16,128]{3,2,1,0:T(8,128)S(1)}, f32[8,4,16,128]{3,2,1,0:T(8,128)S(1)}, f32[8,2,16,128]{3,2,1,0:T(8,128)S(1)}, f32[8,2,16,128]{3,2,1,0:T(8,128)S(1)}, f32[72,128]{1,0:T(8,128)S(1)}) custom-call(f32[8,4,16,128]{3,2,1,0:T(8,128)S(1)} %get-tuple-element.27.own_ref.refs_1_, f32[8,2,16,128]{3,2,1,0:T(8,128)S(1)} %collective-permute-done.refs_4_.from_a, ...), custom_call_target="tpu_custom_call" | custom-call | tf_op jit(solution)/shard_map/pallas_call | solution.py:33
  11.5 0.1 collective-permute-start.2
  11.6 4.5 %collective-permute-start.3 = (f32[8,2,16,128]{3,2,1,0:T(8,128)S(1)}, f32[8,2,16,128]{3,2,1,0:T(8,128)S(1)}, u32[]{:S(2)}, u32[]{:S(2)}) collective-permute-start(f32[8,2,16,128]{3,2,1,0:T(8,128)S(1)} %get-tuple-element.35), channel_id=1, source_target_pairs={{0,15},{1,2},{2,1},{3,4},{4,3},{5,6},{6,5},{7,8},{8,7},{9,10},{10,... | collective-permute-start | bytes 393224 | tf_op jit(solution)/shard_map/ppermute | solution.py:507
  16.1 0.0 collective-permute-start.4
  16.1 5.0 %collective-permute-done.4.refs_3_ = f32[72,128]{1,0:T(8,128)S(1)} collective-permute-done((f32[72,128]{1,0:T(8,128)S(1)}, f32[72,128]{1,0:T(8,128)S(1)}, u32[]{:S(2)}, u32[]{:S(2)}) %collective-permute-start.4) | collective-permute-done | bytes 36896 | tf_op jit(solution)/shard_map/ppermute | solution.py:501
  21.0 0.0 collective-permute-done.2.from_a.refs_0_
  21.0 0.0 collective-permute-done.3.from_b.refs_1_
  21.0 0.0 copy-start
  21.0 0.0 copy-start.1
  21.1 0.0 copy-start.2
  21.1 0.1 collective-permute-start.5
  21.2 0.7 %copy-done = s32[16384,1]{0,1:T(1,128)S(1)} copy-done((s32[16384,1]{0,1:T(1,128)S(1)}, s32[16384,1]{0,1:T(1,128)}, u32[]{:S(2)}) %copy-start) | copy-done | bytes 65560
  21.9 0.0 copy-done.1
  21.9 0.0 copy-done.2
  21.9 1.3 %shard_map.142 = (f32[1024,256]{1,0:T(8,128)S(1)}, f32[144,128]{1,0:T(8,128)S(1)}) custom-call(f32[144,128]{1,0:T(8,128)S(1)} %shard_map.141.refs_0_.refs_4_, s32[128,128]{1,0:T(8,128)S(1)} %bitcast.5, s32[128,128]{1,0:T(8,128)S(1)} %bitcast.9, s32[128,128]{1,0:T(8,128)S(1)} %bitcast.13, f32[144,128]{1,0:T(8,128)S(1)} %shard_map.141.refs_0_.refs_4_), custom_call_target="tpu_custom_call" | custom-call | tf_op jit(solution)/shard_map/pallas_call | solution.py:33
  23.3 2.2 %collective-permute-done.5.refs_1_ = f32[144,128]{1,0:T(8,128)S(1)} collective-permute-done((f32[144,128]{1,0:T(8,128)S(1)}, f32[144,128]{1,0:T(8,128)S(1)}, u32[]{:S(2)}, u32[]{:S(2)}) %collective-permute-start.5) | collective-permute-done | bytes 73760 | tf_op jit(solution)/shard_map/ppermute | solution.py:501
  25.5 0.0 collective-permute-start.6
  25.5 2.2 %shard_map.140 = (f32[4,16,128]{2,1,0:T(8,128)}, f32[3,4,16,128]{3,2,1,0:T(8,128)}, f32[3,4,16,128]{3,2,1,0:T(8,128)}, f32[4,16,128]{2,1,0:T(8,128)}, f32[8,128]{1,0:T(8,128)S(1)}) custom-call(f32[8,4,16,128]{3,2,1,0:T(8,128)S(1)} %get-tuple-element.32.next_ref, f32[8,4,16,128]{3,2,1,0:T(8,128)S(1)} %get-tuple-element.33.half_ref, ...), custom_call_target="tpu_custom_call" | custom-call | tf_op jit(solution)/shard_map/pallas_call | solution.py:33
  27.7 1.3 %shard_map.143 = (f32[1024,256]{1,0:T(8,128)S(1)}, f32[288,128]{1,0:T(8,128)S(1)}) custom-call(f32[1024,256]{1,0:T(8,128)S(1)} %get-tuple-element.42.refs_0_, f32[144,128]{1,0:T(8,128)S(1)} %collective-permute-done.5.refs_1_, s32[128,128]{1,0:T(8,128)S(1)} %bitcast.6, s32[128,128]{1,0:T(8,128)S(1)} %bitcast.10, s32[128,128]{1,0:T(8,128)S(1)} %bitcast.14, ...), custom_call_target="tpu_custom_call" | custom-call | tf_op jit(solution)/shard_map/pallas_call | solution.py:33
  29.0 1.6 %collective-permute-done.6.refs_3_ = f32[288,128]{1,0:T(8,128)S(1)} collective-permute-done((f32[288,128]{1,0:T(8,128)S(1)}, f32[288,128]{1,0:T(8,128)S(1)}, u32[]{:S(2)}, u32[]{:S(2)}) %collective-permute-start.6) | collective-permute-done | bytes 147488 | tf_op jit(solution)/shard_map/ppermute | solution.py:501
  30.6 2.4 %shard_map.144.mine_ref = f32[1536,128]{1,0:T(8,128)S(1)} custom-call(f32[8,128]{1,0:T(8,128)S(1)} %get-tuple-element.40.refs_0_, f32[1024,256]{1,0:T(8,128)S(1)} %get-tuple-element.44.refs_1_, f32[288,128]{1,0:T(8,128)S(1)} %get-tuple-element.45.refs_2_, f32[288,128]{1,0:T(8,128)S(1)} %collective-permute-done.6.refs_3_, s32[128,128]{1,0:T(8,128)S(1)} %bitcast.7, ...), custom_call_target="tpu_custom_call" | custom-call | tf_op jit(solution)/shard_map/pallas_call | solution.py:33
  33.0 0.1 collective-permute-start.7
  33.1 2.3 %collective-permute-done.7.their_ref = f32[1536,128]{1,0:T(8,128)S(1)} collective-permute-done((f32[1536,128]{1,0:T(8,128)S(1)}, f32[1536,128]{1,0:T(8,128)S(1)}, u32[]{:S(2)}, u32[]{:S(2)}) %collective-permute-start.7) | collective-permute-done | bytes 786464 | tf_op jit(solution)/shard_map/ppermute | solution.py:501
  35.4 2.6 %shard_map.145 = (f32[4,2048]{1,0:T(4,128)}, f32[8,128]{1,0:T(8,128)}) custom-call(f32[1536,128]{1,0:T(8,128)S(1)} %shard_map.144.mine_ref, f32[1536,128]{1,0:T(8,128)S(1)} %collective-permute-done.7.their_ref, s32[128,128]{1,0:T(8,128)S(1)} %bitcast.8, s32[128,128]{1,0:T(8,128)S(1)} %bitcast.12, s32[128,128]{1,0:T(8,128)S(1)} %bitcast.16), custom_call_target="tpu_custom_call" | custom-call | tf_op jit(solution)/shard_map/pallas_call | solution.py:33
  (3 shorter events, 0.0 us)
Async XLA Ops:
  1.7 7.3 %collective-permute-start = (f32[8,2,16,128]{3,2,1,0:T(8,128)S(1)}, f32[8,2,16,128]{3,2,1,0:T(8,128)S(1)}, u32[]{:S(2)}, u32[]{:S(2)}) collective-permute-start(f32[8,2,16,128]{3,2,1,0:T(8,128)S(1)} %get-tuple-element.28), channel_id=1, source_target_pairs={{0,1},{1,0},{2,3},{3,2},{4,5},{5,4},{6,7},{7,6},{8,9},{9,8},{10,11... | collective-permute-start | bytes 393224 | tf_op jit(solution)/shard_map/ppermute | solution.py:501
  2.2 8.3 %collective-permute-start.1 = (f32[8,2,16,128]{3,2,1,0:T(8,128)S(1)}, f32[8,2,16,128]{3,2,1,0:T(8,128)S(1)}, u32[]{:S(2)}, u32[]{:S(2)}) collective-permute-start(f32[8,2,16,128]{3,2,1,0:T(8,128)S(1)} %get-tuple-element.29), channel_id=1, source_target_pairs={{0,15},{1,2},{2,1},{3,4},{4,3},{5,6},{6,5},{7,8},{8,7},{9,10},{10,... | collective-permute-start | bytes 393224 | tf_op jit(solution)/shard_map/ppermute | solution.py:507
  11.5 9.6 %collective-permute-start.2 = (f32[8,2,16,128]{3,2,1,0:T(8,128)S(1)}, f32[8,2,16,128]{3,2,1,0:T(8,128)S(1)}, u32[]{:S(2)}, u32[]{:S(2)}) collective-permute-start(f32[8,2,16,128]{3,2,1,0:T(8,128)S(1)} %get-tuple-element.34), channel_id=1, source_target_pairs={{0,1},{1,0},{2,3},{3,2},{4,5},{5,4},{6,7},{7,6},{8,9},{9,8},{10,11... | collective-permute-start | bytes 393224 | tf_op jit(solution)/shard_map/ppermute | solution.py:501
  11.6 9.5 %collective-permute-start.3 = (f32[8,2,16,128]{3,2,1,0:T(8,128)S(1)}, f32[8,2,16,128]{3,2,1,0:T(8,128)S(1)}, u32[]{:S(2)}, u32[]{:S(2)}) collective-permute-start(f32[8,2,16,128]{3,2,1,0:T(8,128)S(1)} %get-tuple-element.35), channel_id=1, source_target_pairs={{0,15},{1,2},{2,1},{3,4},{4,3},{5,6},{6,5},{7,8},{8,7},{9,10},{10,... | collective-permute-start | bytes 393224 | tf_op jit(solution)/shard_map/ppermute | solution.py:507
  16.1 5.0 %collective-permute-start.4 = (f32[72,128]{1,0:T(8,128)S(1)}, f32[72,128]{1,0:T(8,128)S(1)}, u32[]{:S(2)}, u32[]{:S(2)}) collective-permute-start(f32[72,128]{1,0:T(8,128)S(1)} %shard_map.138.load_ref), channel_id=1, source_target_pairs={{0,8},{1,9},{2,10},{3,11},{4,12},{5,13},{6,14},{7,15},{8,0},{9,1},... | collective-permute-start | bytes 110600 | tf_op jit(solution)/shard_map/ppermute | solution.py:501
  21.0 0.8 %copy-start = (s32[16384,1]{0,1:T(1,128)S(1)}, s32[16384,1]{0,1:T(1,128)}, u32[]{:S(2)}) copy-start(s32[16384,1]{0,1:T(1,128)} %param.15) | copy-start | bytes 196612
  21.0 0.9 %copy-start.1 = (s32[16384]{0:T(1024)S(1)}, s32[16384]{0:T(1024)}, u32[]{:S(2)}) copy-start(s32[16384]{0:T(1024)} %param.16) | copy-start | bytes 196612
  21.1 0.9 %copy-start.2 = (s32[16384]{0:T(1024)S(1)}, s32[16384]{0:T(1024)}, u32[]{:S(2)}) copy-start(s32[16384]{0:T(1024)} %param.17) | copy-start | bytes 196612
  21.1 4.4 %collective-permute-start.5 = (f32[144,128]{1,0:T(8,128)S(1)}, f32[144,128]{1,0:T(8,128)S(1)}, u32[]{:S(2)}, u32[]{:S(2)}) collective-permute-start(f32[144,128]{1,0:T(8,128)S(1)} %shard_map.141.refs_0_.refs_4_), channel_id=1, source_target_pairs={{0,4},{1,5},{2,6},{3,7},{4,0},{5,1},{6,2},{7,3},{8,12},{9,13},{10,... | collective-permute-start | bytes 221192 | tf_op jit(solution)/shard_map/ppermute | solution.py:501
  25.5 5.1 %collective-permute-start.6 = (f32[288,128]{1,0:T(8,128)S(1)}, f32[288,128]{1,0:T(8,128)S(1)}, u32[]{:S(2)}, u32[]{:S(2)}) collective-permute-start(f32[288,128]{1,0:T(8,128)S(1)} %constant_dynamic-update-slice_fusion.refs_5_), channel_id=1, source_target_pairs={{0,2},{1,3},{2,0},{3,1},{4,6},{5,7},{6,4},{7,5},{8,10},{9,11},{10,... | collective-permute-start | bytes 442376 | tf_op jit(solution)/shard_map/ppermute | solution.py:501
  33.0 2.4 %collective-permute-start.7 = (f32[1536,128]{1,0:T(8,128)S(1)}, f32[1536,128]{1,0:T(8,128)S(1)}, u32[]{:S(2)}, u32[]{:S(2)}) collective-permute-start(f32[1536,128]{1,0:T(8,128)S(1)} %shard_map.144.mine_ref), channel_id=1, source_target_pairs={{0,1},{1,0},{2,3},{3,2},{4,5},{5,4},{6,7},{7,6},{8,9},{9,8},{10,11... | collective-permute-start | bytes 2359304 | tf_op jit(solution)/shard_map/ppermute | solution.py:501

commit v11 on v8

--- a/solution.py
+++ b/solution.py
@@ -389,6 +389,24 @@
     return kernel
 
 
+def read_hot(points, lat, strips):
+    def kernel(owner_ref, row_ref, lon_ref, hot_ref):
+        block = min(256, lax.axis_size("mag") * lat * strips)
+        me = lax.axis_index("mag")
+        groups = hot_ref.shape[0] // LANES
+        at = pl.ds(pl.multiple_of(me * points, points), points)
+        owner, row, lon = owner_ref[at, :], row_ref[at, :], lon_ref[at, :]
+        group = ((owner * lat + row) * strips + lon // LANES) // block
+        lo = lon % LANES
+        for p in range(points):
+            for g in range(groups):
+                key = jnp.where(group[p : p + 1] == g, lo[p : p + 1], -1).astype(F32)
+                place = slice(p * LANES, (p + 1) * LANES)
+                hot_ref[g * LANES : (g + 1) * LANES, place] = rows_hot(key, LANES)
+
+    return kernel
+
+
 def handing_on(kernel, count):
     def run(*refs):
         outs = count + 1
@@ -396,6 +414,15 @@
         for source, target in zip(given, refs[-count:]):
             target[...] = source[...]
         kernel(*refs[: -outs - count], refs[-outs])
+
+    return run
+
+
+def and_read_hot(kernel, other):
+    def run(*refs):
+        *given, load_ref, total_out, load_out, hot_out = refs
+        kernel(*given, load_ref, total_out, load_out)
+        other(*given[-3:], hot_out)
 
     return run
 
@@ -420,7 +447,17 @@
 
 def solve_and_read(blocks, points, lat, strips):
     def kernel(
-        mine_ref, their_ref, owner_ref, row_ref, lon_ref, flat_ref, out_ref, s_ref, w_ref, phi_ref
+        mine_ref,
+        their_ref,
+        owner_ref,
+        row_ref,
+        lon_ref,
+        hot_ref,
+        flat_ref,
+        out_ref,
+        s_ref,
+        w_ref,
+        phi_ref,
     ):
         me = lax.axis_index("mag")
         devices = lax.axis_size("mag")
@@ -483,17 +520,9 @@
         both = jnp.concatenate(pieces(table), axis=0)
         at = pl.ds(pl.multiple_of(me * points, points), points)
         owner, row, lon = owner_ref[at, :], row_ref[at, :], lon_ref[at, :]
-        hi = (owner * lat + row) * strips + lon // LANES
-        group, hi, lo = hi // block, hi % block, lon % LANES
+        hi = ((owner * lat + row) * strips + lon // LANES) % block
         index = lax.broadcasted_iota(I32, (block, LANES), 0)
-        columns = []
-        for p in range(points):
-            stack = []
-            for g in range(groups):
-                key = jnp.where(group[p : p + 1] == g, lo[p : p + 1], -1).astype(F32)
-                stack.append(rows_hot(key, LANES))
-            columns.append(jnp.concatenate(stack, axis=0))
-        found = jnp.dot(both, jnp.concatenate(columns, axis=1), preferred_element_type=F32)
+        found = jnp.dot(both, hot_ref[...], preferred_element_type=F32)
         found = found[:block] + found[block:]
         for p in range(points):
             part = found[:, p * LANES : (p + 1) * LANES]
@@ -508,10 +537,10 @@
     return lax.ppermute(values, "mag", [(i, i ^ bit) for i in range(devices)])
 
 
-def swap_next(values):
+def swap_next(values, ring):
     devices = lax.axis_size("mag")
     pairs = [(i, (i + (1 if i % 2 else -1)) % devices) for i in range(devices)]
-    return lax.ppermute(values, "mag", pairs)
+    return lax.ppermute(values, "mag", pairs if ring else pairs[1:-1])
 
 
 def shards(
@@ -547,7 +576,7 @@
             )
         )
     )
-    edge_a, edge_b = swap(edge, 1), swap_next(edge)
+    edge_a, edge_b = swap(edge, 1), swap_next(edge, True)
     own_side = call(stage_own, slab)(own)
 
     owner = foot_owner.reshape(-1, LANES)
@@ -557,18 +586,22 @@
     load, own = call(
         pick_current, [shape((points + cells, LANES), F32), slab], after=(own_side,)
     )(own, cell, strip, edge_a, edge_b)
-    eight_a, eight_b = swap(own, 1), swap_next(own)
+    eight_a, eight_b = swap(own, 1), swap_next(own, False)
 
     grid = shape((count, 2 * LANES), F32)
+    hots = shape((count // min(256, count) * LANES, shell_count), BF16)
     total, blocks, done = (), 1, 0
     bit = devices // 2
     while bit > 1:
         arrived = swap(load, bit)
         if blocks > 1:
             kernel = handing_on(scatter_new(done, blocks - done, points, lat, strips), 1)
-            total, load = call(kernel, [grid, shape(load.shape, F32)])(
-                *total, new, owner, row, lon, load
-            )
+            outs = [grid, shape(load.shape, F32)]
+            if blocks == 2:
+                kernel = and_read_hot(kernel, read_hot(points, lat, strips))
+                outs.append(hots)
+            total, load, *rest = call(kernel, outs)(*total, new, owner, row, lon, load)
+            hot = rest[0] if rest else hot
             total, done = (total,), blocks
         before, new = load, arrived
         load = jnp.concatenate([load, arrived], axis=0)
@@ -606,7 +639,7 @@
             pltpu.VMEM((2, devices * lat + 2, strips, LANES), F32),
         ],
         after=(end,),
-    )(mine, theirs, owner, row, lon)
+    )(mine, theirs, owner, row, lon, hot)
     return (
         new_density,
         new_velocity,

time: 32.8 us -> 33.1 us (level)
  starting transfers between devices: 12.4 us -> 10.2 us
  waiting for transfers between devices: 5.05 us -> 7.23 us
    ppermute x2, starting transfers between devices: 8.8 us -> 6.17 us  [swap_next(): return lax.ppermute(values, 'mag', pairs if ring else pairs[1:-1])]
    ppermute x6, waiting for transfers between devices: 4.54 us -> 6.72 us  [swap(): return lax.ppermute(values, 'mag', [(i, i ^ bit) for i in range(devices)])]
    ppermute x6, starting transfers between devices: 3.58 us -> 4.04 us  [swap(): return lax.ppermute(values, 'mag', [(i, i ^ bit) for i in range(devices)])]
where the time goes in v11:
time: 33.1 us; the launch traced here: 32.9 us
  Pallas kernels  14.7 us (44%)
  starting transfers between devices  10.2 us (31%)
  waiting for transfers between devices  7.23 us (22%)
  between operations  0.75 us (2%)
    pallas_call x9, Pallas kernels, run(): pallas(body if after else kernel, outs, many, scratch, in_specs)  14.7 us
    ppermute x6, waiting for transfers between devices, swap(): return lax.ppermute(values, 'mag', [(i, i ^ bit) for i in range(devices)])  6.72 us
    ppermute x2, starting transfers between devices, swap_next(): return lax.ppermute(values, 'mag', pairs if ring else pairs[1:-1])  6.17 us
    ppermute x6, starting transfers between devices, swap(): return lax.ppermute(values, 'mag', [(i, i ^ bit) for i in range(devices)])  4.04 us
  transfers between devices with their start and end apart: 8, of which 5 were waited for; matrix products, arithmetic and copies ran while one was open for 0% of the time, Pallas kernels for 25%

profile of v11, /device:TPU:0, one launch (start us, length us, event | category | flops | bytes accessed | tf_op | source)
XLA Modules:
  0.0 32.9 jit_solution(1218496609904289057)
XLA Ops:
  0.6 1.1 %shard_map.136 = (f32[8,4,16,128]{3,2,1,0:T(8,128)S(1)}, f32[2,2,16,128]{3,2,1,0:T(8,128)S(1)}, s32[8,128]{1,0:T(8,128)S(1)}, f32[64,128]{1,0:T(8,128)S(1)}) custom-call(f32[4,16,128]{2,1,0:T(8,128)} %rho_ref.1, f32[3,4,16,128]{3,2,1,0:T(8,128)} %vel_ref.1, f32[3,4,16,128]{3,2,1,0:T(8,128)} %mag_ref.1, f32[4,16,128]{2,1,0:T(8,128)} %prs_ref.1, ...), custom_call_target="tpu_custom_call" | custom-call | tf_op jit(solution)/shard_map/pallas_call | solution.py:33
  1.7 5.5 %collective-permute-start.1 = (f32[2,2,16,128]{3,2,1,0:T(8,128)S(1)}, f32[2,2,16,128]{3,2,1,0:T(8,128)S(1)}, u32[]{:S(2)}, u32[]{:S(2)}) collective-permute-start(f32[2,2,16,128]{3,2,1,0:T(8,128)S(1)} %get-tuple-element.29), channel_id=1, source_target_pairs={{0,15},{1,2},{2,1},{3,4},{4,3},{5,6},{6,5},{7,8},{8,7},{9,10},{10,... | collective-permute-start | bytes 98312 | tf_op jit(solution)/shard_map/ppermute | solution.py:543
  7.3 0.0 collective-permute-start
  7.3 1.1 %shard_map.137.refs_0_.own_side_ref = f32[8,4,16,128]{3,2,1,0:T(8,128)S(1)} custom-call(f32[8,4,16,128]{3,2,1,0:T(8,128)S(1)} %get-tuple-element.26.own_ref.refs_1_), custom_call_target="tpu_custom_call" | custom-call | tf_op jit(solution)/shard_map/pallas_call | solution.py:33
  8.3 0.5 %collective-permute-done.1.refs_5_ = f32[2,2,16,128]{3,2,1,0:T(8,128)S(1)} collective-permute-done((f32[2,2,16,128]{3,2,1,0:T(8,128)S(1)}, f32[2,2,16,128]{3,2,1,0:T(8,128)S(1)}, u32[]{:S(2)}, u32[]{:S(2)}) %collective-permute-start.1) | collective-permute-done | bytes 32800 | tf_op jit(solution)/shard_map/ppermute | solution.py:543
  8.9 0.0 collective-permute-done.refs_4_
  8.9 0.0 copy-start.2
  8.9 0.3 shard_map.138
  9.2 0.0 copy-start
  9.2 0.0 copy-start.1
  9.2 1.3 %collective-permute-start.4 = (f32[72,128]{1,0:T(8,128)S(1)}, f32[72,128]{1,0:T(8,128)S(1)}, u32[]{:S(2)}, u32[]{:S(2)}) collective-permute-start(f32[72,128]{1,0:T(8,128)S(1)} %get-tuple-element.38), channel_id=1, source_target_pairs={{0,8},{1,9},{2,10},{3,11},{4,12},{5,13},{6,14},{7,15},{8,0},{9,1},... | collective-permute-start | bytes 110600 | tf_op jit(solution)/shard_map/ppermute | solution.py:537
  10.5 0.7 %collective-permute-start.3 = (f32[8,4,16,128]{3,2,1,0:T(8,128)S(1)}, f32[8,4,16,128]{3,2,1,0:T(8,128)S(1)}, u32[]{:S(2)}, u32[]{:S(2)}) collective-permute-start(f32[8,4,16,128]{3,2,1,0:T(8,128)S(1)} %get-tuple-element.30.own_ref), channel_id=1, source_target_pairs={{1,2},{2,1},{3,4},{4,3},{5,6},{6,5},{7,8},{8,7},{9,10},{10,9},{11,... | collective-permute-start | bytes 786440 | tf_op jit(solution)/shard_map/ppermute | solution.py:543
  11.2 2.0 %collective-permute-start.2 = (f32[8,4,16,128]{3,2,1,0:T(8,128)S(1)}, f32[8,4,16,128]{3,2,1,0:T(8,128)S(1)}, u32[]{:S(2)}, u32[]{:S(2)}) collective-permute-start(f32[8,4,16,128]{3,2,1,0:T(8,128)S(1)} %get-tuple-element.30.own_ref), channel_id=1, source_target_pairs={{0,1},{1,0},{2,3},{3,2},{4,5},{5,4},{6,7},{7,6},{8,9},{9,8},{10,11... | collective-permute-start | bytes 786440 | tf_op jit(solution)/shard_map/ppermute | solution.py:537
  13.2 1.0 %collective-permute-done.4 = f32[72,128]{1,0:T(8,128)S(1)} collective-permute-done((f32[72,128]{1,0:T(8,128)S(1)}, f32[72,128]{1,0:T(8,128)S(1)}, u32[]{:S(2)}, u32[]{:S(2)}) %collective-permute-start.4) | collective-permute-done | bytes 36896 | tf_op jit(solution)/shard_map/ppermute | solution.py:537
  14.2 0.6 %collective-permute-start.5 = (f32[144,128]{1,0:T(8,128)S(1)}, f32[144,128]{1,0:T(8,128)S(1)}, u32[]{:S(2)}, u32[]{:S(2)}) collective-permute-start(f32[144,128]{1,0:T(8,128)S(1)} %constant_dynamic-update-slice_fusion.refs_0_.refs_4_), channel_id=1, source_target_pairs={{0,4},{1,5},{2,6},{3,7},{4,0},{5,1},{6,2},{7,3},{8,12},{9,13},{10,... | collective-permute-start | bytes 221192 | tf_op jit(solution)/shard_map/ppermute | solution.py:537
  14.8 0.0 copy-done.2
  14.8 0.0 copy-done
  14.8 0.0 copy-done.1
  14.8 1.6 %shard_map.141 = (f32[1024,256]{1,0:T(8,128)S(1)}, f32[144,128]{1,0:T(8,128)S(1)}, bf16[512,1024]{1,0:T(8,128)(2,1)S(1)}) custom-call(f32[144,128]{1,0:T(8,128)S(1)} %constant_dynamic-update-slice_fusion.refs_0_.refs_4_, s32[128,128]{1,0:T(8,128)S(1)} %bitcast.5, s32[128,128]{1,0:T(8,128)S(1)} %bitcast.9, s32[128,128]{1,0:T(8,128)S(1)} %bitcast.13, ...), custom_call_target="tpu_custom_call" | custom-call | tf_op jit(solution)/shard_map/pallas_call | solution.py:33
  16.4 4.0 %collective-permute-done.5.refs_1_ = f32[144,128]{1,0:T(8,128)S(1)} collective-permute-done((f32[144,128]{1,0:T(8,128)S(1)}, f32[144,128]{1,0:T(8,128)S(1)}, u32[]{:S(2)}, u32[]{:S(2)}) %collective-permute-start.5) | collective-permute-done | bytes 73760 | tf_op jit(solution)/shard_map/ppermute | solution.py:537
  20.4 0.0 collective-permute-start.6
  20.4 1.3 %shard_map.142 = (f32[1024,256]{1,0:T(8,128)S(1)}, f32[288,128]{1,0:T(8,128)S(1)}) custom-call(f32[1024,256]{1,0:T(8,128)S(1)} %get-tuple-element.39.refs_0_, f32[144,128]{1,0:T(8,128)S(1)} %collective-permute-done.5.refs_1_, s32[128,128]{1,0:T(8,128)S(1)} %bitcast.6, s32[128,128]{1,0:T(8,128)S(1)} %bitcast.10, s32[128,128]{1,0:T(8,128)S(1)} %bitcast.14, ...), custom_call_target="tpu_custom_call" | custom-call | tf_op jit(solution)/shard_map/pallas_call | solution.py:33
  21.7 0.0 collective-permute-done.3.eight_b
  21.8 0.0 collective-permute-done.2.eight_a
  21.8 2.2 %shard_map.139 = (f32[8,8,16,128]{3,2,1,0:T(8,128)S(1)}, f32[8,4,16,128]{3,2,1,0:T(8,128)S(1)}) custom-call(f32[8,4,16,128]{3,2,1,0:T(8,128)S(1)} %get-tuple-element.30.own_ref, f32[8,4,16,128]{3,2,1,0:T(8,128)S(1)} %collective-permute-done.2.eight_a, f32[8,4,16,128]{3,2,1,0:T(8,128)S(1)} %collective-permute-done.3.eight_b, ...), custom_call_target="tpu_custom_call" | custom-call | tf_op jit(solution)/shard_map/pallas_call | solution.py:33
  23.9 1.6 %collective-permute-done.6.refs_3_ = f32[288,128]{1,0:T(8,128)S(1)} collective-permute-done((f32[288,128]{1,0:T(8,128)S(1)}, f32[288,128]{1,0:T(8,128)S(1)}, u32[]{:S(2)}, u32[]{:S(2)}) %collective-permute-start.6) | collective-permute-done | bytes 147488 | tf_op jit(solution)/shard_map/ppermute | solution.py:537
  25.6 2.4 %shard_map.143.refs_1_ = f32[1536,128]{1,0:T(8,128)S(1)} custom-call(f32[8,4,16,128]{3,2,1,0:T(8,128)S(1)} %get-tuple-element.32.half_ref.refs_0_, f32[1024,256]{1,0:T(8,128)S(1)} %get-tuple-element.41.refs_1_, f32[288,128]{1,0:T(8,128)S(1)} %get-tuple-element.42.refs_2_, f32[288,128]{1,0:T(8,128)S(1)} %collective-permute-done.6.refs_3_, ...), custom_call_target="tpu_custom_call" | custom-call | tf_op jit(solution)/shard_map/pallas_call | solution.py:33
  28.0 0.1 collective-permute-start.7
  28.0 2.1 %shard_map.140 = (f32[4,16,128]{2,1,0:T(8,128)}, f32[3,4,16,128]{3,2,1,0:T(8,128)}, f32[3,4,16,128]{3,2,1,0:T(8,128)}, f32[4,16,128]{2,1,0:T(8,128)}, f32[8,128]{1,0:T(8,128)S(1)}) custom-call(f32[8,8,16,128]{3,2,1,0:T(8,128)S(1)} %get-tuple-element.31.next_ref, f32[8,4,16,128]{3,2,1,0:T(8,128)S(1)} %get-tuple-element.32.half_ref.refs_0_), custom_call_target="tpu_custom_call" | custom-call | tf_op jit(solution)/shard_map/pallas_call | solution.py:33
  30.2 0.1 collective-permute-done.7.refs_2_
  30.3 2.6 %shard_map.144 = (f32[4,2048]{1,0:T(4,128)}, f32[8,128]{1,0:T(8,128)}) custom-call(f32[8,128]{1,0:T(8,128)S(1)} %get-tuple-element.37.refs_0_, f32[1536,128]{1,0:T(8,128)S(1)} %shard_map.143.refs_1_, f32[1536,128]{1,0:T(8,128)S(1)} %collective-permute-done.7.refs_2_, s32[128,128]{1,0:T(8,128)S(1)} %bitcast.8, s32[128,128]{1,0:T(8,128)S(1)} %bitcast.12, ...), custom_call_target="tpu_custom_call" | custom-call | tf_op jit(solution)/shard_map/pallas_call | solution.py:33
  (4 shorter events, 0.0 us)
Async XLA Ops:
  1.7 7.1 %collective-permute-start.1 = (f32[2,2,16,128]{3,2,1,0:T(8,128)S(1)}, f32[2,2,16,128]{3,2,1,0:T(8,128)S(1)}, u32[]{:S(2)}, u32[]{:S(2)}) collective-permute-start(f32[2,2,16,128]{3,2,1,0:T(8,128)S(1)} %get-tuple-element.29), channel_id=1, source_target_pairs={{0,15},{1,2},{2,1},{3,4},{4,3},{5,6},{6,5},{7,8},{8,7},{9,10},{10,... | collective-permute-start | bytes 98312 | tf_op jit(solution)/shard_map/ppermute | solution.py:543
  7.3 1.6 %collective-permute-start = (f32[2,2,16,128]{3,2,1,0:T(8,128)S(1)}, f32[2,2,16,128]{3,2,1,0:T(8,128)S(1)}, u32[]{:S(2)}, u32[]{:S(2)}) collective-permute-start(f32[2,2,16,128]{3,2,1,0:T(8,128)S(1)} %get-tuple-element.29), channel_id=1, source_target_pairs={{0,1},{1,0},{2,3},{3,2},{4,5},{5,4},{6,7},{7,6},{8,9},{9,8},{10,11... | collective-permute-start | bytes 98312 | tf_op jit(solution)/shard_map/ppermute | solution.py:537
  8.9 6.0 %copy-start.2 = (s32[16384]{0:T(1024)S(1)}, s32[16384]{0:T(1024)}, u32[]{:S(2)}) copy-start(s32[16384]{0:T(1024)} %param.17) | copy-start | bytes 196612
  9.2 5.6 %copy-start = (s32[16384,1]{0,1:T(1,128)S(1)}, s32[16384,1]{0,1:T(1,128)}, u32[]{:S(2)}) copy-start(s32[16384,1]{0,1:T(1,128)} %param.15) | copy-start | bytes 196612
  9.2 5.6 %copy-start.1 = (s32[16384]{0:T(1024)S(1)}, s32[16384]{0:T(1024)}, u32[]{:S(2)}) copy-start(s32[16384]{0:T(1024)} %param.16) | copy-start | bytes 196612
  9.2 5.0 %collective-permute-start.4 = (f32[72,128]{1,0:T(8,128)S(1)}, f32[72,128]{1,0:T(8,128)S(1)}, u32[]{:S(2)}, u32[]{:S(2)}) collective-permute-start(f32[72,128]{1,0:T(8,128)S(1)} %get-tuple-element.38), channel_id=1, source_target_pairs={{0,8},{1,9},{2,10},{3,11},{4,12},{5,13},{6,14},{7,15},{8,0},{9,1},... | collective-permute-start | bytes 110600 | tf_op jit(solution)/shard_map/ppermute | solution.py:537
  10.5 11.2 %collective-permute-start.3 = (f32[8,4,16,128]{3,2,1,0:T(8,128)S(1)}, f32[8,4,16,128]{3,2,1,0:T(8,128)S(1)}, u32[]{:S(2)}, u32[]{:S(2)}) collective-permute-start(f32[8,4,16,128]{3,2,1,0:T(8,128)S(1)} %get-tuple-element.30.own_ref), channel_id=1, source_target_pairs={{1,2},{2,1},{3,4},{4,3},{5,6},{6,5},{7,8},{8,7},{9,10},{10,9},{11,... | collective-permute-start | bytes 786440 | tf_op jit(solution)/shard_map/ppermute | solution.py:543
  11.2 10.6 %collective-permute-start.2 = (f32[8,4,16,128]{3,2,1,0:T(8,128)S(1)}, f32[8,4,16,128]{3,2,1,0:T(8,128)S(1)}, u32[]{:S(2)}, u32[]{:S(2)}) collective-permute-start(f32[8,4,16,128]{3,2,1,0:T(8,128)S(1)} %get-tuple-element.30.own_ref), channel_id=1, source_target_pairs={{0,1},{1,0},{2,3},{3,2},{4,5},{5,4},{6,7},{7,6},{8,9},{9,8},{10,11... | collective-permute-start | bytes 786440 | tf_op jit(solution)/shard_map/ppermute | solution.py:537
  14.2 6.2 %collective-permute-start.5 = (f32[144,128]{1,0:T(8,128)S(1)}, f32[144,128]{1,0:T(8,128)S(1)}, u32[]{:S(2)}, u32[]{:S(2)}) collective-permute-start(f32[144,128]{1,0:T(8,128)S(1)} %constant_dynamic-update-slice_fusion.refs_0_.refs_4_), channel_id=1, source_target_pairs={{0,4},{1,5},{2,6},{3,7},{4,0},{5,1},{6,2},{7,3},{8,12},{9,13},{10,... | collective-permute-start | bytes 221192 | tf_op jit(solution)/shard_map/ppermute | solution.py:537
  20.4 5.1 %collective-permute-start.6 = (f32[288,128]{1,0:T(8,128)S(1)}, f32[288,128]{1,0:T(8,128)S(1)}, u32[]{:S(2)}, u32[]{:S(2)}) collective-permute-start(f32[288,128]{1,0:T(8,128)S(1)} %constant_dynamic-update-slice_fusion.2.refs_5_), channel_id=1, source_target_pairs={{0,2},{1,3},{2,0},{3,1},{4,6},{5,7},{6,4},{7,5},{8,10},{9,11},{10,... | collective-permute-start | bytes 442376 | tf_op jit(solution)/shard_map/ppermute | solution.py:537
  28.0 2.4 %collective-permute-start.7 = (f32[1536,128]{1,0:T(8,128)S(1)}, f32[1536,128]{1,0:T(8,128)S(1)}, u32[]{:S(2)}, u32[]{:S(2)}) collective-permute-start(f32[1536,128]{1,0:T(8,128)S(1)} %shard_map.143.refs_1_), channel_id=1, source_target_pairs={{0,1},{1,0},{2,3},{3,2},{4,5},{5,4},{6,7},{7,6},{8,9},{9,8},{10,11... | collective-permute-start | bytes 2359304 | tf_op jit(solution)/shard_map/ppermute | solution.py:537

commit v12 on v8

--- a/solution.py
+++ b/solution.py
@@ -173,15 +173,20 @@
     lax.fori_loop(0, own_ref.shape[1], body, 0)
 
 
-def stage_one(own_ref, eight_a, eight_b, own_side_ref, next_ref, half_ref, pad_ref, side_ref):
+def stage_one(
+    own_ref, mag_a, mag_b, five_a, five_b, own_side_ref, next_ref, half_ref, pad_ref, side_ref
+):
     me = lax.axis_index("mag")
     last = lax.axis_size("mag") - 1
     even = me % 2 == 0
     cx = own_ref.shape[1]
     for k in range(8):
         for x in range(cx):
-            low = jnp.where(even, eight_b[k, x], eight_a[k, x])
-            high = jnp.where(even, eight_a[k, x], eight_b[k, x])
+            in_field = 4 <= k < 7
+            from_a = mag_a[k - 4, x] if in_field else five_a[min(k, 4), x]
+            from_b = mag_b[k - 4, x] if in_field else five_b[min(k, 4), x]
+            low = jnp.where(even, from_b, from_a)
+            high = jnp.where(even, from_a, from_b)
             pad_ref[k, x] = jnp.where(me == 0, own_ref[k, 0], low)
             pad_ref[k, cx + x] = own_ref[k, x]
             pad_ref[k, 2 * cx + x] = jnp.where(me == last, own_ref[k, cx - 1], high)
@@ -238,12 +243,13 @@
     sweep_planes(next_ref, 2, cx, put, lambda step, q: sideways(q))
 
 
-def pick_current(own_ref, cell_ref, strip_ref, edge_a, edge_b, out_ref, own_out):
+def pick_current(own_ref, cell_ref, strip_ref, mag_a, mag_b, out_ref, five_out):
     me = lax.axis_index("mag")
     last = lax.axis_size("mag") - 1
     even = me % 2 == 0
     cx, ny, nz = own_ref.shape[1:]
-    own_out[...] = own_ref[...]
+    five_out[0:4] = own_ref[0:4]
+    five_out[4] = own_ref[7]
     rows = []
     for x in range(cx):
         bx, by, bz = (own_ref[4 + k, x] for k in range(3))
@@ -252,9 +258,9 @@
             if 0 <= x + step < cx:
                 return own_ref[4 + k, x + step]
             if step < 0:
-                below = jnp.where(even, edge_b[k - 1, 1], edge_a[k - 1, 1])
+                below = jnp.where(even, mag_b[k, cx - 1], mag_a[k, cx - 1])
                 return jnp.where(me == 0, own_ref[4 + k, x], below)
-            above = jnp.where(even, edge_a[k - 1, 0], edge_b[k - 1, 0])
+            above = jnp.where(even, mag_a[k, 0], mag_b[k, 0])
             return jnp.where(me == last, own_ref[4 + k, x], above)
 
         def along_x(k):
@@ -285,13 +291,10 @@
 
 
 def load_arguments(
-    rho_ref, vel_ref, mag_ref, prs_ref, cell_ref, cond_ref, own_out, edge_out, cell_out, strip_out, rows, sems
+    rho_ref, vel_ref, mag_ref, prs_ref, cell_ref, cond_ref, own_out, cell_out, strip_out, rows, sems
 ):
-    last = mag_ref.shape[1] - 1
     pairs = [
         (cond_ref, rows),
-        (mag_ref.at[pl.ds(1, 2), pl.ds(0, 1)], edge_out.at[:, pl.ds(0, 1)]),
-        (mag_ref.at[pl.ds(1, 2), pl.ds(last, 1)], edge_out.at[:, pl.ds(1, 1)]),
         (cell_ref, cell_out),
         (rho_ref, own_out.at[0]),
         (vel_ref, own_out.at[pl.ds(1, 3)]),
@@ -529,10 +532,11 @@
 
     tile = shape((points, LANES), I32)
     slab = shape((8, cx, ny, nz), F32)
-    own, edge, cell, strip = call(
+    mag_a, mag_b = swap(mag_field, 1), swap_next(mag_field)
+    own, cell, strip = call(
         load_arguments,
-        [slab, shape((2, 2, ny, nz), F32), tile, shape((cells, LANES), F32)],
-        [pltpu.VMEM((lat, columns), F32), pltpu.SemaphoreType.DMA((8,))],
+        [slab, tile, shape((cells, LANES), F32)],
+        [pltpu.VMEM((lat, columns), F32), pltpu.SemaphoreType.DMA((6,))],
         [HBM] * 6,
     )(
         *(
@@ -547,17 +551,18 @@
             )
         )
     )
-    edge_a, edge_b = swap(edge, 1), swap_next(edge)
     own_side = call(stage_own, slab)(own)
 
     owner = foot_owner.reshape(-1, LANES)
     row = foot_row.reshape(-1, LANES)
     lon = foot_lon.reshape(-1, LANES)
 
-    load, own = call(
-        pick_current, [shape((points + cells, LANES), F32), slab], after=(own_side,)
-    )(own, cell, strip, edge_a, edge_b)
-    eight_a, eight_b = swap(own, 1), swap_next(own)
+    load, five = call(
+        pick_current,
+        [shape((points + cells, LANES), F32), shape((5, cx, ny, nz), F32)],
+        after=(own_side,),
+    )(own, cell, strip, mag_a, mag_b)
+    five_a, five_b = swap(five, 1), swap_next(five)
 
     grid = shape((count, 2 * LANES), F32)
     total, blocks, done = (), 1, 0
@@ -580,7 +585,7 @@
         stage_one,
         [shape((8, cx + 4, ny, nz), F32), slab],
         [pltpu.VMEM((8, 3 * cx, ny, nz), F32), pltpu.VMEM((8, cx + 4, ny, nz), F32)],
-    )(own, eight_a, eight_b, own_side)
+    )(own, mag_a, mag_b, five_a, five_b, own_side)
 
     grids = shape((count + count // 2, LANES), F32)
     mine = call(

time: 32.8 us -> 31.5 us (0.960)
  waiting for transfers between devices: 5.05 us -> 4.38 us
  starting transfers between devices: 12.4 us -> 11.9 us
    ppermute x6, waiting for transfers between devices: 4.54 us -> 4 us  [swap(): return lax.ppermute(values, 'mag', [(i, i ^ bit) for i in range(devices)])]
    ppermute x6, starting transfers between devices: 3.58 us -> 3.2 us  [swap(): return lax.ppermute(values, 'mag', [(i, i ^ bit) for i in range(devices)])]
  transfers between devices with their start and end apart: 8 -> 8, of which waited for: 5 -> 5; matrix products, arithmetic and copies ran while one was open for 0% -> 0% of each run, Pallas kernels for 25% -> 29%
where the time goes in v12:
time: 31.5 us; the launch traced here: 31.4 us
  Pallas kernels  14.3 us (45%)
  starting transfers between devices  11.9 us (38%)
  waiting for transfers between devices  4.38 us (14%)
  between operations  0.74 us (2%)
    pallas_call x9, Pallas kernels, run(): pallas(body if after else kernel, outs, many, scratch, in_specs)  14.3 us
    ppermute x2, starting transfers between devices, swap_next(): return lax.ppermute(values, 'mag', pairs)  8.7 us
    ppermute x6, waiting for transfers between devices, swap(): return lax.ppermute(values, 'mag', [(i, i ^ bit) for i in range(devices)])  4 us
    ppermute x6, starting transfers between devices, swap(): return lax.ppermute(values, 'mag', [(i, i ^ bit) for i in range(devices)])  3.2 us
  transfers between devices with their start and end apart: 8, of which 5 were waited for; matrix products, arithmetic and copies ran while one was open for 0% of the time, Pallas kernels for 29%

profile of v12, /device:TPU:0, one launch (start us, length us, event | category | flops | bytes accessed | tf_op | source)
XLA Modules:
  0.0 31.4 jit_solution(16714646022162019637)
XLA Ops:
  0.6 5.5 %collective-permute-start.1 = (f32[3,4,16,128]{3,2,1,0:T(8,128)}, f32[3,4,16,128]{3,2,1,0:T(8,128)S(1)}, u32[]{:S(2)}, u32[]{:S(2)}) collective-permute-start(f32[3,4,16,128]{3,2,1,0:T(8,128)} %mag_ref.1), channel_id=1, source_target_pairs={{0,15},{1,2},{2,1},{3,4},{4,3},{5,6},{6,5},{7,8},{8,7},{9,10},{10,... | collective-permute-start | bytes 294920 | tf_op jit(solution)/shard_map/ppermute | solution.py:517
  6.1 0.0 collective-permute-start
  6.1 1.0 %shard_map.136 = (f32[8,4,16,128]{3,2,1,0:T(8,128)S(1)}, s32[8,128]{1,0:T(8,128)S(1)}, f32[64,128]{1,0:T(8,128)S(1)}) custom-call(f32[4,16,128]{2,1,0:T(8,128)} %rho_ref.1, f32[3,4,16,128]{3,2,1,0:T(8,128)} %vel_ref.1, f32[3,4,16,128]{3,2,1,0:T(8,128)} %mag_ref.1, f32[4,16,128]{2,1,0:T(8,128)} %prs_ref.1, s32[8,128]{1,0:T(8,128)} %bitcast.17, f32[4,2048]{1,0:T(4,128)} %cond_ref.1), custom_call_target="tpu_custom_call" | custom-call | tf_op jit(solution)/shard_map/pallas_call | solution.py:33
  7.2 1.1 %shard_map.137.refs_0_.own_side_ref = f32[8,4,16,128]{3,2,1,0:T(8,128)S(1)} custom-call(f32[8,4,16,128]{3,2,1,0:T(8,128)S(1)} %get-tuple-element.24.own_ref.refs_1_), custom_call_target="tpu_custom_call" | custom-call | tf_op jit(solution)/shard_map/pallas_call | solution.py:33
  8.3 0.4 %collective-permute-done.1.refs_5_.mag_b = f32[3,4,16,128]{3,2,1,0:T(8,128)S(1)} collective-permute-done((f32[3,4,16,128]{3,2,1,0:T(8,128)}, f32[3,4,16,128]{3,2,1,0:T(8,128)S(1)}, u32[]{:S(2)}, u32[]{:S(2)}) %collective-permute-start.1) | collective-permute-done | bytes 98336 | tf_op jit(solution)/shard_map/ppermute | solution.py:517
  8.7 0.0 collective-permute-done.refs_4_.mag_a
  8.7 0.0 copy-start.2
  8.7 0.3 shard_map.138
  9.0 0.0 copy-start
  9.0 0.0 copy-start.1
  9.0 1.4 %collective-permute-start.4 = (f32[72,128]{1,0:T(8,128)S(1)}, f32[72,128]{1,0:T(8,128)S(1)}, u32[]{:S(2)}, u32[]{:S(2)}) collective-permute-start(f32[72,128]{1,0:T(8,128)S(1)} %get-tuple-element.35), channel_id=1, source_target_pairs={{0,8},{1,9},{2,10},{3,11},{4,12},{5,13},{6,14},{7,15},{8,0},{9,1},... | collective-permute-start | bytes 110600 | tf_op jit(solution)/shard_map/ppermute | solution.py:511
  10.4 3.2 %collective-permute-start.3 = (f32[5,4,16,128]{3,2,1,0:T(8,128)S(1)}, f32[5,4,16,128]{3,2,1,0:T(8,128)S(1)}, u32[]{:S(2)}, u32[]{:S(2)}) collective-permute-start(f32[5,4,16,128]{3,2,1,0:T(8,128)S(1)} %get-tuple-element.27), channel_id=1, source_target_pairs={{0,15},{1,2},{2,1},{3,4},{4,3},{5,6},{6,5},{7,8},{8,7},{9,10},{10,... | collective-permute-start | bytes 491528 | tf_op jit(solution)/shard_map/ppermute | solution.py:517
  13.6 0.0 collective-permute-start.2
  13.6 0.5 %collective-permute-done.4 = f32[72,128]{1,0:T(8,128)S(1)} collective-permute-done((f32[72,128]{1,0:T(8,128)S(1)}, f32[72,128]{1,0:T(8,128)S(1)}, u32[]{:S(2)}, u32[]{:S(2)}) %collective-permute-start.4) | collective-permute-done | bytes 36896 | tf_op jit(solution)/shard_map/ppermute | solution.py:511
  14.1 0.2 collective-permute-start.5
  14.3 0.0 copy-done.2
  14.3 0.0 copy-done
  14.3 0.0 copy-done.1
  14.3 1.3 %shard_map.141 = (f32[1024,256]{1,0:T(8,128)S(1)}, f32[144,128]{1,0:T(8,128)S(1)}) custom-call(f32[144,128]{1,0:T(8,128)S(1)} %constant_dynamic-update-slice_fusion.refs_0_.refs_4_, s32[128,128]{1,0:T(8,128)S(1)} %bitcast.5, s32[128,128]{1,0:T(8,128)S(1)} %bitcast.9, s32[128,128]{1,0:T(8,128)S(1)} %bitcast.13, ...), custom_call_target="tpu_custom_call" | custom-call | tf_op jit(solution)/shard_map/pallas_call | solution.py:33
  15.6 2.8 %collective-permute-done.5.refs_1_ = f32[144,128]{1,0:T(8,128)S(1)} collective-permute-done((f32[144,128]{1,0:T(8,128)S(1)}, f32[144,128]{1,0:T(8,128)S(1)}, u32[]{:S(2)}, u32[]{:S(2)}) %collective-permute-start.5) | collective-permute-done | bytes 73760 | tf_op jit(solution)/shard_map/ppermute | solution.py:511
  18.4 1.6 %collective-permute-start.6 = (f32[288,128]{1,0:T(8,128)S(1)}, f32[288,128]{1,0:T(8,128)S(1)}, u32[]{:S(2)}, u32[]{:S(2)}) collective-permute-start(f32[288,128]{1,0:T(8,128)S(1)} %constant_dynamic-update-slice_fusion.2.refs_5_), channel_id=1, source_target_pairs={{0,2},{1,3},{2,0},{3,1},{4,6},{5,7},{6,4},{7,5},{8,10},{9,11},{10,... | collective-permute-start | bytes 442376 | tf_op jit(solution)/shard_map/ppermute | solution.py:511
  20.0 1.3 %shard_map.142 = (f32[1024,256]{1,0:T(8,128)S(1)}, f32[288,128]{1,0:T(8,128)S(1)}) custom-call(f32[1024,256]{1,0:T(8,128)S(1)} %get-tuple-element.36.refs_0_, f32[144,128]{1,0:T(8,128)S(1)} %collective-permute-done.5.refs_1_, s32[128,128]{1,0:T(8,128)S(1)} %bitcast.6, s32[128,128]{1,0:T(8,128)S(1)} %bitcast.10, s32[128,128]{1,0:T(8,128)S(1)} %bitcast.14, ...), custom_call_target="tpu_custom_call" | custom-call | tf_op jit(solution)/shard_map/pallas_call | solution.py:33
  21.3 0.0 collective-permute-done.3.five_b
  21.3 0.0 collective-permute-done.2.five_a
  21.3 2.2 %shard_map.139 = (f32[8,8,16,128]{3,2,1,0:T(8,128)S(1)}, f32[8,4,16,128]{3,2,1,0:T(8,128)S(1)}) custom-call(f32[8,4,16,128]{3,2,1,0:T(8,128)S(1)} %get-tuple-element.24.own_ref.refs_1_, f32[3,4,16,128]{3,2,1,0:T(8,128)S(1)} %collective-permute-done.refs_4_.mag_a, f32[3,4,16,128]{3,2,1,0:T(8,128)S(1)} %collective-permute-done.1.refs_5_.mag_b, ...), custom_call_target="tpu_custom_call" | custom-call | tf_op jit(solution)/shard_map/pallas_call | solution.py:33
  23.5 0.5 %collective-permute-done.6.refs_3_ = f32[288,128]{1,0:T(8,128)S(1)} collective-permute-done((f32[288,128]{1,0:T(8,128)S(1)}, f32[288,128]{1,0:T(8,128)S(1)}, u32[]{:S(2)}, u32[]{:S(2)}) %collective-permute-start.6) | collective-permute-done | bytes 147488 | tf_op jit(solution)/shard_map/ppermute | solution.py:511
  24.0 2.4 %shard_map.143.refs_1_ = f32[1536,128]{1,0:T(8,128)S(1)} custom-call(f32[8,4,16,128]{3,2,1,0:T(8,128)S(1)} %get-tuple-element.29.half_ref.refs_0_, f32[1024,256]{1,0:T(8,128)S(1)} %get-tuple-element.38.refs_1_, f32[288,128]{1,0:T(8,128)S(1)} %get-tuple-element.39.refs_2_, f32[288,128]{1,0:T(8,128)S(1)} %collective-permute-done.6.refs_3_, ...), custom_call_target="tpu_custom_call" | custom-call | tf_op jit(solution)/shard_map/pallas_call | solution.py:33
  26.4 0.1 collective-permute-start.7
  26.5 2.1 %shard_map.140 = (f32[4,16,128]{2,1,0:T(8,128)}, f32[3,4,16,128]{3,2,1,0:T(8,128)}, f32[3,4,16,128]{3,2,1,0:T(8,128)}, f32[4,16,128]{2,1,0:T(8,128)}, f32[8,128]{1,0:T(8,128)S(1)}) custom-call(f32[8,8,16,128]{3,2,1,0:T(8,128)S(1)} %get-tuple-element.28.next_ref, f32[8,4,16,128]{3,2,1,0:T(8,128)S(1)} %get-tuple-element.29.half_ref.refs_0_), custom_call_target="tpu_custom_call" | custom-call | tf_op jit(solution)/shard_map/pallas_call | solution.py:33
  28.6 0.1 collective-permute-done.7.refs_2_
  28.8 2.6 %shard_map.144 = (f32[4,2048]{1,0:T(4,128)}, f32[8,128]{1,0:T(8,128)}) custom-call(f32[8,128]{1,0:T(8,128)S(1)} %get-tuple-element.34.refs_0_, f32[1536,128]{1,0:T(8,128)S(1)} %shard_map.143.refs_1_, f32[1536,128]{1,0:T(8,128)S(1)} %collective-permute-done.7.refs_2_, s32[128,128]{1,0:T(8,128)S(1)} %bitcast.8, s32[128,128]{1,0:T(8,128)S(1)} %bitcast.12, ...), custom_call_target="tpu_custom_call" | custom-call | tf_op jit(solution)/shard_map/pallas_call | solution.py:33
  (4 shorter events, 0.0 us)
Async XLA Ops:
  0.6 8.0 %collective-permute-start.1 = (f32[3,4,16,128]{3,2,1,0:T(8,128)}, f32[3,4,16,128]{3,2,1,0:T(8,128)S(1)}, u32[]{:S(2)}, u32[]{:S(2)}) collective-permute-start(f32[3,4,16,128]{3,2,1,0:T(8,128)} %mag_ref.1), channel_id=1, source_target_pairs={{0,15},{1,2},{2,1},{3,4},{4,3},{5,6},{6,5},{7,8},{8,7},{9,10},{10,... | collective-permute-start | bytes 294920 | tf_op jit(solution)/shard_map/ppermute | solution.py:517
  6.1 2.5 %collective-permute-start = (f32[3,4,16,128]{3,2,1,0:T(8,128)}, f32[3,4,16,128]{3,2,1,0:T(8,128)S(1)}, u32[]{:S(2)}, u32[]{:S(2)}) collective-permute-start(f32[3,4,16,128]{3,2,1,0:T(8,128)} %mag_ref.1), channel_id=1, source_target_pairs={{0,1},{1,0},{2,3},{3,2},{4,5},{5,4},{6,7},{7,6},{8,9},{9,8},{10,11... | collective-permute-start | bytes 294920 | tf_op jit(solution)/shard_map/ppermute | solution.py:511
  8.7 5.6 %copy-start.2 = (s32[16384]{0:T(1024)S(1)}, s32[16384]{0:T(1024)}, u32[]{:S(2)}) copy-start(s32[16384]{0:T(1024)} %param.17) | copy-start | bytes 196612
  9.0 5.3 %copy-start = (s32[16384,1]{0,1:T(1,128)S(1)}, s32[16384,1]{0,1:T(1,128)}, u32[]{:S(2)}) copy-start(s32[16384,1]{0,1:T(1,128)} %param.15) | copy-start | bytes 196612
  9.0 5.3 %copy-start.1 = (s32[16384]{0:T(1024)S(1)}, s32[16384]{0:T(1024)}, u32[]{:S(2)}) copy-start(s32[16384]{0:T(1024)} %param.16) | copy-start | bytes 196612
  9.0 5.1 %collective-permute-start.4 = (f32[72,128]{1,0:T(8,128)S(1)}, f32[72,128]{1,0:T(8,128)S(1)}, u32[]{:S(2)}, u32[]{:S(2)}) collective-permute-start(f32[72,128]{1,0:T(8,128)S(1)} %get-tuple-element.35), channel_id=1, source_target_pairs={{0,8},{1,9},{2,10},{3,11},{4,12},{5,13},{6,14},{7,15},{8,0},{9,1},... | collective-permute-start | bytes 110600 | tf_op jit(solution)/shard_map/ppermute | solution.py:511
  10.4 10.9 %collective-permute-start.3 = (f32[5,4,16,128]{3,2,1,0:T(8,128)S(1)}, f32[5,4,16,128]{3,2,1,0:T(8,128)S(1)}, u32[]{:S(2)}, u32[]{:S(2)}) collective-permute-start(f32[5,4,16,128]{3,2,1,0:T(8,128)S(1)} %get-tuple-element.27), channel_id=1, source_target_pairs={{0,15},{1,2},{2,1},{3,4},{4,3},{5,6},{6,5},{7,8},{8,7},{9,10},{10,... | collective-permute-start | bytes 491528 | tf_op jit(solution)/shard_map/ppermute | solution.py:517
  13.6 7.7 %collective-permute-start.2 = (f32[5,4,16,128]{3,2,1,0:T(8,128)S(1)}, f32[5,4,16,128]{3,2,1,0:T(8,128)S(1)}, u32[]{:S(2)}, u32[]{:S(2)}) collective-permute-start(f32[5,4,16,128]{3,2,1,0:T(8,128)S(1)} %get-tuple-element.27), channel_id=1, source_target_pairs={{0,1},{1,0},{2,3},{3,2},{4,5},{5,4},{6,7},{7,6},{8,9},{9,8},{10,11... | collective-permute-start | bytes 491528 | tf_op jit(solution)/shard_map/ppermute | solution.py:511
  14.1 4.4 %collective-permute-start.5 = (f32[144,128]{1,0:T(8,128)S(1)}, f32[144,128]{1,0:T(8,128)S(1)}, u32[]{:S(2)}, u32[]{:S(2)}) collective-permute-start(f32[144,128]{1,0:T(8,128)S(1)} %constant_dynamic-update-slice_fusion.refs_0_.refs_4_), channel_id=1, source_target_pairs={{0,4},{1,5},{2,6},{3,7},{4,0},{5,1},{6,2},{7,3},{8,12},{9,13},{10,... | collective-permute-start | bytes 221192 | tf_op jit(solution)/shard_map/ppermute | solution.py:511
  18.4 5.6 %collective-permute-start.6 = (f32[288,128]{1,0:T(8,128)S(1)}, f32[288,128]{1,0:T(8,128)S(1)}, u32[]{:S(2)}, u32[]{:S(2)}) collective-permute-start(f32[288,128]{1,0:T(8,128)S(1)} %constant_dynamic-update-slice_fusion.2.refs_5_), channel_id=1, source_target_pairs={{0,2},{1,3},{2,0},{3,1},{4,6},{5,7},{6,4},{7,5},{8,10},{9,11},{10,... | collective-permute-start | bytes 442376 | tf_op jit(solution)/shard_map/ppermute | solution.py:511
  26.4 2.4 %collective-permute-start.7 = (f32[1536,128]{1,0:T(8,128)S(1)}, f32[1536,128]{1,0:T(8,128)S(1)}, u32[]{:S(2)}, u32[]{:S(2)}) collective-permute-start(f32[1536,128]{1,0:T(8,128)S(1)} %shard_map.143.refs_1_), channel_id=1, source_target_pairs={{0,1},{1,0},{2,3},{3,2},{4,5},{5,4},{6,7},{7,6},{8,9},{9,8},{10,11... | collective-permute-start | bytes 2359304 | tf_op jit(solution)/shard_map/ppermute | solution.py:511
